TPU v7x, 32 devices: a whole 2x2x4 slice. The times are simulated.
32 devices in a mesh: groups: 2 (over y), frames: 8 (over z, x), bins: 2 (over core).
Axes of the slice: x: 2, y: 2, z: 4, core: 2. Of those that a mesh axis runs over, the one named last changes fastest.
Arguments:
- spectrum: float32 [2048, 32768], P('bins', ('groups', 'frames')), parts along dimension 1, may hold values from 0.1 to 10
- atoms_by_bin: float32 [256, 4096], P('frames', ('groups', 'bins')), parts along dimension 1, may hold values from 0.03 to 2.12, as said below
- activations: float32 [256, 32768], P('bins', ('groups', 'frames')), parts along dimension 1, may hold values from 0.01 to 2.05, as said below
Outputs:
- new_activations: float32 [256, 32768], P('bins', ('groups', 'frames')), parts along dimension 1
- new_atoms: float32 [256, 4096], P('frames', ('groups', 'bins')), parts along dimension 1
There are 2 independent parts, one for each index of `groups`. A program takes and returns all parts, laid end to end along the dimension named above; each array names one. Nothing has to cross between parts.
Inputs may be any that keep to these rules, and one draw needn't show every extreme that they name: `atoms_by_bin`: every entry is positive. `activations`: every entry is positive.
All inputs are finite; a program needn't handle non-finite values.
Results may differ from a plain program's by a relative error of at most 0.0003.
Values sent between devices are 32-bit elements; how exact they have to be, the bound alone decides.
No kernel may reach another device: no remote copies, remote signals or barrier semaphores. Data moves between devices by JAX's collectives and lax.ppermute only.
A program may use at most 64 MiB of HBM per device.

v0:
```python
import jax
import jax.numpy as jnp
from jax import lax
from jax.sharding import PartitionSpec as P


def body(spectrum, atoms_by_bin, activations):
    highest = lax.Precision.HIGHEST
    basis = lax.all_gather(atoms_by_bin, "frames", axis=0, tiled=True)
    old_full = lax.all_gather(activations, "bins", axis=0, tiled=True)
    column_mass = lax.psum(jnp.sum(basis, axis=1), "bins")
    model = jnp.dot(basis.T, old_full, precision=highest, preferred_element_type=jnp.float32)
    ratio = spectrum / model
    numer_part = jnp.dot(basis, ratio, precision=highest, preferred_element_type=jnp.float32)
    numer_own = lax.psum_scatter(numer_part, "bins", scatter_dimension=0, tiled=True)
    own_atoms = activations.shape[0]
    mass_own = lax.dynamic_slice_in_dim(
        column_mass, lax.axis_index("bins") * own_atoms, own_atoms, 0
    )
    new_activations = activations * numer_own / mass_own[:, None]
    fresh_full = lax.all_gather(new_activations, "bins", axis=0, tiled=True)
    model_next = jnp.dot(basis.T, fresh_full, precision=highest, preferred_element_type=jnp.float32)
    ratio_next = spectrum / model_next
    basis_part = lax.dot_general(
        fresh_full,
        ratio_next,
        (((1,), (1,)), ((), ())),
        precision=highest,
        preferred_element_type=jnp.float32,
    )
    row_part = jnp.sum(fresh_full, axis=1)
    basis_atoms = atoms_by_bin.shape[0]
    offset = lax.axis_index("frames") * basis_atoms
    basis_total, row_total = lax.psum((basis_part, row_part), "frames")
    basis_own = lax.dynamic_slice_in_dim(basis_total, offset, basis_atoms, 0)
    row_own = lax.dynamic_slice_in_dim(row_total, offset, basis_atoms, 0)
    new_atoms = atoms_by_bin * basis_own / row_own[:, None]
    return (new_activations, new_atoms)


def solution(mesh):
    placed = (
        P("bins", ("groups", "frames")),
        P("frames", ("groups", "bins")),
        P("bins", ("groups", "frames")),
    )
    return jax.shard_map(
        body,
        mesh=mesh,
        in_specs=placed,
        out_specs=(P("bins", ("groups", "frames")), P("frames", ("groups", "bins"))),
        check_vma=False,
    )
```

profile of v0, /device:TPU:0, one launch (start us, length us, event | category | flops | bytes accessed | tf_op | source)
XLA Modules:
  0.0 229.2 jit_solution(8778665360878678428)
XLA Ops:
  7.2 0.0 all-gather.4.cloned.1.call-start
  7.2 0.7 all-gather.4.cloned.1.call-update
  7.9 0.0 all-gather.6.cloned.1.call-start
  7.9 0.7 all-gather.6.cloned.1.call-update
  8.6 0.0 reduce-scatter.2.cloned.1.call-start
  8.7 44.3 %all-gather.4.cloned.1.call-done = f32[256,1024]{1,0:T(8,128)} async-done(((f32[32,1024]{1,0:T(8,128)}), f32[256,1024]{1,0:T(8,128)}) %all-gather.4.cloned.1.call-update) | async-done | bytes 1048592 | tf_op jit(solution)/shard_map/all_gather | solution.py:9
  53.0 0.0 copy-start
  53.0 10.9 %all-gather.6.cloned.1.call-done = f32[256,2048]{1,0:T(8,128)} async-done(((f32[128,2048]{1,0:T(8,128)}), f32[256,2048]{1,0:T(8,128)}) %all-gather.6.cloned.1.call-update) | async-done | bytes 2097168 | tf_op jit(solution)/shard_map/all_gather | solution.py:10
  63.9 9.2 %fusion.6 = f32[1024,2048]{1,0:T(8,128)S(1)} fusion(f32[256,1024]{1,0:T(8,128)} %all-gather.4.cloned.1.call-done, f32[256,2048]{1,0:T(8,128)} %all-gather.6.cloned.1.call-done), kind=kOutput, calls=%fused_computation.7 | convolution fusion | flops 6442450944 | bytes 11534336 | tf_op jit(solution)/shard_map/dot_general | solution.py:12
  73.1 0.0 copy-done
  73.2 0.0 copy-start.3
  73.2 17.0 %fusion.3 = f32[256,2048]{0,1:T(8,128)} fusion(f32[256,1024]{1,0:T(8,128)S(1)} %copy-done, f32[1024,2048]{1,0:T(8,128)} %param.3, f32[1024,2048]{1,0:T(8,128)S(1)} %fusion.6), kind=kOutput, calls=%fused_computation.4 | convolution fusion | flops 6444548096 | bytes 19922944 | tf_op jit(solution)/shard_map/dot_general | solution.py:14
  90.2 0.0 reduce-scatter.2.cloned.1.call-update
  90.2 0.0 all-gather.8.cloned.1.call-start
  90.2 0.0 copy-done.3
  90.3 0.3 copy.5
  90.6 0.1 reduce_sum.18
  90.7 2.5 %psum.21 = f32[256]{0:T(256)S(1)} all-reduce(f32[256]{0:T(256)S(1)} %reduce_sum.18), channel_id=1, replica_groups=mesh['groups'=2,'frames'=8,'bins'=2] {'bins'}, use_global_device_ids=true, to_apply=%region_2.0 | all-reduce | flops 256 | bytes 2048 | tf_op jit(solution)/shard_map/psum | solution.py:11
  93.2 0.1 dynamic_slice.9
  93.3 7.8 %reduce-scatter.2.cloned.1.call-done = f32[128,2048]{0,1:T(8,128)} async-done(((f32[256,2048]{0,1:T(8,128)}), f32[128,2048]{0,1:T(8,128)}) %reduce-scatter.2.cloned.1.call-update) | async-done | bytes 1048592 | tf_op jit(solution)/shard_map/reduce_scatter | solution.py:15
  101.1 2.3 %multiply_divide_fusion = f32[128,2048]{0,1:T(8,128)} fusion(f32[128,2048]{0,1:T(8,128)S(1)} %copy.5, f32[128,2048]{0,1:T(8,128)} %reduce-scatter.2.cloned.1.call-done, f32[128]{0:T(128)S(1)} %dynamic_slice.9), kind=kLoop, calls=%fused_computation.5 | loop fusion | flops 524288 | bytes 3146240 | tf_op jit(solution)/shard_map/div | solution.py:20
  103.4 0.0 all-gather.8.cloned.1.call-update
  103.4 0.3 all-reduce.2.cloned.1.call-start
  103.7 11.4 %all-gather.8.cloned.1.call-done = f32[256,2048]{0,1:T(8,128)} async-done(((f32[128,2048]{0,1:T(8,128)}), f32[256,2048]{0,1:T(8,128)}) %all-gather.8.cloned.1.call-update) | async-done | bytes 2097168 | tf_op jit(solution)/shard_map/all_gather | solution.py:21
  115.1 0.0 copy-start.1
  115.1 9.1 %fusion.7 = f32[2048,1024]{0,1:T(8,128)S(1)} fusion(f32[256,2048]{0,1:T(8,128)} %all-gather.8.cloned.1.call-done, f32[256,1024]{1,0:T(8,128)S(1)} %copy-done), kind=kOutput, calls=%fused_computation.8 | convolution fusion | flops 6442450944 | bytes 11534336 | tf_op jit(solution)/shard_map/dot_general | solution.py:22
  124.2 0.0 copy-done.1
  124.2 0.0 copy-start.2
  124.2 0.0 copy-start.4
  124.2 17.3 %fusion = f32[256,1024]{1,0:T(8,128)} fusion(f32[256,2048]{0,1:T(8,128)S(1)} %copy-done.1, f32[1024,2048]{1,0:T(8,128)} %param.3, f32[2048,1024]{0,1:T(8,128)S(1)} %fusion.7), kind=kOutput, calls=%fused_computation.1 | convolution fusion | flops 6444548096 | bytes 19922944 | tf_op jit(solution)/shard_map/dot_general | solution.py:24
  141.6 0.0 all-reduce.2.cloned.1.call-update
  141.6 0.0 copy-done.2
  141.6 1.3 copy.6
  142.9 0.3 reduce_sum.19
  143.2 21.9 %psum.23 = f32[256]{0:T(256)S(1)} all-reduce(f32[256]{0:T(256)S(1)} %reduce_sum.19), channel_id=1, replica_groups=mesh['groups'=2,'frames'=8,'bins'=2] {'frames'}, use_global_device_ids=true, to_apply=%region_5.0 | all-reduce | flops 256 | bytes 2048 | tf_op jit(solution)/shard_map/psum | solution.py:34
  165.1 0.1 dynamic_slice.11
  165.2 55.8 %all-reduce.2.cloned.1.call-done = f32[256,1024]{1,0:T(8,128)} async-done(((f32[256,1024]{1,0:T(8,128)}), f32[256,1024]{1,0:T(8,128)}) %all-reduce.2.cloned.1.call-update) | async-done | bytes 1048592 | tf_op jit(solution)/shard_map/psum | solution.py:34
  221.0 0.0 copy-done.4
  221.0 1.6 multiply_divide_fusion.1
Async XLA Ops:
  7.2 45.8 %all-gather.4.cloned.1.call-start = ((), (), s32[]{:S(2)}) async-start(), calls=%async_computation.1 | async-start | bytes 1179648 | tf_op jit(solution)/shard_map/all_gather | solution.py:9
  7.9 56.0 %all-gather.6.cloned.1.call-start = ((), (), s32[]{:S(2)}) async-start(), calls=%async_computation.2 | async-start | bytes 3145728 | tf_op jit(solution)/shard_map/all_gather | solution.py:10
  8.6 92.5 %reduce-scatter.2.cloned.1.call-start = ((), (), s32[]{:S(2)}) async-start(), calls=%async_computation.3 | async-start | bytes 3145728 | tf_op jit(solution)/shard_map/reduce_scatter | solution.py:15
  53.0 20.1 %copy-start = (f32[256,1024]{1,0:T(8,128)S(1)}, f32[256,1024]{1,0:T(8,128)}, u32[]{:S(2)}) copy-start(f32[256,1024]{1,0:T(8,128)} %all-gather.4.cloned.1.call-done) | copy-start | bytes 3145732
  73.2 17.1 %copy-start.3 = (f32[128,2048]{1,0:T(8,128)S(1)}, f32[128,2048]{1,0:T(8,128)}, u32[]{:S(2)}) copy-start(f32[128,2048]{1,0:T(8,128)} %param.5) | copy-start | bytes 3145732
  90.2 24.9 %all-gather.8.cloned.1.call-start = ((), (), s32[]{:S(2)}) async-start(), calls=%async_computation.4 | async-start | bytes 3145728 | tf_op jit(solution)/shard_map/all_gather | solution.py:21
  103.4 117.6 %all-reduce.2.cloned.1.call-start = ((), (), s32[]{:S(2)}) async-start(), calls=%async_computation.5 | async-start | bytes 2097152 | tf_op jit(solution)/shard_map/psum | solution.py:34
  115.1 9.1 %copy-start.1 = (f32[256,2048]{0,1:T(8,128)S(1)}, f32[256,2048]{0,1:T(8,128)}, u32[]{:S(2)}) copy-start(f32[256,2048]{0,1:T(8,128)} %all-gather.8.cloned.1.call-done) | copy-start | bytes 6291460
  124.2 17.4 %copy-start.2 = (f32[128,2048]{0,1:T(8,128)S(1)}, f32[128,2048]{0,1:T(8,128)}, u32[]{:S(2)}) copy-start(f32[128,2048]{0,1:T(8,128)} %multiply_divide_fusion) | copy-start | bytes 3145732
  124.2 96.8 %copy-start.4 = (f32[32,1024]{1,0:T(8,128)S(1)}, f32[32,1024]{1,0:T(8,128)}, u32[]{:S(2)}) copy-start(f32[32,1024]{1,0:T(8,128)} %param.4) | copy-start | bytes 393220
Sparse Core Ops, SparseCore 0:
  10.1 42.8 all-gather.3
  54.5 9.3 all-gather.5
  90.3 10.7 reduce-scatter.1
  103.6 11.5 all-gather.7
  141.7 79.2 all-reduce.1
where the time goes:
time: 229 us
  waiting for transfers between devices  132 us (58%)
  matrix products  52.6 us (23%)
  blocking collectives  24.4 us (11%)
  between operations  13.9 us (6%)
  other arithmetic  4.36 us (2%)
    psum x1, waiting for transfers between devices, body(): basis_total, row_total = lax.psum((basis_part, row_part), 'frames')  55.8 us
    all_gather x1, waiting for transfers between devices, body(): basis = lax.all_gather(atoms_by_bin, 'frames', axis=0, tiled=True)  44.3 us
    psum x1, blocking collectives, body(): basis_total, row_total = lax.psum((basis_part, row_part), 'frames')  21.9 us
    dot_general x1, matrix products, body(): lax.dot_general(fresh_full, ratio_next, (((1,), (1,)), ((), ())), precisi...  17.3 us
    dot_general x1, matrix products, body(): jnp.dot(basis, ratio, precision=highest, preferred_element_type=jnp.float32)  17 us
    all_gather x1, waiting for transfers between devices, body(): fresh_full = lax.all_gather(new_activations, 'bins', axis=0, tiled=True)  11.4 us
    all_gather x1, waiting for transfers between devices, body(): old_full = lax.all_gather(activations, 'bins', axis=0, tiled=True)  10.9 us
    dot_general x1, matrix products, body(): jnp.dot(basis.T, old_full, precision=highest, preferred_element_type=jnp....  9.22 us
  transfers between devices with their start and end apart: 5, of which 5 were waited for; matrix products, arithmetic and copies ran while one was open for 1% of the time, Pallas kernels for 0%

commit v1 on v0

v1 whole, which is shorter than its diff:
```python
import functools

import jax
import jax.numpy as jnp
from jax import lax
from jax.experimental import pallas as pl
from jax.experimental.pallas import tpu as pltpu
from jax.sharding import PartitionSpec as P

f32, bf16 = jnp.float32, jnp.bfloat16
VMEM_LIMIT = 40 * 2**20


def split(x):
    hi = x.astype(bf16)
    return hi, (x - hi.astype(f32)).astype(bf16)


def dot(a, b):
    return jnp.dot(a, b, preferred_element_type=f32)


def dot_nt(a, b):
    return lax.dot_general(a, b, (((1,), (1,)), ((), ())), preferred_element_type=f32)


def quotient(v, m):
    r = pl.reciprocal(m, approx=True)
    r = r * (2.0 - m * r)
    return v * r


def rows_at(start, rows):
    return pl.ds(pl.multiple_of(start * rows, rows), rows)


def first_kernel(idx, v, hown, hoth, *rest, n_w, n_dev, fc):
    ws = rest[:n_w]
    numer, wt3o, mass = rest[n_w : n_w + 3]
    w2, wt3, h, rhi, rlo = rest[n_w + 3 :]
    bins = v.shape[0]
    atoms = h.shape[0]

    @pl.when(pl.program_id(0) == 0)
    def _():
        rows = ws[0].shape[0]
        for s, w in enumerate(ws):
            x = w[...]
            hi, lo = split(x)
            src = lax.rem(idx[0] - s + n_dev, n_dev) if n_w > 1 else 0
            at = rows_at(src, rows)
            at2 = rows_at(src + atoms // rows, rows)
            w2[at, :] = hi
            w2[at2, :] = lo
            mass[at, :] = jnp.broadcast_to(jnp.sum(x, axis=1, keepdims=True), (rows, 128))
        t = w2[:atoms, :].T
        wt3[:, :atoms] = t
        wt3[:, 2 * atoms :] = t
        wt3[:, atoms : 2 * atoms] = w2[atoms:, :].T
        wt3o[...] = wt3[...]

    half = hown.shape[0]
    h[rows_at(idx[1], half), :] = hown[...]
    h[rows_at(1 - idx[1], half), :] = hoth[...]
    hhi, hlo = split(h[...])
    h3 = jnp.concatenate([hhi, hhi, hlo], axis=0)
    for f in range(0, bins, fc):
        m = dot(wt3[f : f + fc, :], h3)
        hi, lo = split(quotient(v[f : f + fc, :], m))
        rhi[f : f + fc, :] = hi
        rlo[f : f + fc, :] = lo
    numer[...] = dot(w2[:atoms, :], rhi[...]) + dot(w2[atoms:, :], rhi[...]) + dot(w2[:atoms, :], rlo[...])


def call_first(idx, spectrum, hown, hoth, ws, n_dev, block=1024, fc=256):
    bins, frames = spectrum.shape
    half = hown.shape[0]
    atoms = 2 * half
    block = min(block, frames)
    part = lambda r: pl.BlockSpec((r, block), lambda i: (0, i))
    whole = lambda a: pl.BlockSpec(a, lambda i: (0, 0))
    return pl.pallas_call(
        functools.partial(first_kernel, n_w=len(ws), n_dev=n_dev, fc=fc),
        grid=(frames // block,),
        in_specs=[pl.BlockSpec(memory_space=pltpu.SMEM), part(bins), part(half), part(half)]
        + [whole(w.shape) for w in ws],
        out_specs=[part(atoms), whole((bins, 3 * atoms)), whole((atoms, 128))],
        out_shape=[
            jax.ShapeDtypeStruct((atoms, frames), f32),
            jax.ShapeDtypeStruct((bins, 3 * atoms), bf16),
            jax.ShapeDtypeStruct((atoms, 128), f32),
        ],
        scratch_shapes=[
            pltpu.VMEM((2 * atoms, bins), bf16),
            pltpu.VMEM((bins, 3 * atoms), bf16),
            pltpu.VMEM((atoms, block), f32),
            pltpu.VMEM((bins, block), bf16),
            pltpu.VMEM((bins, block), bf16),
        ],
        compiler_params=pltpu.CompilerParams(vmem_limit_bytes=VMEM_LIMIT),
    )(idx, spectrum, hown, hoth, *ws)


def second_kernel(idx, v, hown, hoth, nown, noth, massa, massb, wt3, *rest, n_out, n_dev, fc, steps):
    newact = rest[0]
    outs = rest[1 : 1 + n_out]
    h, acc, row_acc, accn = rest[1 + n_out :]
    bins = v.shape[0]
    atoms = h.shape[0]
    half = hown.shape[0]
    i = pl.program_id(0)
    own = rows_at(idx[1], half)
    oth = rows_at(1 - idx[1], half)

    def fresh_of(old, at):
        mass = massa[at, :] + massb[at, :]
        return old[...] * (nown[at, :] + noth[at, :]) / mass[:, :1]

    fresh_own = fresh_of(hown, own)
    newact[...] = fresh_own
    h[own, :] = fresh_own
    h[oth, :] = fresh_of(hoth, oth)
    fresh = h[...]
    hhi, hlo = split(fresh)
    h3 = jnp.concatenate([hhi, hhi, hlo], axis=0)

    @pl.when(i == 0)
    def _():
        row_acc[...] = jnp.zeros_like(row_acc)
        acc[...] = jnp.zeros_like(acc)

    row_acc[...] += jnp.broadcast_to(jnp.sum(fresh, axis=1, keepdims=True), row_acc.shape)
    for f in range(0, bins, fc):
        m = dot(wt3[f : f + fc, :], h3)
        hi, lo = split(quotient(v[f : f + fc, :], m))
        acc[f : f + fc, :] += dot_nt(hi, hhi) + dot_nt(hi, hlo) + dot_nt(lo, hhi)

    @pl.when(i == steps - 1)
    def _():
        accn[...] = acc[...].T
        rows = atoms // n_out
        for s, o in enumerate(outs):
            target = lax.rem(idx[0] + s, n_dev) if n_out > 1 else 0
            at = rows_at(target, rows)
            o[:, :bins] = accn[at, :]
            o[:, bins:] = row_acc[at, :]


def call_second(idx, spectrum, hown, hoth, nown, noth, massa, massb, wt3, n_out, n_dev, block=1024, fc=256):
    bins, frames = spectrum.shape
    half = hown.shape[0]
    atoms = 2 * half
    block = min(block, frames)
    part = lambda r: pl.BlockSpec((r, block), lambda i: (0, i))
    whole = lambda a: pl.BlockSpec(a, lambda i: (0, 0))
    return pl.pallas_call(
        functools.partial(second_kernel, n_out=n_out, n_dev=n_dev, fc=fc, steps=frames // block),
        grid=(frames // block,),
        in_specs=[
            pl.BlockSpec(memory_space=pltpu.SMEM),
            part(bins),
            part(half),
            part(half),
            part(atoms),
            part(atoms),
            whole((atoms, 128)),
            whole((atoms, 128)),
            whole((bins, 3 * atoms)),
        ],
        out_specs=[part(half)] + [whole((atoms // n_out, bins + 128))] * n_out,
        out_shape=[jax.ShapeDtypeStruct((half, frames), f32)]
        + [jax.ShapeDtypeStruct((atoms // n_out, bins + 128), f32)] * n_out,
        scratch_shapes=[
            pltpu.VMEM((atoms, block), f32),
            pltpu.VMEM((bins, atoms), f32),
            pltpu.VMEM((atoms, 128), f32),
            pltpu.VMEM((atoms, bins), f32),
        ],
        compiler_params=pltpu.CompilerParams(vmem_limit_bytes=VMEM_LIMIT),
    )(idx, spectrum, hown, hoth, nown, noth, massa, massb, wt3)


def body(spectrum, atoms_by_bin, activations, *, n_dev):
    swap = [(0, 1), (1, 0)]
    idx = jnp.stack([lax.axis_index("frames"), lax.axis_index("bins")]).astype(jnp.int32)
    bins = spectrum.shape[0]
    rows = atoms_by_bin.shape[0]
    direct = n_dev <= 8 and rows % 16 == 0
    shift = lambda x, s: lax.ppermute(x, "frames", [(i, (i + s) % n_dev) for i in range(n_dev)])
    if direct:
        ws = [atoms_by_bin] + [shift(atoms_by_bin, s) for s in range(1, n_dev)]
    else:
        ws = [lax.all_gather(atoms_by_bin, "frames", axis=0, tiled=True)]
    other = lax.ppermute(activations, "bins", swap)
    numer, wt3, mass = call_first(idx, spectrum, activations, other, ws, n_dev)
    numer_other = lax.ppermute(numer, "bins", swap)
    mass_other = lax.ppermute(mass, "bins", swap)
    n_out = n_dev if direct else 1
    fresh, *parts = call_second(
        idx, spectrum, activations, other, numer, numer_other, mass, mass_other, wt3, n_out, n_dev
    )
    if direct:
        total = parts[0]
        for s in range(1, n_dev):
            total = total + shift(parts[s], s)
    else:
        total = lax.psum_scatter(parts[0], "frames", scatter_dimension=0, tiled=True)
    return fresh, atoms_by_bin * total[:, :bins] / total[:, bins : bins + 1]


def solution(mesh):
    return jax.shard_map(
        functools.partial(body, n_dev=mesh.shape["frames"]),
        mesh=mesh,
        in_specs=(P("bins", ("groups", "frames")), P("frames", ("groups", "bins")), P("bins", ("groups", "frames"))),
        out_specs=(P("bins", ("groups", "frames")), P("frames", ("groups", "bins"))),
        check_vma=False,
    )
```

time: 229 us -> 92.2 us (0.40)
  the two profiles are of different devices: /device:TPU:0 before, /device:TPU:11 now
where the time goes in v1:
time: 92.2 us; the launch traced here: 92.1 us
  waiting for transfers between devices  36.6 us (40%)
  starting transfers between devices  28.5 us (31%)
  Pallas kernels  23.2 us (25%)
  local copies, waits for them, and re-layouts  2.24 us (2%)
    ppermute x14, waiting for transfers between devices, body(): lax.ppermute(x, 'frames', [(i, (i + s) % n_dev) for i in range(n_dev)])  32.7 us
    ppermute x14, starting transfers between devices, body(): lax.ppermute(x, 'frames', [(i, (i + s) % n_dev) for i in range(n_dev)])  26.2 us
    pallas_call x1, Pallas kernels, call_second(): pl.pallas_call(functools.partial(second_kernel, n_out=n_out, n_dev=n_dev,...  12.8 us
    pallas_call x1, Pallas kernels, call_first(): pl.pallas_call(functools.partial(first_kernel, n_w=len(ws), n_dev=n_dev,...  10.4 us
    ppermute x1, waiting for transfers between devices, body(): mass_other = lax.ppermute(mass, 'bins', swap)  3.89 us
    unnamed x6, local copies, waits for them, and re-layouts  2.13 us
  transfers between devices with their start and end apart: 17, of which 10 were waited for; matrix products, arithmetic and copies ran while one was open for 0% of the time, Pallas kernels for 0%

profile of v1, /device:TPU:11, one launch (start us, length us, event | category | flops | bytes accessed | tf_op | source)
XLA Modules:
  0.0 92.1 jit_solution(14276885427178026253)
XLA Ops:
  0.6 0.7 collective-permute-start
  1.4 0.3 collective-permute-start.7
  1.6 0.0 collective-permute-start.6
  1.6 4.3 %collective-permute-start.5 = (f32[32,1024]{1,0:T(8,128)}, f32[32,1024]{1,0:T(8,128)S(1)}, u32[]{:S(2)}, u32[]{:S(2)}) collective-permute-start(f32[32,1024]{1,0:T(8,128)} %rest_0_.1), channel_id=1, source_target_pairs={{0,10},{2,12},{4,14},{6,0},{8,2},{10,4},{12,6},{14,8},{1,11},{3,13... | collective-permute-start | bytes 393224 | tf_op jit(solution)/shard_map/ppermute | solution.py:189
  5.9 0.0 collective-permute-start.4
  5.9 1.6 %collective-permute-done.7.rest_7_ = f32[32,1024]{1,0:T(8,128)S(1)} collective-permute-done((f32[32,1024]{1,0:T(8,128)}, f32[32,1024]{1,0:T(8,128)S(1)}, u32[]{:S(2)}, u32[]{:S(2)}) %collective-permute-start.7) | collective-permute-done | bytes 131104 | tf_op jit(solution)/shard_map/ppermute | solution.py:189
  7.5 1.4 %collective-permute-start.3 = (f32[32,1024]{1,0:T(8,128)}, f32[32,1024]{1,0:T(8,128)S(1)}, u32[]{:S(2)}, u32[]{:S(2)}) collective-permute-start(f32[32,1024]{1,0:T(8,128)} %rest_0_.1), channel_id=1, source_target_pairs={{0,6},{2,8},{4,10},{6,12},{8,14},{10,0},{12,2},{14,4},{1,7},{3,9},... | collective-permute-start | bytes 393224 | tf_op jit(solution)/shard_map/ppermute | solution.py:189
  8.9 0.0 collective-permute-done.6.rest_6_
  8.9 1.2 %collective-permute-start.2 = (f32[32,1024]{1,0:T(8,128)}, f32[32,1024]{1,0:T(8,128)S(1)}, u32[]{:S(2)}, u32[]{:S(2)}) collective-permute-start(f32[32,1024]{1,0:T(8,128)} %rest_0_.1), channel_id=1, source_target_pairs={{0,4},{2,6},{4,8},{6,10},{8,12},{10,14},{12,0},{14,2},{1,5},{3,7},... | collective-permute-start | bytes 393224 | tf_op jit(solution)/shard_map/ppermute | solution.py:189
  10.2 4.0 %collective-permute-done.5.rest_5_ = f32[32,1024]{1,0:T(8,128)S(1)} collective-permute-done((f32[32,1024]{1,0:T(8,128)}, f32[32,1024]{1,0:T(8,128)S(1)}, u32[]{:S(2)}, u32[]{:S(2)}) %collective-permute-start.5) | collective-permute-done | bytes 131104 | tf_op jit(solution)/shard_map/ppermute | solution.py:189
  14.2 9.5 %collective-permute-start.1 = (f32[32,1024]{1,0:T(8,128)}, f32[32,1024]{1,0:T(8,128)S(1)}, u32[]{:S(2)}, u32[]{:S(2)}) collective-permute-start(f32[32,1024]{1,0:T(8,128)} %rest_0_.1), channel_id=1, source_target_pairs={{0,2},{2,4},{4,6},{6,8},{8,10},{10,12},{12,14},{14,0},{1,3},{3,5},... | collective-permute-start | bytes 393224 | tf_op jit(solution)/shard_map/ppermute | solution.py:189
  23.8 0.1 pad_add_fusion.idx
  23.8 0.0 collective-permute-done.4.rest_4_
  23.8 0.0 collective-permute-done.3.rest_3_
  23.8 1.4 %collective-permute-done.2.rest_2_ = f32[32,1024]{1,0:T(8,128)S(1)} collective-permute-done((f32[32,1024]{1,0:T(8,128)}, f32[32,1024]{1,0:T(8,128)S(1)}, u32[]{:S(2)}, u32[]{:S(2)}) %collective-permute-start.2) | collective-permute-done | bytes 131104 | tf_op jit(solution)/shard_map/ppermute | solution.py:189
  25.3 1.8 %collective-permute-done.1.rest_1_ = f32[32,1024]{1,0:T(8,128)S(1)} collective-permute-done((f32[32,1024]{1,0:T(8,128)}, f32[32,1024]{1,0:T(8,128)S(1)}, u32[]{:S(2)}, u32[]{:S(2)}) %collective-permute-start.1) | collective-permute-done | bytes 131104 | tf_op jit(solution)/shard_map/ppermute | solution.py:189
  27.1 0.0 collective-permute-done.hoth
  27.1 0.0 copy-start
  27.1 1.2 %copy-done = f32[128,2048]{1,0:T(8,128)S(1)} copy-done((f32[128,2048]{1,0:T(8,128)S(1)}, f32[128,2048]{1,0:T(8,128)}, u32[]{:S(2)}) %copy-start) | copy-done | bytes 1048600
  28.3 0.0 copy-start.1
  28.3 0.9 copy-done.1
  29.2 10.4 %shard_map.50 = (f32[256,2048]{1,0:T(8,128)S(1)}, bf16[1024,768]{1,0:T(8,128)(2,1)S(1)}, f32[256,128]{1,0:T(8,128)S(1)}) custom-call(s32[2]{0:T(128)S(1)} %pad_add_fusion.idx, f32[1024,2048]{1,0:T(8,128)} %v.3, f32[128,2048]{1,0:T(8,128)S(1)} %copy-done, f32[128,2048]{1,0:T(8,128)S(1)} %collective-permute-done.hoth, f32[32,1024]{1,0:T(8,128)S(1)} %copy-done.1, ...), custom_call_target="tpu_custom_call" | custom-call | tf_op jit(solution)/shard_map/pallas_call | solution.py:82
  39.7 1.5 %collective-permute-start.8 = (f32[256,2048]{1,0:T(8,128)S(1)}, f32[256,2048]{1,0:T(8,128)S(1)}, u32[]{:S(2)}, u32[]{:S(2)}) collective-permute-start(f32[256,2048]{1,0:T(8,128)S(1)} %get-tuple-element.14.nown), channel_id=1, source_target_pairs={{0,1},{1,0},{2,3},{3,2},{4,5},{5,4},{6,7},{7,6},{8,9},{9,8},{10,11... | collective-permute-start | bytes 6291464 | tf_op jit(solution)/shard_map/ppermute | solution.py:196
  41.2 0.1 collective-permute-start.9
  41.3 3.9 %collective-permute-done.9.massb = f32[256,128]{1,0:T(8,128)S(1)} collective-permute-done((f32[256,128]{1,0:T(8,128)S(1)}, f32[256,128]{1,0:T(8,128)S(1)}, u32[]{:S(2)}, u32[]{:S(2)}) %collective-permute-start.9) | collective-permute-done | bytes 131104 | tf_op jit(solution)/shard_map/ppermute | solution.py:197
  45.2 0.0 collective-permute-done.8.noth
  45.2 0.0 copy-start.2
  45.2 12.8 %shard_map.51 = (f32[128,2048]{1,0:T(8,128)}, f32[32,1152]{1,0:T(8,128)S(1)}, f32[32,1152]{1,0:T(8,128)S(1)}, f32[32,1152]{1,0:T(8,128)S(1)}, f32[32,1152]{1,0:T...) custom-call(s32[2]{0:T(128)S(1)} %pad_add_fusion.idx, ...), custom_call_target="tpu_custom_call" | custom-call | tf_op jit(solution)/shard_map/pallas_call | solution.py:156
  58.0 3.0 %collective-permute-start.10 = (f32[32,1152]{1,0:T(8,128)S(1)}, f32[32,1152]{1,0:T(8,128)S(1)}, u32[]{:S(2)}, u32[]{:S(2)}) collective-permute-start(f32[32,1152]{1,0:T(8,128)S(1)} %get-tuple-element.19), channel_id=1, source_target_pairs={{0,2},{2,4},{4,6},{6,8},{8,10},{10,12},{12,14},{14,0},{1,3},{3,5},... | collective-permute-start | bytes 442376 | tf_op jit(solution)/shard_map/ppermute | solution.py:189
  60.9 0.0 collective-permute-start.11
  61.0 3.8 %collective-permute-start.12 = (f32[32,1152]{1,0:T(8,128)S(1)}, f32[32,1152]{1,0:T(8,128)S(1)}, u32[]{:S(2)}, u32[]{:S(2)}) collective-permute-start(f32[32,1152]{1,0:T(8,128)S(1)} %get-tuple-element.21), channel_id=1, source_target_pairs={{0,6},{2,8},{4,10},{6,12},{8,14},{10,0},{12,2},{14,4},{1,7},{3,9},... | collective-permute-start | bytes 442376 | tf_op jit(solution)/shard_map/ppermute | solution.py:189
  64.7 0.0 collective-permute-start.13
  64.7 1.8 %collective-permute-start.14 = (f32[32,1152]{1,0:T(8,128)S(1)}, f32[32,1152]{1,0:T(8,128)S(1)}, u32[]{:S(2)}, u32[]{:S(2)}) collective-permute-start(f32[32,1152]{1,0:T(8,128)S(1)} %get-tuple-element.23), channel_id=1, source_target_pairs={{0,10},{2,12},{4,14},{6,0},{8,2},{10,4},{12,6},{14,8},{1,11},{3,13... | collective-permute-start | bytes 442376 | tf_op jit(solution)/shard_map/ppermute | solution.py:189
  66.5 0.0 collective-permute-done.10
  66.5 0.9 collective-permute-start.15
  67.4 1.4 %collective-permute-done.11 = f32[32,1152]{1,0:T(8,128)S(1)} collective-permute-done((f32[32,1152]{1,0:T(8,128)S(1)}, f32[32,1152]{1,0:T(8,128)S(1)}, u32[]{:S(2)}, u32[]{:S(2)}) %collective-permute-start.11) | collective-permute-done | bytes 147488 | tf_op jit(solution)/shard_map/ppermute | solution.py:189
  68.8 0.0 collective-permute-start.16
  68.8 13.9 %collective-permute-done.12 = f32[32,1152]{1,0:T(8,128)S(1)} collective-permute-done((f32[32,1152]{1,0:T(8,128)S(1)}, f32[32,1152]{1,0:T(8,128)S(1)}, u32[]{:S(2)}, u32[]{:S(2)}) %collective-permute-start.12) | collective-permute-done | bytes 147488 | tf_op jit(solution)/shard_map/ppermute | solution.py:189
  82.7 3.2 %collective-permute-done.13 = f32[32,1152]{1,0:T(8,128)S(1)} collective-permute-done((f32[32,1152]{1,0:T(8,128)S(1)}, f32[32,1152]{1,0:T(8,128)S(1)}, u32[]{:S(2)}, u32[]{:S(2)}) %collective-permute-start.13) | collective-permute-done | bytes 147488 | tf_op jit(solution)/shard_map/ppermute | solution.py:189
  85.9 0.0 collective-permute-done.14
  85.9 3.2 %collective-permute-done.15 = f32[32,1152]{1,0:T(8,128)S(1)} collective-permute-done((f32[32,1152]{1,0:T(8,128)S(1)}, f32[32,1152]{1,0:T(8,128)S(1)}, u32[]{:S(2)}, u32[]{:S(2)}) %collective-permute-start.15) | collective-permute-done | bytes 147488 | tf_op jit(solution)/shard_map/ppermute | solution.py:189
  89.1 2.1 %collective-permute-done.16 = f32[32,1152]{1,0:T(8,128)S(1)} collective-permute-done((f32[32,1152]{1,0:T(8,128)S(1)}, f32[32,1152]{1,0:T(8,128)S(1)}, u32[]{:S(2)}, u32[]{:S(2)}) %collective-permute-start.16) | collective-permute-done | bytes 147488 | tf_op jit(solution)/shard_map/ppermute | solution.py:189
  91.1 0.1 add_add_fusion
  91.2 0.1 slice_reduce_fusion
  91.3 0.0 copy-done.2
  91.3 0.7 fusion
Async XLA Ops:
  0.6 26.5 %collective-permute-start = (f32[128,2048]{1,0:T(8,128)}, f32[128,2048]{1,0:T(8,128)S(1)}, u32[]{:S(2)}, u32[]{:S(2)}) collective-permute-start(f32[128,2048]{1,0:T(8,128)} %hown.3), channel_id=1, source_target_pairs={{0,1},{1,0},{2,3},{3,2},{4,5},{5,4},{6,7},{7,6},{8,9},{9,8},{10,11... | collective-permute-start | bytes 3145736 | tf_op jit(solution)/shard_map/ppermute | solution.py:194
  1.4 6.2 %collective-permute-start.7 = (f32[32,1024]{1,0:T(8,128)}, f32[32,1024]{1,0:T(8,128)S(1)}, u32[]{:S(2)}, u32[]{:S(2)}) collective-permute-start(f32[32,1024]{1,0:T(8,128)} %rest_0_.1), channel_id=1, source_target_pairs={{0,14},{2,0},{4,2},{6,4},{8,6},{10,8},{12,10},{14,12},{1,15},{3,1}... | collective-permute-start | bytes 393224 | tf_op jit(solution)/shard_map/ppermute | solution.py:189
  1.6 7.3 %collective-permute-start.6 = (f32[32,1024]{1,0:T(8,128)}, f32[32,1024]{1,0:T(8,128)S(1)}, u32[]{:S(2)}, u32[]{:S(2)}) collective-permute-start(f32[32,1024]{1,0:T(8,128)} %rest_0_.1), channel_id=1, source_target_pairs={{0,12},{2,14},{4,0},{6,2},{8,4},{10,6},{12,8},{14,10},{1,13},{3,15... | collective-permute-start | bytes 393224 | tf_op jit(solution)/shard_map/ppermute | solution.py:189
  1.6 12.6 %collective-permute-start.5 = (f32[32,1024]{1,0:T(8,128)}, f32[32,1024]{1,0:T(8,128)S(1)}, u32[]{:S(2)}, u32[]{:S(2)}) collective-permute-start(f32[32,1024]{1,0:T(8,128)} %rest_0_.1), channel_id=1, source_target_pairs={{0,10},{2,12},{4,14},{6,0},{8,2},{10,4},{12,6},{14,8},{1,11},{3,13... | collective-permute-start | bytes 393224 | tf_op jit(solution)/shard_map/ppermute | solution.py:189
  5.9 17.9 %collective-permute-start.4 = (f32[32,1024]{1,0:T(8,128)}, f32[32,1024]{1,0:T(8,128)S(1)}, u32[]{:S(2)}, u32[]{:S(2)}) collective-permute-start(f32[32,1024]{1,0:T(8,128)} %rest_0_.1), channel_id=1, source_target_pairs={{0,8},{2,10},{4,12},{6,14},{8,0},{10,2},{12,4},{14,6},{1,9},{3,11}... | collective-permute-start | bytes 393224 | tf_op jit(solution)/shard_map/ppermute | solution.py:189
  7.5 16.3 %collective-permute-start.3 = (f32[32,1024]{1,0:T(8,128)}, f32[32,1024]{1,0:T(8,128)S(1)}, u32[]{:S(2)}, u32[]{:S(2)}) collective-permute-start(f32[32,1024]{1,0:T(8,128)} %rest_0_.1), channel_id=1, source_target_pairs={{0,6},{2,8},{4,10},{6,12},{8,14},{10,0},{12,2},{14,4},{1,7},{3,9},... | collective-permute-start | bytes 393224 | tf_op jit(solution)/shard_map/ppermute | solution.py:189
  8.9 16.4 %collective-permute-start.2 = (f32[32,1024]{1,0:T(8,128)}, f32[32,1024]{1,0:T(8,128)S(1)}, u32[]{:S(2)}, u32[]{:S(2)}) collective-permute-start(f32[32,1024]{1,0:T(8,128)} %rest_0_.1), channel_id=1, source_target_pairs={{0,4},{2,6},{4,8},{6,10},{8,12},{10,14},{12,0},{14,2},{1,5},{3,7},... | collective-permute-start | bytes 393224 | tf_op jit(solution)/shard_map/ppermute | solution.py:189
  14.2 12.9 %collective-permute-start.1 = (f32[32,1024]{1,0:T(8,128)}, f32[32,1024]{1,0:T(8,128)S(1)}, u32[]{:S(2)}, u32[]{:S(2)}) collective-permute-start(f32[32,1024]{1,0:T(8,128)} %rest_0_.1), channel_id=1, source_target_pairs={{0,2},{2,4},{4,6},{6,8},{8,10},{10,12},{12,14},{14,0},{1,3},{3,5},... | collective-permute-start | bytes 393224 | tf_op jit(solution)/shard_map/ppermute | solution.py:189
  27.1 1.2 %copy-start = (f32[128,2048]{1,0:T(8,128)S(1)}, f32[128,2048]{1,0:T(8,128)}, u32[]{:S(2)}) copy-start(f32[128,2048]{1,0:T(8,128)} %hown.3) | copy-start | bytes 3145732
  28.3 0.9 copy-start.1
  39.7 5.5 %collective-permute-start.8 = (f32[256,2048]{1,0:T(8,128)S(1)}, f32[256,2048]{1,0:T(8,128)S(1)}, u32[]{:S(2)}, u32[]{:S(2)}) collective-permute-start(f32[256,2048]{1,0:T(8,128)S(1)} %get-tuple-element.14.nown), channel_id=1, source_target_pairs={{0,1},{1,0},{2,3},{3,2},{4,5},{5,4},{6,7},{7,6},{8,9},{9,8},{10,11... | collective-permute-start | bytes 6291464 | tf_op jit(solution)/shard_map/ppermute | solution.py:196
  41.2 4.0 %collective-permute-start.9 = (f32[256,128]{1,0:T(8,128)S(1)}, f32[256,128]{1,0:T(8,128)S(1)}, u32[]{:S(2)}, u32[]{:S(2)}) collective-permute-start(f32[256,128]{1,0:T(8,128)S(1)} %get-tuple-element.15.massa), channel_id=1, source_target_pairs={{0,1},{1,0},{2,3},{3,2},{4,5},{5,4},{6,7},{7,6},{8,9},{9,8},{10,11... | collective-permute-start | bytes 393224 | tf_op jit(solution)/shard_map/ppermute | solution.py:197
  45.2 46.2 %copy-start.2 = (f32[32,1024]{1,0:T(8,128)S(1)}, f32[32,1024]{1,0:T(8,128)}, u32[]{:S(2)}) copy-start(f32[32,1024]{1,0:T(8,128)} %rest_0_.1) | copy-start | bytes 393220
  58.0 8.6 %collective-permute-start.10 = (f32[32,1152]{1,0:T(8,128)S(1)}, f32[32,1152]{1,0:T(8,128)S(1)}, u32[]{:S(2)}, u32[]{:S(2)}) collective-permute-start(f32[32,1152]{1,0:T(8,128)S(1)} %get-tuple-element.19), channel_id=1, source_target_pairs={{0,2},{2,4},{4,6},{6,8},{8,10},{10,12},{12,14},{14,0},{1,3},{3,5},... | collective-permute-start | bytes 442376 | tf_op jit(solution)/shard_map/ppermute | solution.py:189
  60.9 7.9 %collective-permute-start.11 = (f32[32,1152]{1,0:T(8,128)S(1)}, f32[32,1152]{1,0:T(8,128)S(1)}, u32[]{:S(2)}, u32[]{:S(2)}) collective-permute-start(f32[32,1152]{1,0:T(8,128)S(1)} %get-tuple-element.20), channel_id=1, source_target_pairs={{0,4},{2,6},{4,8},{6,10},{8,12},{10,14},{12,0},{14,2},{1,5},{3,7},... | collective-permute-start | bytes 442376 | tf_op jit(solution)/shard_map/ppermute | solution.py:189
  61.0 21.8 %collective-permute-start.12 = (f32[32,1152]{1,0:T(8,128)S(1)}, f32[32,1152]{1,0:T(8,128)S(1)}, u32[]{:S(2)}, u32[]{:S(2)}) collective-permute-start(f32[32,1152]{1,0:T(8,128)S(1)} %get-tuple-element.21), channel_id=1, source_target_pairs={{0,6},{2,8},{4,10},{6,12},{8,14},{10,0},{12,2},{14,4},{1,7},{3,9},... | collective-permute-start | bytes 442376 | tf_op jit(solution)/shard_map/ppermute | solution.py:189
  64.7 21.2 %collective-permute-start.13 = (f32[32,1152]{1,0:T(8,128)S(1)}, f32[32,1152]{1,0:T(8,128)S(1)}, u32[]{:S(2)}, u32[]{:S(2)}) collective-permute-start(f32[32,1152]{1,0:T(8,128)S(1)} %get-tuple-element.22), channel_id=1, source_target_pairs={{0,8},{2,10},{4,12},{6,14},{8,0},{10,2},{12,4},{14,6},{1,9},{3,11}... | collective-permute-start | bytes 442376 | tf_op jit(solution)/shard_map/ppermute | solution.py:189
  64.7 21.2 %collective-permute-start.14 = (f32[32,1152]{1,0:T(8,128)S(1)}, f32[32,1152]{1,0:T(8,128)S(1)}, u32[]{:S(2)}, u32[]{:S(2)}) collective-permute-start(f32[32,1152]{1,0:T(8,128)S(1)} %get-tuple-element.23), channel_id=1, source_target_pairs={{0,10},{2,12},{4,14},{6,0},{8,2},{10,4},{12,6},{14,8},{1,11},{3,13... | collective-permute-start | bytes 442376 | tf_op jit(solution)/shard_map/ppermute | solution.py:189
  66.5 22.6 %collective-permute-start.15 = (f32[32,1152]{1,0:T(8,128)S(1)}, f32[32,1152]{1,0:T(8,128)S(1)}, u32[]{:S(2)}, u32[]{:S(2)}) collective-permute-start(f32[32,1152]{1,0:T(8,128)S(1)} %get-tuple-element.24), channel_id=1, source_target_pairs={{0,12},{2,14},{4,0},{6,2},{8,4},{10,6},{12,8},{14,10},{1,13},{3,15... | collective-permute-start | bytes 442376 | tf_op jit(solution)/shard_map/ppermute | solution.py:189
  68.8 22.3 %collective-permute-start.16 = (f32[32,1152]{1,0:T(8,128)S(1)}, f32[32,1152]{1,0:T(8,128)S(1)}, u32[]{:S(2)}, u32[]{:S(2)}) collective-permute-start(f32[32,1152]{1,0:T(8,128)S(1)} %get-tuple-element.25), channel_id=1, source_target_pairs={{0,14},{2,0},{4,2},{6,4},{8,6},{10,8},{12,10},{14,12},{1,15},{3,1}... | collective-permute-start | bytes 442376 | tf_op jit(solution)/shard_map/ppermute | solution.py:189

commit v2 on v0

v2 whole, which is shorter than its diff:
```python
import functools

import jax
import jax.numpy as jnp
from jax import lax
from jax.experimental import pallas as pl
from jax.experimental.pallas import tpu as pltpu
from jax.sharding import PartitionSpec as P

f32, bf16 = jnp.float32, jnp.bfloat16
WHOLE = pl.BlockSpec(memory_space=pltpu.VMEM)
SCALARS = pl.BlockSpec(memory_space=pltpu.SMEM)
PARAMS = pltpu.CompilerParams(vmem_limit_bytes=36 * 2**20)
CROSS = 6


def split(x):
    hi = x.astype(bf16)
    return hi, (x - hi.astype(f32)).astype(bf16)


def dot(a, b):
    return jnp.dot(a, b, preferred_element_type=f32)


def dot_nt(a, b):
    return lax.dot_general(a, b, (((1,), (1,)), ((), ())), preferred_element_type=f32)


def rows_at(start, rows):
    return pl.ds(pl.multiple_of(start * rows, rows), rows)


def prepare_activations(idx, hown, hoth, h2):
    half = hown.shape[0]
    for place, old in ((idx[1], hown), (1 - idx[1], hoth)):
        hi, lo = split(old[...])
        h2[rows_at(place, half), :] = hi
        h2[rows_at(place + 2, half), :] = lo


def prepare_basis(idx, *refs, first):
    *ws, w2, wt, mass = refs
    rows = ws[0].shape[0]
    half = len(ws) * rows
    for s, w in enumerate(ws):
        x = w[...]
        hi, lo = split(x)
        place = (idx[0] ^ (s ^ first)) if len(ws) > 1 else 0
        w2[rows_at(place, rows), :] = hi
        w2[rows_at(place + half // rows, rows), :] = lo
        mass[rows_at(place, rows), :] = jnp.broadcast_to(jnp.sum(x, axis=1, keepdims=True), (rows, 128))
    wt[...] = w2[...].T


def first_kernel(h2, v, *refs, fc, nc):
    *parts, numer, rhi, rlo = refs
    w2, wt = parts[0::2], parts[1::2]
    bins, frames = v.shape
    atoms = h2.shape[0] // 2
    half = w2[0].shape[0] // 2
    whi = jnp.concatenate([w[:half, :] for w in w2], axis=0)
    wlo = jnp.concatenate([w[half:, :] for w in w2], axis=0)
    for n in range(0, frames, nc):
        at = slice(n, n + nc)
        hhi, hlo = h2[:atoms, at], h2[atoms:, at]
        h3 = jnp.concatenate([hhi, hhi, hlo], axis=0)
        for f in range(0, bins, fc):
            wthi = [w[f : f + fc, :half] for w in wt]
            wtlo = [w[f : f + fc, half:] for w in wt]
            m = dot(jnp.concatenate(wthi + wtlo + wthi, axis=1), h3)
            hi, lo = split(v[f : f + fc, at] / m)
            rhi[f : f + fc, at] = hi
            rlo[f : f + fc, at] = lo
        numer[:, at] = dot(whi, rhi[:, at]) + dot(wlo, rhi[:, at]) + dot(whi, rlo[:, at])


def second_kernel(idx, v, hown, hoth, nown, noth, *refs, n_parts, n_out, fc, nc):
    wt = refs[:n_parts]
    masses = refs[n_parts : 3 * n_parts]
    newact = refs[3 * n_parts]
    outs = refs[3 * n_parts + 1 : 3 * n_parts + 1 + n_out]
    h, acc, mass, row_mass = refs[3 * n_parts + 1 + n_out :]
    bins, frames = v.shape
    atoms = h.shape[0]
    half = hown.shape[0]
    part = atoms // n_parts
    for p in range(n_parts):
        mass[p * part : (p + 1) * part, :] = masses[p][...] + masses[n_parts + p][...]
    own, oth = rows_at(idx[1], half), rows_at(1 - idx[1], half)
    sums = None
    for n in range(0, frames, nc):
        at = slice(n, n + nc)
        fresh = hown[:, at] * (nown[own, at] + noth[own, at]) / mass[own, :1]
        newact[:, at] = fresh
        h[own, :] = fresh
        h[oth, :] = hoth[:, at] * (nown[oth, at] + noth[oth, at]) / mass[oth, :1]
        fresh = h[...]
        hhi, hlo = split(fresh)
        h3 = jnp.concatenate([hhi, hhi, hlo], axis=0)
        row = jnp.sum(fresh, axis=1, keepdims=True)
        sums = row if sums is None else sums + row
        for f in range(0, bins, fc):
            wthi = [w[f : f + fc, :part] for w in wt]
            wtlo = [w[f : f + fc, part:] for w in wt]
            m = dot(jnp.concatenate(wthi + wtlo + wthi, axis=1), h3)
            hi, lo = split(v[f : f + fc, at] / m)
            term = dot_nt(hhi, hi) + dot_nt(hlo, hi) + dot_nt(hhi, lo)
            if n == 0:
                acc[:, f : f + fc] = term
            else:
                acc[:, f : f + fc] += term
    row_mass[...] = jnp.broadcast_to(sums, row_mass.shape)
    if n_out == 1:
        outs[0][:, :bins] = acc[...]
        outs[0][:, bins:] = row_mass[...]
        return
    rows = atoms // n_out
    lane = lax.broadcasted_iota(jnp.int32, (8, 128), 1) // (1024 // rows)
    for s, o in enumerate(outs):
        place = (idx[0] ^ (s & 3)) + (s & 4)
        base = pl.multiple_of(place * rows, rows)
        packed = jnp.zeros((8, 128), f32)
        for i in range(rows // 8):
            at = pl.ds(base + 8 * i, 8)
            packed = jnp.where(lane == i, row_mass[at, :], packed)
            for j in range(bins // 128):
                k = 8 * (i * (bins // 128) + j)
                o[k : k + 8, :] = acc[at, 128 * j : 128 * (j + 1)]
        o[rows * bins // 128 :, :] = packed


def last_kernel(old, total, more, new):
    rows, bins = old.shape
    x = total[rows * bins // 128 :, :] + more[rows * bins // 128 :, :]
    for i in range(rows // 8):
        lane = i * (1024 // rows)
        mass = x[:, lane : lane + 1]
        for j in range(bins // 128):
            k = 8 * (i * (bins // 128) + j)
            at = (slice(8 * i, 8 * i + 8), slice(128 * j, 128 * (j + 1)))
            new[at] = old[at] * (total[k : k + 8, :] + more[k : k + 8, :]) / mass


def call(kernel, ins, outs, scratch=(), scalars=False):
    in_specs = [WHOLE] * len(ins)
    if scalars:
        in_specs[0] = SCALARS
    return pl.pallas_call(
        kernel,
        in_specs=in_specs,
        out_specs=[WHOLE] * len(outs),
        out_shape=[jax.ShapeDtypeStruct(*o) for o in outs],
        scratch_shapes=[pltpu.VMEM(*s) for s in scratch],
        compiler_params=PARAMS,
    )(*ins)


def hop(x, step):
    return lax.ppermute(x, "frames", [(i, i ^ step) for i in range(8)])


def body(spectrum, atoms_by_bin, activations, *, n_dev):
    swap = lambda x: lax.ppermute(x, "bins", [(0, 1), (1, 0)])
    bins, frames = spectrum.shape
    half = activations.shape[0]
    atoms = 2 * half
    rows = atoms_by_bin.shape[0]
    cube = n_dev == 8 and rows % 16 == 0
    place, core = lax.axis_index("frames"), lax.axis_index("bins")
    idx = jnp.stack([place & 3, core ^ (place >> 2)] if cube else [place, core]).astype(jnp.int32)

    def prepare(ws, first):
        k = sum(w.shape[0] for w in ws)
        return call(
            functools.partial(prepare_basis, first=first),
            [idx, *ws],
            [((2 * k, bins), bf16), ((bins, 2 * k), bf16), ((k, 128), f32)],
            scalars=True,
        )

    if cube:
        far = hop(atoms_by_bin, CROSS)
        near = [hop(atoms_by_bin, s) for s in (1, 2, 3)]
        fars = [hop(far, s) for s in (1, 2, 3)]
        basis = [prepare([atoms_by_bin, *near], 0), prepare([far, *fars], CROSS & 3)]
    else:
        basis = [prepare([lax.all_gather(atoms_by_bin, "frames", axis=0, tiled=True)], 0)]
    other = swap(activations)
    (h2,) = call(prepare_activations, [idx, activations, other], [((2 * atoms, frames), bf16)], scalars=True)
    w2, wt, mass = zip(*basis)
    (numer,) = call(
        functools.partial(first_kernel, fc=256, nc=512),
        [h2, spectrum, *[x for b in basis for x in b[:2]]],
        [((atoms, frames), f32)],
        scratch=[((bins, frames), bf16), ((bins, frames), bf16)],
    )
    mass_other = [swap(m) for m in mass]
    n_out = n_dev if cube else 1
    out = (rows * bins // 128 + 8, 128) if cube else (atoms, bins + 128)
    fresh, *parts = call(
        functools.partial(second_kernel, n_parts=len(basis), n_out=n_out, fc=256, nc=512),
        [idx, spectrum, activations, other, numer, swap(numer), *wt, *mass, *mass_other],
        [((half, frames), f32)] + [(out, f32)] * n_out,
        scratch=[((atoms, 512), f32), ((atoms, bins), f32), ((atoms, 128), f32), ((atoms, 128), f32)],
        scalars=True,
    )
    if cube:
        total = parts[CROSS]
        for s in (3, 2, 1):
            total = total + hop(parts[s ^ CROSS], s)
        more = hop(total, CROSS)
        total = parts[0]
        for s in (3, 2, 1):
            total = total + hop(parts[s], s)
        (new,) = call(last_kernel, [atoms_by_bin, total, more], [((rows, bins), f32)])
        return fresh, new
    total = lax.psum_scatter(parts[0], "frames", scatter_dimension=0, tiled=True)
    return fresh, atoms_by_bin * total[:, :bins] / total[:, bins : bins + 1]


def solution(mesh):
    return jax.shard_map(
        functools.partial(body, n_dev=mesh.shape["frames"]),
        mesh=mesh,
        in_specs=(P("bins", ("groups", "frames")), P("frames", ("groups", "bins")), P("bins", ("groups", "frames"))),
        out_specs=(P("bins", ("groups", "frames")), P("frames", ("groups", "bins"))),
        check_vma=False,
    )
```

time: 229 us -> 68.2 us (0.30)
  waiting for transfers between devices: 132 us -> 16.6 us
  matrix products: 52.6 us -> 0 us
  starting transfers between devices: 0.42 us -> 25.7 us
  blocking collectives: 24.4 us -> 0 us
  Pallas kernels: 0 us -> 19.4 us
  between operations: 13.9 us -> 0.71 us
  other arithmetic: 4.36 us -> 0.16 us
  local copies, waits for them, and re-layouts: 1.81 us -> 5.51 us
    all_gather x3 -> x0, waiting for transfers between devices: 66.6 us -> none  [the longest x1 44.3 us: body(): basis = lax.all_gather(atoms_by_bin, 'frames', axis=0, tiled=True)]
    psum x1 -> x0, waiting for transfers between devices: 55.8 us -> none  [body(): basis_total, row_total = lax.psum((basis_part, row_part), 'frames')]
    dot_general x4 -> x0, matrix products: 52.6 us -> none  [the longest x1 17.3 us: body(): lax.dot_general(fresh_full, ratio_next, (((1,), (1,)), ((), ())), precisi...]
    ppermute x0 -> x18, starting transfers between devices: none -> 25.7 us  [the longest x14 24.5 us: hop(): return lax.ppermute(x, 'frames', [(i, i ^ step) for i in range(8)])]
    psum x2 -> x0, blocking collectives: 24.4 us -> none  [the longest x1 21.9 us: body(): basis_total, row_total = lax.psum((basis_part, row_part), 'frames')]
    pallas_call x0 -> x6, Pallas kernels: none -> 19.4 us  [call(): pl.pallas_call(kernel, in_specs=in_specs, out_specs=[WHOLE] * len(outs),...]
    ppermute x0 -> x18, waiting for transfers between devices: none -> 16.6 us  [the longest x14 12.8 us: hop(): return lax.ppermute(x, 'frames', [(i, i ^ step) for i in range(8)])]
    reduce_scatter x1 -> x0, waiting for transfers between devices: 7.84 us -> none  [body(): lax.psum_scatter(numer_part, 'bins', scatter_dimension=0, tiled=True)]
  transfers between devices with their start and end apart: 5 -> 18, of which waited for: 5 -> 13; matrix products, arithmetic and copies ran while one was open for 1% -> 0% of each run, Pallas kernels for 0% -> 2%
where the time goes in v2:
time: 68.2 us; the launch traced here: 68 us
  starting transfers between devices  25.7 us (38%)
  Pallas kernels  19.4 us (28%)
  waiting for transfers between devices  16.6 us (24%)
  local copies, waits for them, and re-layouts  5.51 us (8%)
  between operations  0.71 us (1%)
    ppermute x14, starting transfers between devices, hop(): return lax.ppermute(x, 'frames', [(i, i ^ step) for i in range(8)])  24.5 us
    pallas_call x6, Pallas kernels, call(): pl.pallas_call(kernel, in_specs=in_specs, out_specs=[WHOLE] * len(outs),...  19.4 us
    ppermute x14, waiting for transfers between devices, hop(): return lax.ppermute(x, 'frames', [(i, i ^ step) for i in range(8)])  12.8 us
    unnamed x10, local copies, waits for them, and re-layouts  5.51 us
    ppermute x4, waiting for transfers between devices, body(): swap = lambda x: lax.ppermute(x, 'bins', [(0, 1), (1, 0)])  3.76 us
  transfers between devices with their start and end apart: 18, of which 13 were waited for; matrix products, arithmetic and copies ran while one was open for 0% of the time, Pallas kernels for 2%

profile of v2, /device:TPU:0, one launch (start us, length us, event | category | flops | bytes accessed | tf_op | source)
XLA Modules:
  0.0 68.0 jit_solution(11530378392544488103)
XLA Ops:
  0.6 0.5 collective-permute-start
  1.1 4.7 %collective-permute-start.4 = (f32[32,1024]{1,0:T(8,128)}, f32[32,1024]{1,0:T(8,128)S(1)}, u32[]{:S(2)}, u32[]{:S(2)}) collective-permute-start(f32[32,1024]{1,0:T(8,128)} %old.1), channel_id=1, source_target_pairs={{0,12},{2,14},{4,8},{6,10},{8,4},{10,6},{12,0},{14,2},{1,13},{3,15... | collective-permute-start | bytes 393224 | tf_op jit(solution)/shard_map/ppermute | solution.py:160
  5.8 0.5 collective-permute-start.3
  6.3 2.5 %collective-permute-start.2 = (f32[32,1024]{1,0:T(8,128)}, f32[32,1024]{1,0:T(8,128)S(1)}, u32[]{:S(2)}, u32[]{:S(2)}) collective-permute-start(f32[32,1024]{1,0:T(8,128)} %old.1), channel_id=1, source_target_pairs={{0,4},{2,6},{4,0},{6,2},{8,12},{10,14},{12,8},{14,10},{1,5},{3,7},... | collective-permute-start | bytes 393224 | tf_op jit(solution)/shard_map/ppermute | solution.py:160
  8.8 0.5 collective-permute-start.1
  9.3 1.1 %collective-permute-done.4.refs_0_ = f32[32,1024]{1,0:T(8,128)S(1)} collective-permute-done((f32[32,1024]{1,0:T(8,128)}, f32[32,1024]{1,0:T(8,128)S(1)}, u32[]{:S(2)}, u32[]{:S(2)}) %collective-permute-start.4) | collective-permute-done | bytes 131104 | tf_op jit(solution)/shard_map/ppermute | solution.py:160
  10.4 3.2 %collective-permute-start.7 = (f32[32,1024]{1,0:T(8,128)S(1)}, f32[32,1024]{1,0:T(8,128)S(1)}, u32[]{:S(2)}, u32[]{:S(2)}) collective-permute-start(f32[32,1024]{1,0:T(8,128)S(1)} %collective-permute-done.4.refs_0_), channel_id=1, source_target_pairs={{0,6},{2,4},{4,2},{6,0},{8,14},{10,12},{12,10},{14,8},{1,7},{3,5},... | collective-permute-start | bytes 393224 | tf_op jit(solution)/shard_map/ppermute | solution.py:160
  13.6 0.5 collective-permute-done.3.refs_3_
  14.1 2.1 %collective-permute-start.6 = (f32[32,1024]{1,0:T(8,128)S(1)}, f32[32,1024]{1,0:T(8,128)S(1)}, u32[]{:S(2)}, u32[]{:S(2)}) collective-permute-start(f32[32,1024]{1,0:T(8,128)S(1)} %collective-permute-done.4.refs_0_), channel_id=1, source_target_pairs={{0,4},{2,6},{4,0},{6,2},{8,12},{10,14},{12,8},{14,10},{1,5},{3,7},... | collective-permute-start | bytes 393224 | tf_op jit(solution)/shard_map/ppermute | solution.py:160
  16.2 0.0 collective-permute-done.2.refs_2_
  16.2 1.3 %collective-permute-start.5 = (f32[32,1024]{1,0:T(8,128)S(1)}, f32[32,1024]{1,0:T(8,128)S(1)}, u32[]{:S(2)}, u32[]{:S(2)}) collective-permute-start(f32[32,1024]{1,0:T(8,128)S(1)} %collective-permute-done.4.refs_0_), channel_id=1, source_target_pairs={{0,2},{2,0},{4,6},{6,4},{8,10},{10,8},{12,14},{14,12},{1,3},{3,1},... | collective-permute-start | bytes 393224 | tf_op jit(solution)/shard_map/ppermute | solution.py:160
  17.4 0.1 pad_add_fusion.idx
  17.5 0.0 collective-permute-done.1.refs_1_
  17.5 0.0 copy-start.3
  17.5 0.9 %copy-done.3 = f32[32,1024]{1,0:T(8,128)S(1)} copy-done((f32[32,1024]{1,0:T(8,128)S(1)}, f32[32,1024]{1,0:T(8,128)}, u32[]{:S(2)}) %copy-start.3) | copy-done | bytes 131096
  18.4 0.8 %shard_map.51 = (bf16[256,1024]{1,0:T(8,128)(2,1)S(1)}, bf16[1024,256]{1,0:T(8,128)(2,1)S(1)}, f32[128,128]{1,0:T(8,128)S(1)}) custom-call(s32[2]{0:T(128)S(1)} %pad_add_fusion.idx, f32[32,1024]{1,0:T(8,128)S(1)} %copy-done.3, f32[32,1024]{1,0:T(8,128)S(1)} %collective-permute-done.1.refs_1_, f32[32,1024]{1,0:T(8,128)S(1)} %collective-permute-done.2.refs_2_, ...), custom_call_target="tpu_custom_call" | custom-call | tf_op jit(solution)/shard_map/pallas_call | solution.py:149
  19.3 0.5 collective-permute-done.7.refs_3_
  19.7 1.8 %collective-permute-done.6.refs_2_ = f32[32,1024]{1,0:T(8,128)S(1)} collective-permute-done((f32[32,1024]{1,0:T(8,128)S(1)}, f32[32,1024]{1,0:T(8,128)S(1)}, u32[]{:S(2)}, u32[]{:S(2)}) %collective-permute-start.6) | collective-permute-done | bytes 131104 | tf_op jit(solution)/shard_map/ppermute | solution.py:160
  21.5 0.9 %collective-permute-done.5.refs_1_ = f32[32,1024]{1,0:T(8,128)S(1)} collective-permute-done((f32[32,1024]{1,0:T(8,128)S(1)}, f32[32,1024]{1,0:T(8,128)S(1)}, u32[]{:S(2)}, u32[]{:S(2)}) %collective-permute-start.5) | collective-permute-done | bytes 131104 | tf_op jit(solution)/shard_map/ppermute | solution.py:160
  22.4 0.8 %shard_map.52 = (bf16[256,1024]{1,0:T(8,128)(2,1)S(1)}, bf16[1024,256]{1,0:T(8,128)(2,1)S(1)}, f32[128,128]{1,0:T(8,128)S(1)}) custom-call(s32[2]{0:T(128)S(1)} %pad_add_fusion.idx, f32[32,1024]{1,0:T(8,128)S(1)} %collective-permute-done.4.refs_0_, f32[32,1024]{1,0:T(8,128)S(1)} %collective-permute-done.5.refs_1_, ...), custom_call_target="tpu_custom_call" | custom-call | tf_op jit(solution)/shard_map/pallas_call | solution.py:149
  23.3 0.0 collective-permute-done.hoth
  23.3 0.0 copy-start.2
  23.3 1.2 %copy-done.2 = f32[128,2048]{1,0:T(8,128)S(1)} copy-done((f32[128,2048]{1,0:T(8,128)S(1)}, f32[128,2048]{1,0:T(8,128)}, u32[]{:S(2)}) %copy-start.2) | copy-done | bytes 1048600
  24.5 0.9 %shard_map.50.h2 = bf16[512,2048]{1,0:T(8,128)(2,1)S(1)} custom-call(s32[2]{0:T(128)S(1)} %pad_add_fusion.idx, f32[128,2048]{1,0:T(8,128)S(1)} %copy-done.2, f32[128,2048]{1,0:T(8,128)S(1)} %collective-permute-done.hoth), custom_call_target="tpu_custom_call" | custom-call | tf_op jit(solution)/shard_map/pallas_call | solution.py:149
  25.4 0.0 copy-start
  25.4 3.4 %copy-done = f32[1024,2048]{1,0:T(8,128)S(1)} copy-done((f32[1024,2048]{1,0:T(8,128)S(1)}, f32[1024,2048]{1,0:T(8,128)}, u32[]{:S(2)}) %copy-start) | copy-done | bytes 8388632
  28.8 0.0 copy-start.1
  28.8 6.8 %shard_map.53.nown = f32[256,2048]{1,0:T(8,128)S(1)} custom-call(bf16[512,2048]{1,0:T(8,128)(2,1)S(1)} %shard_map.50.h2, f32[1024,2048]{1,0:T(8,128)S(1)} %copy-done, bf16[256,1024]{1,0:T(8,128)(2,1)S(1)} %get-tuple-element.17.refs_0_, bf16[1024,256]{1,0:T(8,128)(2,1)S(1)} %get-tuple-element.18.refs_1_.refs_0_, ...), custom_call_target="tpu_custom_call" | custom-call | tf_op jit(solution)/shard_map/pallas_call | solution.py:149
  35.5 0.1 collective-permute-start.8
  35.6 0.5 collective-permute-start.9
  36.1 0.0 copy-start.4
  36.1 0.1 collective-permute-start.10
  36.2 3.7 %collective-permute-done.9.refs_4_ = f32[128,128]{1,0:T(8,128)S(1)} collective-permute-done((f32[128,128]{1,0:T(8,128)S(1)}, f32[128,128]{1,0:T(8,128)S(1)}, u32[]{:S(2)}, u32[]{:S(2)}) %collective-permute-start.9) | collective-permute-done | bytes 65568 | tf_op jit(solution)/shard_map/ppermute | solution.py:164
  39.9 0.1 collective-permute-done.10.refs_5_
  40.0 0.0 collective-permute-done.8.noth
  40.0 0.0 copy-done.1
  40.0 9.3 %shard_map.54 = (f32[128,2048]{1,0:T(8,128)}, f32[264,128]{1,0:T(8,128)S(1)}, f32[264,128]{1,0:T(8,128)S(1)}, f32[264,128]{1,0:T(8,128)S(1)}, f32[264,128]{1,0:T...) custom-call(s32[2]{0:T(128)S(1)} %pad_add_fusion.idx, ...), custom_call_target="tpu_custom_call" | custom-call | tf_op jit(solution)/shard_map/pallas_call | solution.py:149
  49.3 1.7 %collective-permute-start.14 = (f32[264,128]{1,0:T(8,128)S(1)}, f32[264,128]{1,0:T(8,128)S(1)}, u32[]{:S(2)}, u32[]{:S(2)}) collective-permute-start(f32[264,128]{1,0:T(8,128)S(1)} %get-tuple-element.29), channel_id=1, source_target_pairs={{0,6},{2,4},{4,2},{6,0},{8,14},{10,12},{12,10},{14,8},{1,7},{3,5},... | collective-permute-start | bytes 405512 | tf_op jit(solution)/shard_map/ppermute | solution.py:160
  51.0 0.4 collective-permute-start.15
  51.4 1.4 %collective-permute-start.16 = (f32[264,128]{1,0:T(8,128)S(1)}, f32[264,128]{1,0:T(8,128)S(1)}, u32[]{:S(2)}, u32[]{:S(2)}) collective-permute-start(f32[264,128]{1,0:T(8,128)S(1)} %get-tuple-element.31), channel_id=1, source_target_pairs={{0,2},{2,0},{4,6},{6,4},{8,10},{10,8},{12,14},{14,12},{1,3},{3,1},... | collective-permute-start | bytes 405512 | tf_op jit(solution)/shard_map/ppermute | solution.py:160
  52.8 1.7 %collective-permute-start.11 = (f32[264,128]{1,0:T(8,128)S(1)}, f32[264,128]{1,0:T(8,128)S(1)}, u32[]{:S(2)}, u32[]{:S(2)}) collective-permute-start(f32[264,128]{1,0:T(8,128)S(1)} %get-tuple-element.25), channel_id=1, source_target_pairs={{0,6},{2,4},{4,2},{6,0},{8,14},{10,12},{12,10},{14,8},{1,7},{3,5},... | collective-permute-start | bytes 405512 | tf_op jit(solution)/shard_map/ppermute | solution.py:160
  54.5 0.4 collective-permute-start.12
  54.8 1.8 %collective-permute-done.14 = f32[264,128]{1,0:T(8,128)S(1)} collective-permute-done((f32[264,128]{1,0:T(8,128)S(1)}, f32[264,128]{1,0:T(8,128)S(1)}, u32[]{:S(2)}, u32[]{:S(2)}) %collective-permute-start.14) | collective-permute-done | bytes 135200 | tf_op jit(solution)/shard_map/ppermute | solution.py:160
  56.6 0.6 collective-permute-start.13
  57.2 1.4 %collective-permute-done.15 = f32[264,128]{1,0:T(8,128)S(1)} collective-permute-done((f32[264,128]{1,0:T(8,128)S(1)}, f32[264,128]{1,0:T(8,128)S(1)}, u32[]{:S(2)}, u32[]{:S(2)}) %collective-permute-start.15) | collective-permute-done | bytes 135200 | tf_op jit(solution)/shard_map/ppermute | solution.py:160
  58.7 1.0 %collective-permute-done.16 = f32[264,128]{1,0:T(8,128)S(1)} collective-permute-done((f32[264,128]{1,0:T(8,128)S(1)}, f32[264,128]{1,0:T(8,128)S(1)}, u32[]{:S(2)}, u32[]{:S(2)}) %collective-permute-start.16) | collective-permute-done | bytes 135200 | tf_op jit(solution)/shard_map/ppermute | solution.py:160
  59.7 3.7 %collective-permute-start.17 = (f32[264,128]{1,0:T(8,128)S(1)}, f32[264,128]{1,0:T(8,128)S(1)}, u32[]{:S(2)}, u32[]{:S(2)}) collective-permute-start(f32[264,128]{1,0:T(8,128)S(1)} %add_add_fusion), channel_id=1, source_target_pairs={{0,12},{2,14},{4,8},{6,10},{8,4},{10,6},{12,0},{14,2},{1,13},{3,15... | collective-permute-start | bytes 405512 | tf_op jit(solution)/shard_map/ppermute | solution.py:160
  63.3 0.0 collective-permute-done.11
  63.3 0.4 collective-permute-done.12
  63.7 0.8 %collective-permute-done.13 = f32[264,128]{1,0:T(8,128)S(1)} collective-permute-done((f32[264,128]{1,0:T(8,128)S(1)}, f32[264,128]{1,0:T(8,128)S(1)}, u32[]{:S(2)}, u32[]{:S(2)}) %collective-permute-start.13) | collective-permute-done | bytes 135200 | tf_op jit(solution)/shard_map/ppermute | solution.py:160
  64.5 2.7 %collective-permute-done.17.more = f32[264,128]{1,0:T(8,128)S(1)} collective-permute-done((f32[264,128]{1,0:T(8,128)S(1)}, f32[264,128]{1,0:T(8,128)S(1)}, u32[]{:S(2)}, u32[]{:S(2)}) %collective-permute-start.17) | collective-permute-done | bytes 135200 | tf_op jit(solution)/shard_map/ppermute | solution.py:160
  67.2 0.0 copy-done.4
  67.2 0.7 %shard_map.55 = f32[32,1024]{1,0:T(8,128)} custom-call(f32[32,1024]{1,0:T(8,128)S(1)} %copy-done.4, f32[264,128]{1,0:T(8,128)S(1)} %add_add_fusion.1.total, f32[264,128]{1,0:T(8,128)S(1)} %collective-permute-done.17.more), custom_call_target="tpu_custom_call" | custom-call | tf_op jit(solution)/shard_map/pallas_call | solution.py:149
  (2 shorter events, 0.1 us)
Async XLA Ops:
  0.6 22.6 %collective-permute-start = (f32[128,2048]{1,0:T(8,128)}, f32[128,2048]{1,0:T(8,128)S(1)}, u32[]{:S(2)}, u32[]{:S(2)}) collective-permute-start(f32[128,2048]{1,0:T(8,128)} %hown.3), channel_id=1, source_target_pairs={{0,1},{1,0},{2,3},{3,2},{4,5},{5,4},{6,7},{7,6},{8,9},{9,8},{10,11... | collective-permute-start | bytes 3145736 | tf_op jit(solution)/shard_map/ppermute | solution.py:164
  1.1 9.3 %collective-permute-start.4 = (f32[32,1024]{1,0:T(8,128)}, f32[32,1024]{1,0:T(8,128)S(1)}, u32[]{:S(2)}, u32[]{:S(2)}) collective-permute-start(f32[32,1024]{1,0:T(8,128)} %old.1), channel_id=1, source_target_pairs={{0,12},{2,14},{4,8},{6,10},{8,4},{10,6},{12,0},{14,2},{1,13},{3,15... | collective-permute-start | bytes 393224 | tf_op jit(solution)/shard_map/ppermute | solution.py:160
  5.8 8.3 %collective-permute-start.3 = (f32[32,1024]{1,0:T(8,128)}, f32[32,1024]{1,0:T(8,128)S(1)}, u32[]{:S(2)}, u32[]{:S(2)}) collective-permute-start(f32[32,1024]{1,0:T(8,128)} %old.1), channel_id=1, source_target_pairs={{0,6},{2,4},{4,2},{6,0},{8,14},{10,12},{12,10},{14,8},{1,7},{3,5},... | collective-permute-start | bytes 393224 | tf_op jit(solution)/shard_map/ppermute | solution.py:160
  6.3 9.9 %collective-permute-start.2 = (f32[32,1024]{1,0:T(8,128)}, f32[32,1024]{1,0:T(8,128)S(1)}, u32[]{:S(2)}, u32[]{:S(2)}) collective-permute-start(f32[32,1024]{1,0:T(8,128)} %old.1), channel_id=1, source_target_pairs={{0,4},{2,6},{4,0},{6,2},{8,12},{10,14},{12,8},{14,10},{1,5},{3,7},... | collective-permute-start | bytes 393224 | tf_op jit(solution)/shard_map/ppermute | solution.py:160
  8.8 8.7 %collective-permute-start.1 = (f32[32,1024]{1,0:T(8,128)}, f32[32,1024]{1,0:T(8,128)S(1)}, u32[]{:S(2)}, u32[]{:S(2)}) collective-permute-start(f32[32,1024]{1,0:T(8,128)} %old.1), channel_id=1, source_target_pairs={{0,2},{2,0},{4,6},{6,4},{8,10},{10,8},{12,14},{14,12},{1,3},{3,1},... | collective-permute-start | bytes 393224 | tf_op jit(solution)/shard_map/ppermute | solution.py:160
  10.4 9.3 %collective-permute-start.7 = (f32[32,1024]{1,0:T(8,128)S(1)}, f32[32,1024]{1,0:T(8,128)S(1)}, u32[]{:S(2)}, u32[]{:S(2)}) collective-permute-start(f32[32,1024]{1,0:T(8,128)S(1)} %collective-permute-done.4.refs_0_), channel_id=1, source_target_pairs={{0,6},{2,4},{4,2},{6,0},{8,14},{10,12},{12,10},{14,8},{1,7},{3,5},... | collective-permute-start | bytes 393224 | tf_op jit(solution)/shard_map/ppermute | solution.py:160
  14.1 7.4 %collective-permute-start.6 = (f32[32,1024]{1,0:T(8,128)S(1)}, f32[32,1024]{1,0:T(8,128)S(1)}, u32[]{:S(2)}, u32[]{:S(2)}) collective-permute-start(f32[32,1024]{1,0:T(8,128)S(1)} %collective-permute-done.4.refs_0_), channel_id=1, source_target_pairs={{0,4},{2,6},{4,0},{6,2},{8,12},{10,14},{12,8},{14,10},{1,5},{3,7},... | collective-permute-start | bytes 393224 | tf_op jit(solution)/shard_map/ppermute | solution.py:160
  16.2 6.2 %collective-permute-start.5 = (f32[32,1024]{1,0:T(8,128)S(1)}, f32[32,1024]{1,0:T(8,128)S(1)}, u32[]{:S(2)}, u32[]{:S(2)}) collective-permute-start(f32[32,1024]{1,0:T(8,128)S(1)} %collective-permute-done.4.refs_0_), channel_id=1, source_target_pairs={{0,2},{2,0},{4,6},{6,4},{8,10},{10,8},{12,14},{14,12},{1,3},{3,1},... | collective-permute-start | bytes 393224 | tf_op jit(solution)/shard_map/ppermute | solution.py:160
  17.5 0.9 %copy-start.3 = (f32[32,1024]{1,0:T(8,128)S(1)}, f32[32,1024]{1,0:T(8,128)}, u32[]{:S(2)}) copy-start(f32[32,1024]{1,0:T(8,128)} %old.1) | copy-start | bytes 393220
  23.3 1.2 %copy-start.2 = (f32[128,2048]{1,0:T(8,128)S(1)}, f32[128,2048]{1,0:T(8,128)}, u32[]{:S(2)}) copy-start(f32[128,2048]{1,0:T(8,128)} %hown.3) | copy-start | bytes 3145732
  25.4 3.4 %copy-start = (f32[1024,2048]{1,0:T(8,128)S(1)}, f32[1024,2048]{1,0:T(8,128)}, u32[]{:S(2)}) copy-start(f32[1024,2048]{1,0:T(8,128)} %v.3) | copy-start | bytes 25165828
  28.8 11.2 %copy-start.1 = (f32[1024,2048]{1,0:T(8,128)S(1)}, f32[1024,2048]{1,0:T(8,128)}, u32[]{:S(2)}) copy-start(f32[1024,2048]{1,0:T(8,128)} %v.3) | copy-start | bytes 25165828
  35.5 4.4 %collective-permute-start.8 = (f32[256,2048]{1,0:T(8,128)S(1)}, f32[256,2048]{1,0:T(8,128)S(1)}, u32[]{:S(2)}, u32[]{:S(2)}) collective-permute-start(f32[256,2048]{1,0:T(8,128)S(1)} %shard_map.53.nown), channel_id=1, source_target_pairs={{0,1},{1,0},{2,3},{3,2},{4,5},{5,4},{6,7},{7,6},{8,9},{9,8},{10,11... | collective-permute-start | bytes 6291464 | tf_op jit(solution)/shard_map/ppermute | solution.py:164
  35.6 4.2 %collective-permute-start.9 = (f32[128,128]{1,0:T(8,128)S(1)}, f32[128,128]{1,0:T(8,128)S(1)}, u32[]{:S(2)}, u32[]{:S(2)}) collective-permute-start(f32[128,128]{1,0:T(8,128)S(1)} %get-tuple-element.21.refs_2_), channel_id=1, source_target_pairs={{0,1},{1,0},{2,3},{3,2},{4,5},{5,4},{6,7},{7,6},{8,9},{9,8},{10,11... | collective-permute-start | bytes 196616 | tf_op jit(solution)/shard_map/ppermute | solution.py:164
  36.1 31.1 %copy-start.4 = (f32[32,1024]{1,0:T(8,128)S(1)}, f32[32,1024]{1,0:T(8,128)}, u32[]{:S(2)}) copy-start(f32[32,1024]{1,0:T(8,128)} %old.1) | copy-start | bytes 393220
  36.1 3.8 %collective-permute-start.10 = (f32[128,128]{1,0:T(8,128)S(1)}, f32[128,128]{1,0:T(8,128)S(1)}, u32[]{:S(2)}, u32[]{:S(2)}) collective-permute-start(f32[128,128]{1,0:T(8,128)S(1)} %get-tuple-element.22.refs_3_), channel_id=1, source_target_pairs={{0,1},{1,0},{2,3},{3,2},{4,5},{5,4},{6,7},{7,6},{8,9},{9,8},{10,11... | collective-permute-start | bytes 196616 | tf_op jit(solution)/shard_map/ppermute | solution.py:164
  49.3 7.3 %collective-permute-start.14 = (f32[264,128]{1,0:T(8,128)S(1)}, f32[264,128]{1,0:T(8,128)S(1)}, u32[]{:S(2)}, u32[]{:S(2)}) collective-permute-start(f32[264,128]{1,0:T(8,128)S(1)} %get-tuple-element.29), channel_id=1, source_target_pairs={{0,6},{2,4},{4,2},{6,0},{8,14},{10,12},{12,10},{14,8},{1,7},{3,5},... | collective-permute-start | bytes 405512 | tf_op jit(solution)/shard_map/ppermute | solution.py:160
  51.0 7.7 %collective-permute-start.15 = (f32[264,128]{1,0:T(8,128)S(1)}, f32[264,128]{1,0:T(8,128)S(1)}, u32[]{:S(2)}, u32[]{:S(2)}) collective-permute-start(f32[264,128]{1,0:T(8,128)S(1)} %get-tuple-element.30), channel_id=1, source_target_pairs={{0,4},{2,6},{4,0},{6,2},{8,12},{10,14},{12,8},{14,10},{1,5},{3,7},... | collective-permute-start | bytes 405512 | tf_op jit(solution)/shard_map/ppermute | solution.py:160
  51.4 8.3 %collective-permute-start.16 = (f32[264,128]{1,0:T(8,128)S(1)}, f32[264,128]{1,0:T(8,128)S(1)}, u32[]{:S(2)}, u32[]{:S(2)}) collective-permute-start(f32[264,128]{1,0:T(8,128)S(1)} %get-tuple-element.31), channel_id=1, source_target_pairs={{0,2},{2,0},{4,6},{6,4},{8,10},{10,8},{12,14},{14,12},{1,3},{3,1},... | collective-permute-start | bytes 405512 | tf_op jit(solution)/shard_map/ppermute | solution.py:160
  52.8 10.6 %collective-permute-start.11 = (f32[264,128]{1,0:T(8,128)S(1)}, f32[264,128]{1,0:T(8,128)S(1)}, u32[]{:S(2)}, u32[]{:S(2)}) collective-permute-start(f32[264,128]{1,0:T(8,128)S(1)} %get-tuple-element.25), channel_id=1, source_target_pairs={{0,6},{2,4},{4,2},{6,0},{8,14},{10,12},{12,10},{14,8},{1,7},{3,5},... | collective-permute-start | bytes 405512 | tf_op jit(solution)/shard_map/ppermute | solution.py:160
  54.5 9.2 %collective-permute-start.12 = (f32[264,128]{1,0:T(8,128)S(1)}, f32[264,128]{1,0:T(8,128)S(1)}, u32[]{:S(2)}, u32[]{:S(2)}) collective-permute-start(f32[264,128]{1,0:T(8,128)S(1)} %get-tuple-element.26), channel_id=1, source_target_pairs={{0,4},{2,6},{4,0},{6,2},{8,12},{10,14},{12,8},{14,10},{1,5},{3,7},... | collective-permute-start | bytes 405512 | tf_op jit(solution)/shard_map/ppermute | solution.py:160
  56.6 7.9 %collective-permute-start.13 = (f32[264,128]{1,0:T(8,128)S(1)}, f32[264,128]{1,0:T(8,128)S(1)}, u32[]{:S(2)}, u32[]{:S(2)}) collective-permute-start(f32[264,128]{1,0:T(8,128)S(1)} %get-tuple-element.27), channel_id=1, source_target_pairs={{0,2},{2,0},{4,6},{6,4},{8,10},{10,8},{12,14},{14,12},{1,3},{3,1},... | collective-permute-start | bytes 405512 | tf_op jit(solution)/shard_map/ppermute | solution.py:160
  59.7 7.6 %collective-permute-start.17 = (f32[264,128]{1,0:T(8,128)S(1)}, f32[264,128]{1,0:T(8,128)S(1)}, u32[]{:S(2)}, u32[]{:S(2)}) collective-permute-start(f32[264,128]{1,0:T(8,128)S(1)} %add_add_fusion), channel_id=1, source_target_pairs={{0,12},{2,14},{4,8},{6,10},{8,4},{10,6},{12,0},{14,2},{1,13},{3,15... | collective-permute-start | bytes 405512 | tf_op jit(solution)/shard_map/ppermute | solution.py:160

commit v3 on v0

v3 whole, which is shorter than its diff:
```python
import functools

import jax
import jax.numpy as jnp
from jax import lax
from jax.experimental import pallas as pl
from jax.experimental.pallas import tpu as pltpu
from jax.sharding import PartitionSpec as P

f32, bf16 = jnp.float32, jnp.bfloat16
WHOLE = pl.BlockSpec(memory_space=pltpu.VMEM)
SCALARS = pl.BlockSpec(memory_space=pltpu.SMEM)
HBM = pl.BlockSpec(memory_space=pl.ANY)
GATHER_CROSS, REDUCE_CROSS = 6, 6
PIECES = 2
FC, NC = 256, 512


def split(x):
    hi = x.astype(bf16)
    return hi, (x - hi.astype(f32)).astype(bf16)


def dot(a, b):
    return jnp.dot(a, b, preferred_element_type=f32)


def dot_nt(a, b):
    return lax.dot_general(a, b, (((1,), (1,)), ((), ())), preferred_element_type=f32)


def rows_at(start, rows):
    return pl.ds(pl.multiple_of(start * rows, rows), rows)


def pack(columns, rows):
    lane = lax.broadcasted_iota(jnp.int32, (8, 128), 1) // (1024 // rows)
    tile = jnp.zeros((8, 128), f32)
    for i in range(rows // 8):
        tile = jnp.where(lane == i, columns(8 * i), tile)
    return tile


def unpack(tile, i, rows):
    lane = i * (1024 // rows)
    return jnp.broadcast_to(tile[:, lane : lane + 1], (8, 128))


def prepare(idx, ws, w2, wt, mass, first):
    rows = ws[0].shape[0]
    half = len(ws) * rows
    for s, w in enumerate(ws):
        x = w[...]
        hi, lo = split(x)
        place = (idx[0] ^ (s ^ first)) if len(ws) > 1 else 0
        w2[rows_at(place, rows), :] = hi
        w2[rows_at(place + half // rows, rows), :] = lo
        mass[rows_at(place, rows), :] = jnp.broadcast_to(jnp.sum(x, axis=1, keepdims=True), (rows, 128))
    wt[...] = w2[...].T


def prepare_kernel(idx, *refs):
    *ws, w2, wt, mass = refs
    prepare(idx, ws, w2, wt, mass, 0)


def order_kernel(idx, hown, hoth, h, h2):
    half = hown.shape[0]
    for place, old in ((idx[1], hown), (1 - idx[1], hoth)):
        x = old[...]
        hi, lo = split(x)
        h[rows_at(place, half), :] = x
        h2[rows_at(place, half), :] = hi
        h2[rows_at(place + 2, half), :] = lo


def by_three(parts, rows):
    half = parts[0].shape[1] // 2
    hi = [w[rows, :half] for w in parts]
    lo = [w[rows, half:] for w in parts]
    return jnp.concatenate(hi + lo + hi, axis=1)


def first_kernel(idx, v, h2, *refs, start, n_parts, masses, raw):
    refs = list(refs)
    take = lambda n: [refs.pop(0) for _ in range(n)]
    w2, wt = take(n_parts), take(n_parts)
    mass, ws, (numer,) = take(masses), take(raw), take(1)
    if raw:
        made = take(3)
        prepare(idx, ws, *made, GATHER_CROSS & 3)
        w2.append(made[0])
        wt.append(made[1])
        mass.append(made[2])
    rhi, rlo = refs
    bins, frames = rhi.shape
    atoms = h2.shape[0] // 2
    whi = jnp.concatenate([w[: w.shape[0] // 2, :] for w in w2], axis=0)
    wlo = jnp.concatenate([w[w.shape[0] // 2 :, :] for w in w2], axis=0)
    for n in range(0, frames, NC):
        at, src = slice(n, n + NC), slice(start + n, start + n + NC)
        h3 = jnp.concatenate([h2[:atoms, src], h2[:atoms, src], h2[atoms:, src]], axis=0)
        for f in range(0, bins, FC):
            m = dot(by_three(wt, slice(f, f + FC)), h3)
            hi, lo = split(v[f : f + FC, src] / m)
            rhi[f : f + FC, at] = hi
            rlo[f : f + FC, at] = lo
        numer[:atoms, at] = dot(whi, rhi[:, at]) + dot(wlo, rhi[:, at]) + dot(whi, rlo[:, at])
    if mass:
        part = mass[0].shape[0]
        numer[atoms:, :] = jnp.zeros((8, frames), f32)
        numer[atoms:, :128] = pack(lambda i: mass[i // part][i % part : i % part + 8, :], atoms)


def second_kernel(idx, v, h, mine, theirs, nown, noth, *refs, start, n_parts, before, n_out):
    refs = list(refs)
    take = lambda n: [refs.pop(0) for _ in range(n)]
    wt = take(n_parts)
    if before:
        acc_in, row_in, _ = take(3)
    (newact,) = take(1)
    outs = take(max(n_out, 2) if n_out != 1 else 1)
    fresh_own, f2, rhi, rlo, acc, scale, o_sems = refs
    bins, frames = rhi.shape
    atoms = h.shape[0]
    half = atoms // 2
    tile = 1.0 / (mine[atoms:, :128] + theirs[atoms:, :128])
    for i in range(atoms // 8):
        scale[8 * i : 8 * i + 8, :] = unpack(tile, i, atoms)
    sums = row_in[:, :1] if before else None
    written = []
    for n in range(0, frames, NC):
        at, src = slice(n, n + NC), slice(start + n, start + n + NC)
        fresh = h[:, src] * (nown[:atoms, at] + noth[:atoms, at]) * scale[:, :1]
        fresh_own[:, at] = fresh
        hhi, hlo = split(fresh)
        f2[:atoms, at] = hhi
        f2[atoms:, at] = hlo
        row = jnp.sum(fresh, axis=1, keepdims=True)
        sums = row if sums is None else sums + row
        written.append(
            pltpu.make_async_copy(
                fresh_own.at[rows_at(idx[1], half), pl.ds(n, NC)],
                newact.at[:, pl.ds(start + n, NC)],
                o_sems.at[n // NC],
            )
        )
        written[-1].start()
    for n in range(0, frames, NC):
        at, src = slice(n, n + NC), slice(start + n, start + n + NC)
        h3 = jnp.concatenate([f2[:atoms, at], f2[:atoms, at], f2[atoms:, at]], axis=0)
        for f in range(0, bins, FC):
            m = dot(by_three(wt, slice(f, f + FC)), h3)
            hi, lo = split(v[f : f + FC, src] / m)
            rhi[f : f + FC, at] = hi
            rlo[f : f + FC, at] = lo
    total = dot_nt(f2[:atoms, :], rhi[...]) + dot_nt(f2[atoms:, :], rhi[...]) + dot_nt(f2[:atoms, :], rlo[...])
    if before:
        total = total + acc_in[...]
    row_mass = jnp.broadcast_to(sums, (atoms, 128))
    if n_out == 0:
        outs[0][...] = total
        outs[1][...] = row_mass
    elif n_out == 1:
        outs[0][:, :bins] = total
        outs[0][:, bins:] = row_mass
    else:
        acc[...] = total
        scale[...] = row_mass
        rows = atoms // n_out
        for s, o in enumerate(outs):
            place = (idx[0] ^ (s & 3)) + (s & 4)
            base = pl.multiple_of(place * rows, rows)
            for i in range(rows // 8):
                for j in range(bins // 128):
                    k = 8 * (i * (bins // 128) + j)
                    o[k : k + 8, :] = acc[pl.ds(base + 8 * i, 8), 128 * j : 128 * (j + 1)]
            o[rows * bins // 128 :, :] = pack(lambda i: scale[pl.ds(base + i, 8), :], rows)
    for copy in written:
        copy.wait()


def last_kernel(old, total, more, new):
    rows, bins = old.shape
    x = 1.0 / (total[rows * bins // 128 :, :] + more[rows * bins // 128 :, :])
    for i in range(rows // 8):
        scale = unpack(x, i, rows)
        for j in range(bins // 128):
            k = 8 * (i * (bins // 128) + j)
            at = (slice(8 * i, 8 * i + 8), slice(128 * j, 128 * (j + 1)))
            new[at] = old[at] * (total[k : k + 8, :] + more[k : k + 8, :]) * scale


def call(kernel, ins, outs, scratch=(), in_specs=(), out_specs=(), aliases=None, mib=28, flops=0):
    return pl.pallas_call(
        kernel,
        in_specs=list(in_specs) + [WHOLE] * (len(ins) - len(in_specs)),
        out_specs=list(out_specs) + [WHOLE] * (len(outs) - len(out_specs)),
        out_shape=[jax.ShapeDtypeStruct(*o) for o in outs],
        scratch_shapes=[pltpu.VMEM(*s) if isinstance(s, tuple) else s for s in scratch],
        input_output_aliases=aliases or {},
        compiler_params=pltpu.CompilerParams(vmem_limit_bytes=mib * 2**20),
        cost_estimate=pl.CostEstimate(flops=flops, bytes_accessed=0, transcendentals=0) if flops else None,
    )(*ins)


def hop(x, step):
    return lax.ppermute(x, "frames", [(i, i ^ step) for i in range(8)])


def body(spectrum, atoms_by_bin, activations, *, n_dev):
    swap = lambda x: lax.ppermute(x, "bins", [(0, 1), (1, 0)])
    bins, frames = spectrum.shape
    half = activations.shape[0]
    atoms = 2 * half
    rows = atoms_by_bin.shape[0]
    cube = n_dev == 8 and rows % 16 == 0
    place, core = lax.axis_index("frames"), lax.axis_index("bins")
    idx = jnp.stack([place & 3, core ^ (place >> 2)] if cube else [place, core]).astype(jnp.int32)
    size = frames // PIECES

    def basis_outs(k):
        return [((2 * k, bins), bf16), ((bins, 2 * k), bf16), ((k, 128), f32)]

    other = swap(activations)
    raw = []
    if cube:
        far = hop(atoms_by_bin, GATHER_CROSS)
        near = [hop(atoms_by_bin, s) for s in (1, 2, 3)]
        raw = [far] + [hop(far, s) for s in (1, 2, 3)]
        near = [atoms_by_bin, *near]
    else:
        near = [lax.all_gather(atoms_by_bin, "frames", axis=0, tiled=True)]
    h, h2 = call(
        order_kernel,
        [idx, activations, other],
        [((atoms, frames), f32), ((2 * atoms, frames), bf16)],
        in_specs=[SCALARS],
        mib=16,
        flops=10**9,
    )
    k = sum(w.shape[0] for w in near)
    w2, wt, mass = call(prepare_kernel, [idx, *near], basis_outs(k), in_specs=[SCALARS], mib=16, flops=10**10)
    w2, wt, mass = [w2], [wt], [mass]
    numers = []
    for p in range(PIECES):
        numer, *made = call(
            functools.partial(first_kernel, start=p * size, n_parts=len(wt), masses=len(mass), raw=len(raw)),
            [idx, spectrum, h2, *w2, *wt, *mass, *raw],
            [((atoms + 8 * (p == 0), size), f32)] + (basis_outs(atoms - k) if raw else []),
            scratch=[((bins, size), bf16), ((bins, size), bf16)],
            in_specs=[SCALARS],
        )
        if raw:
            w2.append(made[0])
            wt.append(made[1])
        raw, mass = [], []
        numers.append((numer, swap(numer)))
    n_out = n_dev if cube else 1
    block = (rows * bins // 128 + 8, 128) if cube else (atoms, bins + 128)
    carried = []
    for p in range(PIECES):
        final = p == PIECES - 1
        ins = [idx, spectrum, h, *numers[0], *numers[p], *wt]
        fresh, *carried = call(
            functools.partial(
                second_kernel, start=p * size, n_parts=len(wt), before=p > 0, n_out=n_out if final else 0
            ),
            ins + carried + ([fresh] if p else []),
            [((half, frames), f32)]
            + ([(block, f32)] * n_out if final else [((atoms, bins), f32), ((atoms, 128), f32)]),
            scratch=[
                ((atoms, size), f32),
                ((2 * atoms, size), bf16),
                ((bins, size), bf16),
                ((bins, size), bf16),
                ((atoms, bins), f32),
                ((atoms, 128), f32),
                pltpu.SemaphoreType.DMA((size // NC,)),
            ],
            in_specs=[SCALARS] + ([WHOLE] * (len(ins) + 1) + [HBM] if p else []),
            out_specs=[HBM],
            aliases={len(ins) + 2: 0} if p else None,
        )
    parts = carried
    if cube:
        total = parts[REDUCE_CROSS]
        for s in (3, 2, 1):
            total = total + hop(parts[s ^ REDUCE_CROSS], s)
        more = hop(total, REDUCE_CROSS)
        total = parts[0]
        for s in (3, 2, 1):
            total = total + hop(parts[s], s)
        (new,) = call(last_kernel, [atoms_by_bin, total, more], [((rows, bins), f32)], mib=16)
        return fresh, new
    total = lax.psum_scatter(parts[0], "frames", scatter_dimension=0, tiled=True)
    return fresh, atoms_by_bin * total[:, :bins] / total[:, bins : bins + 1]


def solution(mesh):
    return jax.shard_map(
        functools.partial(body, n_dev=mesh.shape["frames"]),
        mesh=mesh,
        in_specs=(P("bins", ("groups", "frames")), P("frames", ("groups", "bins")), P("bins", ("groups", "frames"))),
        out_specs=(P("bins", ("groups", "frames")), P("frames", ("groups", "bins"))),
        check_vma=False,
    )
```

time: 229 us -> 59.7 us (0.26)
  waiting for transfers between devices: 132 us -> 13.1 us
  matrix products: 52.6 us -> 0 us
  blocking collectives: 24.4 us -> 0 us
  starting transfers between devices: 0.42 us -> 23.8 us
  Pallas kernels: 0 us -> 20.4 us
  between operations: 13.9 us -> 0.72 us
  other arithmetic: 4.36 us -> 0.16 us
    all_gather x3 -> x0, waiting for transfers between devices: 66.6 us -> none  [the longest x1 44.3 us: body(): basis = lax.all_gather(atoms_by_bin, 'frames', axis=0, tiled=True)]
    psum x1 -> x0, waiting for transfers between devices: 55.8 us -> none  [body(): basis_total, row_total = lax.psum((basis_part, row_part), 'frames')]
    dot_general x4 -> x0, matrix products: 52.6 us -> none  [the longest x1 17.3 us: body(): lax.dot_general(fresh_full, ratio_next, (((1,), (1,)), ((), ())), precisi...]
    psum x2 -> x0, blocking collectives: 24.4 us -> none  [the longest x1 21.9 us: body(): basis_total, row_total = lax.psum((basis_part, row_part), 'frames')]
    ppermute x0 -> x17, starting transfers between devices: none -> 23.8 us  [the longest x14 23.2 us: hop(): return lax.ppermute(x, 'frames', [(i, i ^ step) for i in range(8)])]
    pallas_call x0 -> x7, Pallas kernels: none -> 20.4 us  [call(): pl.pallas_call(kernel, in_specs=list(in_specs) + [WHOLE] * (len(ins) - le...]
    ppermute x0 -> x17, waiting for transfers between devices: none -> 13.1 us  [the longest x14 13.1 us: hop(): return lax.ppermute(x, 'frames', [(i, i ^ step) for i in range(8)])]
    reduce_scatter x1 -> x0, waiting for transfers between devices: 7.84 us -> none  [body(): lax.psum_scatter(numer_part, 'bins', scatter_dimension=0, tiled=True)]
  transfers between devices with their start and end apart: 5 -> 17, of which waited for: 5 -> 11; matrix products, arithmetic and copies ran while one was open for 1% -> 0% of each run, Pallas kernels for 0% -> 17%
where the time goes in v3:
time: 59.7 us; the launch traced here: 59.6 us
  starting transfers between devices  23.8 us (40%)
  Pallas kernels  20.4 us (34%)
  waiting for transfers between devices  13.1 us (22%)
  local copies, waits for them, and re-layouts  1.3 us (2%)
  between operations  0.72 us (1%)
    ppermute x14, starting transfers between devices, hop(): return lax.ppermute(x, 'frames', [(i, i ^ step) for i in range(8)])  23.2 us
    pallas_call x7, Pallas kernels, call(): pl.pallas_call(kernel, in_specs=list(in_specs) + [WHOLE] * (len(ins) - le...  20.4 us
    ppermute x14, waiting for transfers between devices, hop(): return lax.ppermute(x, 'frames', [(i, i ^ step) for i in range(8)])  13.1 us
    unnamed x10, local copies, waits for them, and re-layouts  1.3 us
  transfers between devices with their start and end apart: 17, of which 11 were waited for; matrix products, arithmetic and copies ran while one was open for 0% of the time, Pallas kernels for 17%

profile of v3, /device:TPU:0, one launch (start us, length us, event | category | flops | bytes accessed | tf_op | source)
XLA Modules:
  0.0 59.6 jit_solution(14370645155419845109)
XLA Ops:
  0.6 5.1 %collective-permute-start.4 = (f32[32,1024]{1,0:T(8,128)}, f32[32,1024]{1,0:T(8,128)S(1)}, u32[]{:S(2)}, u32[]{:S(2)}) collective-permute-start(f32[32,1024]{1,0:T(8,128)} %old.1), channel_id=1, source_target_pairs={{0,12},{2,14},{4,8},{6,10},{8,4},{10,6},{12,0},{14,2},{1,13},{3,15... | collective-permute-start | bytes 393224 | tf_op jit(solution)/shard_map/ppermute | solution.py:208
  5.7 0.5 collective-permute-start.3
  6.2 2.5 %collective-permute-start.2 = (f32[32,1024]{1,0:T(8,128)}, f32[32,1024]{1,0:T(8,128)S(1)}, u32[]{:S(2)}, u32[]{:S(2)}) collective-permute-start(f32[32,1024]{1,0:T(8,128)} %old.1), channel_id=1, source_target_pairs={{0,4},{2,6},{4,0},{6,2},{8,12},{10,14},{12,8},{14,10},{1,5},{3,7},... | collective-permute-start | bytes 393224 | tf_op jit(solution)/shard_map/ppermute | solution.py:208
  8.7 0.5 collective-permute-start.1
  9.2 0.0 collective-permute-start
  9.2 0.0 slice-start
  9.2 0.1 pad_add_fusion.idx
  9.3 0.0 slice-start.1
  9.3 1.0 %collective-permute-done.4.refs_3_ = f32[32,1024]{1,0:T(8,128)S(1)} collective-permute-done((f32[32,1024]{1,0:T(8,128)}, f32[32,1024]{1,0:T(8,128)S(1)}, u32[]{:S(2)}, u32[]{:S(2)}) %collective-permute-start.4) | collective-permute-done | bytes 131104 | tf_op jit(solution)/shard_map/ppermute | solution.py:208
  10.3 2.6 %collective-permute-start.7 = (f32[32,1024]{1,0:T(8,128)S(1)}, f32[32,1024]{1,0:T(8,128)S(1)}, u32[]{:S(2)}, u32[]{:S(2)}) collective-permute-start(f32[32,1024]{1,0:T(8,128)S(1)} %collective-permute-done.4.refs_3_), channel_id=1, source_target_pairs={{0,6},{2,4},{4,2},{6,0},{8,14},{10,12},{12,10},{14,8},{1,7},{3,5},... | collective-permute-start | bytes 393224 | tf_op jit(solution)/shard_map/ppermute | solution.py:208
  12.9 0.9 %collective-permute-done.3.refs_3_ = f32[32,1024]{1,0:T(8,128)S(1)} collective-permute-done((f32[32,1024]{1,0:T(8,128)}, f32[32,1024]{1,0:T(8,128)S(1)}, u32[]{:S(2)}, u32[]{:S(2)}) %collective-permute-start.3) | collective-permute-done | bytes 131104 | tf_op jit(solution)/shard_map/ppermute | solution.py:208
  13.8 2.2 %collective-permute-start.6 = (f32[32,1024]{1,0:T(8,128)S(1)}, f32[32,1024]{1,0:T(8,128)S(1)}, u32[]{:S(2)}, u32[]{:S(2)}) collective-permute-start(f32[32,1024]{1,0:T(8,128)S(1)} %collective-permute-done.4.refs_3_), channel_id=1, source_target_pairs={{0,4},{2,6},{4,0},{6,2},{8,12},{10,14},{12,8},{14,10},{1,5},{3,7},... | collective-permute-start | bytes 393224 | tf_op jit(solution)/shard_map/ppermute | solution.py:208
  16.1 0.1 collective-permute-done.2.refs_2_
  16.2 1.1 %collective-permute-start.5 = (f32[32,1024]{1,0:T(8,128)S(1)}, f32[32,1024]{1,0:T(8,128)S(1)}, u32[]{:S(2)}, u32[]{:S(2)}) collective-permute-start(f32[32,1024]{1,0:T(8,128)S(1)} %collective-permute-done.4.refs_3_), channel_id=1, source_target_pairs={{0,2},{2,0},{4,6},{6,4},{8,10},{10,8},{12,14},{14,12},{1,3},{3,1},... | collective-permute-start | bytes 393224 | tf_op jit(solution)/shard_map/ppermute | solution.py:208
  17.2 0.0 collective-permute-done.1.refs_1_
  17.2 0.0 copy-start
  17.2 0.9 %copy-done = f32[32,1024]{1,0:T(8,128)S(1)} copy-done((f32[32,1024]{1,0:T(8,128)S(1)}, f32[32,1024]{1,0:T(8,128)}, u32[]{:S(2)}) %copy-start) | copy-done | bytes 131096
  18.1 0.0 copy-start.2
  18.1 0.8 %shard_map.51 = (bf16[256,1024]{1,0:T(8,128)(2,1)S(1)}, bf16[1024,256]{1,0:T(8,128)(2,1)S(1)}, f32[128,128]{1,0:T(8,128)S(1)}) custom-call(s32[2]{0:T(128)S(1)} %pad_add_fusion.idx, f32[32,1024]{1,0:T(8,128)S(1)} %copy-done, f32[32,1024]{1,0:T(8,128)S(1)} %collective-permute-done.1.refs_1_, f32[32,1024]{1,0:T(8,128)S(1)} %collective-permute-done.2.refs_2_, ...), custom_call_target="tpu_custom_call" | custom-call | flops 10000000000 | tf_op jit(solution)/shard_map/pallas_call | solution.py:195
  19.0 0.0 collective-permute-done.hoth
  19.0 0.4 copy-done.2
  19.3 1.0 %shard_map.50 = (f32[256,2048]{1,0:T(8,128)S(1)}, bf16[512,2048]{1,0:T(8,128)(2,1)S(1)}) custom-call(s32[2]{0:T(128)S(1)} %pad_add_fusion.idx, f32[128,2048]{1,0:T(8,128)S(1)} %copy-done.2, f32[128,2048]{1,0:T(8,128)S(1)} %collective-permute-done.hoth), custom_call_target="tpu_custom_call" | custom-call | flops 1000000000 | tf_op jit(solution)/shard_map/pallas_call | solution.py:195
  20.4 0.0 collective-permute-done.7.refs_6_
  20.4 0.6 %collective-permute-done.6.refs_5_ = f32[32,1024]{1,0:T(8,128)S(1)} collective-permute-done((f32[32,1024]{1,0:T(8,128)S(1)}, f32[32,1024]{1,0:T(8,128)S(1)}, u32[]{:S(2)}, u32[]{:S(2)}) %collective-permute-start.6) | collective-permute-done | bytes 131104 | tf_op jit(solution)/shard_map/ppermute | solution.py:208
  21.0 0.8 %collective-permute-done.5.refs_4_ = f32[32,1024]{1,0:T(8,128)S(1)} collective-permute-done((f32[32,1024]{1,0:T(8,128)S(1)}, f32[32,1024]{1,0:T(8,128)S(1)}, u32[]{:S(2)}, u32[]{:S(2)}) %collective-permute-start.5) | collective-permute-done | bytes 131104 | tf_op jit(solution)/shard_map/ppermute | solution.py:208
  21.8 0.0 slice-done
  21.8 0.0 slice-done.1
  21.8 4.8 %shard_map.52 = (f32[264,1024]{1,0:T(8,128)S(1)}, bf16[256,1024]{1,0:T(8,128)(2,1)S(1)}, bf16[1024,256]{1,0:T(8,128)(2,1)S(1)}, f32[128,128]{1,0:T(8,128)}) custom-call(s32[2]{0:T(128)S(1)} %pad_add_fusion.idx, f32[1024,2048]{1,0:T(8,128)S(1)} %bitcast.3, bf16[512,2048]{1,0:T(8,128)(2,1)S(1)} %get-tuple-element.23.h2, ...), custom_call_target="tpu_custom_call" | custom-call | tf_op jit(solution)/shard_map/pallas_call | solution.py:195
  26.6 0.0 collective-permute-start.8
  26.6 4.1 %shard_map.53.nown = f32[256,1024]{1,0:T(8,128)S(1)} custom-call(s32[2]{0:T(128)S(1)} %pad_add_fusion.idx, f32[1024,2048]{1,0:T(8,128)S(1)} %bitcast.3, bf16[512,2048]{1,0:T(8,128)(2,1)S(1)} %get-tuple-element.23.h2, bf16[256,1024]{1,0:T(8,128)(2,1)S(1)} %get-tuple-element.24.refs_0_, bf16[256,1024]{1,0:T(8,128)(2,1)S(1)} %get-tuple-element.28.refs_1_, ...), custom_call_target="tpu_custom_call" | custom-call | tf_op jit(solution)/shard_map/pallas_call | solution.py:195
  30.7 0.6 collective-permute-start.9
  31.3 0.0 collective-permute-done.8.theirs.noth
  31.3 4.4 %shard_map.54 = (f32[128,2048]{1,0:T(8,128)}, f32[256,1024]{1,0:T(8,128)S(1)}, f32[256,128]{1,0:T(8,128)S(1)}) custom-call(s32[2]{0:T(128)S(1)} %pad_add_fusion.idx, f32[1024,2048]{1,0:T(8,128)S(1)} %bitcast.3, f32[256,2048]{1,0:T(8,128)S(1)} %get-tuple-element.22.h, f32[264,1024]{1,0:T(8,128)S(1)} %get-tuple-element.27.mine.nown, ...), custom_call_target="tpu_custom_call" | custom-call | tf_op jit(solution)/shard_map/pallas_call | solution.py:195
  35.7 0.0 collective-permute-done.9.noth
  35.7 0.0 copy-start.1
  35.7 4.5 %shard_map.55 = (f32[128,2048]{1,0:T(8,128)}, f32[264,128]{1,0:T(8,128)S(1)}, f32[264,128]{1,0:T(8,128)S(1)}, f32[264,128]{1,0:T(8,128)S(1)}, f32[264,128]{1,0:T...) custom-call(s32[2]{0:T(128)S(1)} %pad_add_fusion.idx, ...), custom_call_target="tpu_custom_call", output_to_operand_aliasing={{0}: (11, {})} | custom-call | tf_op jit(solution)/shard_map/pallas_call | solution.py:195
  40.3 2.2 %collective-permute-start.13 = (f32[264,128]{1,0:T(8,128)S(1)}, f32[264,128]{1,0:T(8,128)S(1)}, u32[]{:S(2)}, u32[]{:S(2)}) collective-permute-start(f32[264,128]{1,0:T(8,128)S(1)} %get-tuple-element.39), channel_id=1, source_target_pairs={{0,6},{2,4},{4,2},{6,0},{8,14},{10,12},{12,10},{14,8},{1,7},{3,5},... | collective-permute-start | bytes 405512 | tf_op jit(solution)/shard_map/ppermute | solution.py:208
  42.4 0.1 collective-permute-start.14
  42.5 1.3 %collective-permute-start.15 = (f32[264,128]{1,0:T(8,128)S(1)}, f32[264,128]{1,0:T(8,128)S(1)}, u32[]{:S(2)}, u32[]{:S(2)}) collective-permute-start(f32[264,128]{1,0:T(8,128)S(1)} %get-tuple-element.41), channel_id=1, source_target_pairs={{0,2},{2,0},{4,6},{6,4},{8,10},{10,8},{12,14},{14,12},{1,3},{3,1},... | collective-permute-start | bytes 405512 | tf_op jit(solution)/shard_map/ppermute | solution.py:208
  43.8 2.1 %collective-permute-start.10 = (f32[264,128]{1,0:T(8,128)S(1)}, f32[264,128]{1,0:T(8,128)S(1)}, u32[]{:S(2)}, u32[]{:S(2)}) collective-permute-start(f32[264,128]{1,0:T(8,128)S(1)} %get-tuple-element.35), channel_id=1, source_target_pairs={{0,6},{2,4},{4,2},{6,0},{8,14},{10,12},{12,10},{14,8},{1,7},{3,5},... | collective-permute-start | bytes 405512 | tf_op jit(solution)/shard_map/ppermute | solution.py:208
  45.9 0.1 collective-permute-start.11
  46.0 1.7 %collective-permute-done.13 = f32[264,128]{1,0:T(8,128)S(1)} collective-permute-done((f32[264,128]{1,0:T(8,128)S(1)}, f32[264,128]{1,0:T(8,128)S(1)}, u32[]{:S(2)}, u32[]{:S(2)}) %collective-permute-start.13) | collective-permute-done | bytes 135200 | tf_op jit(solution)/shard_map/ppermute | solution.py:208
  47.7 0.7 %collective-permute-start.12 = (f32[264,128]{1,0:T(8,128)S(1)}, f32[264,128]{1,0:T(8,128)S(1)}, u32[]{:S(2)}, u32[]{:S(2)}) collective-permute-start(f32[264,128]{1,0:T(8,128)S(1)} %get-tuple-element.37), channel_id=1, source_target_pairs={{0,2},{2,0},{4,6},{6,4},{8,10},{10,8},{12,14},{14,12},{1,3},{3,1},... | collective-permute-start | bytes 405512 | tf_op jit(solution)/shard_map/ppermute | solution.py:208
  48.4 1.4 %collective-permute-done.14 = f32[264,128]{1,0:T(8,128)S(1)} collective-permute-done((f32[264,128]{1,0:T(8,128)S(1)}, f32[264,128]{1,0:T(8,128)S(1)}, u32[]{:S(2)}, u32[]{:S(2)}) %collective-permute-start.14) | collective-permute-done | bytes 135200 | tf_op jit(solution)/shard_map/ppermute | solution.py:208
  49.8 2.0 %collective-permute-done.15 = f32[264,128]{1,0:T(8,128)S(1)} collective-permute-done((f32[264,128]{1,0:T(8,128)S(1)}, f32[264,128]{1,0:T(8,128)S(1)}, u32[]{:S(2)}, u32[]{:S(2)}) %collective-permute-start.15) | collective-permute-done | bytes 135200 | tf_op jit(solution)/shard_map/ppermute | solution.py:208
  51.8 2.3 %collective-permute-start.16 = (f32[264,128]{1,0:T(8,128)S(1)}, f32[264,128]{1,0:T(8,128)S(1)}, u32[]{:S(2)}, u32[]{:S(2)}) collective-permute-start(f32[264,128]{1,0:T(8,128)S(1)} %add_add_fusion), channel_id=1, source_target_pairs={{0,12},{2,14},{4,8},{6,10},{8,4},{10,6},{12,0},{14,2},{1,13},{3,15... | collective-permute-start | bytes 405512 | tf_op jit(solution)/shard_map/ppermute | solution.py:208
  54.2 0.0 collective-permute-done.10
  54.2 0.9 %collective-permute-done.11 = f32[264,128]{1,0:T(8,128)S(1)} collective-permute-done((f32[264,128]{1,0:T(8,128)S(1)}, f32[264,128]{1,0:T(8,128)S(1)}, u32[]{:S(2)}, u32[]{:S(2)}) %collective-permute-start.11) | collective-permute-done | bytes 135200 | tf_op jit(solution)/shard_map/ppermute | solution.py:208
  55.1 0.3 collective-permute-done.12
  55.5 3.4 %collective-permute-done.16.more = f32[264,128]{1,0:T(8,128)S(1)} collective-permute-done((f32[264,128]{1,0:T(8,128)S(1)}, f32[264,128]{1,0:T(8,128)S(1)}, u32[]{:S(2)}, u32[]{:S(2)}) %collective-permute-start.16) | collective-permute-done | bytes 135200 | tf_op jit(solution)/shard_map/ppermute | solution.py:208
  58.8 0.0 copy-done.1
  58.8 0.7 %shard_map.56 = f32[32,1024]{1,0:T(8,128)} custom-call(f32[32,1024]{1,0:T(8,128)S(1)} %copy-done.1, f32[264,128]{1,0:T(8,128)S(1)} %add_add_fusion.1.total, f32[264,128]{1,0:T(8,128)S(1)} %collective-permute-done.16.more), custom_call_target="tpu_custom_call" | custom-call | tf_op jit(solution)/shard_map/pallas_call | solution.py:195
  (3 shorter events, 0.1 us)
Async XLA Ops:
  0.6 9.7 %collective-permute-start.4 = (f32[32,1024]{1,0:T(8,128)}, f32[32,1024]{1,0:T(8,128)S(1)}, u32[]{:S(2)}, u32[]{:S(2)}) collective-permute-start(f32[32,1024]{1,0:T(8,128)} %old.1), channel_id=1, source_target_pairs={{0,12},{2,14},{4,8},{6,10},{8,4},{10,6},{12,0},{14,2},{1,13},{3,15... | collective-permute-start | bytes 393224 | tf_op jit(solution)/shard_map/ppermute | solution.py:208
  5.7 8.1 %collective-permute-start.3 = (f32[32,1024]{1,0:T(8,128)}, f32[32,1024]{1,0:T(8,128)S(1)}, u32[]{:S(2)}, u32[]{:S(2)}) collective-permute-start(f32[32,1024]{1,0:T(8,128)} %old.1), channel_id=1, source_target_pairs={{0,6},{2,4},{4,2},{6,0},{8,14},{10,12},{12,10},{14,8},{1,7},{3,5},... | collective-permute-start | bytes 393224 | tf_op jit(solution)/shard_map/ppermute | solution.py:208
  6.2 9.9 %collective-permute-start.2 = (f32[32,1024]{1,0:T(8,128)}, f32[32,1024]{1,0:T(8,128)S(1)}, u32[]{:S(2)}, u32[]{:S(2)}) collective-permute-start(f32[32,1024]{1,0:T(8,128)} %old.1), channel_id=1, source_target_pairs={{0,4},{2,6},{4,0},{6,2},{8,12},{10,14},{12,8},{14,10},{1,5},{3,7},... | collective-permute-start | bytes 393224 | tf_op jit(solution)/shard_map/ppermute | solution.py:208
  8.7 8.5 %collective-permute-start.1 = (f32[32,1024]{1,0:T(8,128)}, f32[32,1024]{1,0:T(8,128)S(1)}, u32[]{:S(2)}, u32[]{:S(2)}) collective-permute-start(f32[32,1024]{1,0:T(8,128)} %old.1), channel_id=1, source_target_pairs={{0,2},{2,0},{4,6},{6,4},{8,10},{10,8},{12,14},{14,12},{1,3},{3,1},... | collective-permute-start | bytes 393224 | tf_op jit(solution)/shard_map/ppermute | solution.py:208
  9.2 9.7 %collective-permute-start = (f32[128,2048]{1,0:T(8,128)}, f32[128,2048]{1,0:T(8,128)S(1)}, u32[]{:S(2)}, u32[]{:S(2)}) collective-permute-start(f32[128,2048]{1,0:T(8,128)} %hown.1), channel_id=1, source_target_pairs={{0,1},{1,0},{2,3},{3,2},{4,5},{5,4},{6,7},{7,6},{8,9},{9,8},{10,11... | collective-permute-start | bytes 3145736 | tf_op jit(solution)/shard_map/ppermute | solution.py:212
  9.2 12.5 %slice-start = ((s8[8388608]{0:T(1024)(128)(4,1)}), s8[4194304]{0:T(1024)(128)(4,1)S(1)}, s32[]{:S(2)}) async-start(s8[8388608]{0:T(1024)(128)(4,1)} %bitcast.2), calls=%async_computation | async-start | bytes 8388608
  9.3 12.5 %slice-start.1 = ((s8[8388608]{0:T(1024)(128)(4,1)}), s8[4194304]{0:T(1024)(128)(4,1)S(1)}, s32[]{:S(2)}) async-start(s8[8388608]{0:T(1024)(128)(4,1)} %bitcast.2), calls=%async_computation.1 | async-start | bytes 8388608
  10.3 10.0 %collective-permute-start.7 = (f32[32,1024]{1,0:T(8,128)S(1)}, f32[32,1024]{1,0:T(8,128)S(1)}, u32[]{:S(2)}, u32[]{:S(2)}) collective-permute-start(f32[32,1024]{1,0:T(8,128)S(1)} %collective-permute-done.4.refs_3_), channel_id=1, source_target_pairs={{0,6},{2,4},{4,2},{6,0},{8,14},{10,12},{12,10},{14,8},{1,7},{3,5},... | collective-permute-start | bytes 393224 | tf_op jit(solution)/shard_map/ppermute | solution.py:208
  13.8 7.1 %collective-permute-start.6 = (f32[32,1024]{1,0:T(8,128)S(1)}, f32[32,1024]{1,0:T(8,128)S(1)}, u32[]{:S(2)}, u32[]{:S(2)}) collective-permute-start(f32[32,1024]{1,0:T(8,128)S(1)} %collective-permute-done.4.refs_3_), channel_id=1, source_target_pairs={{0,4},{2,6},{4,0},{6,2},{8,12},{10,14},{12,8},{14,10},{1,5},{3,7},... | collective-permute-start | bytes 393224 | tf_op jit(solution)/shard_map/ppermute | solution.py:208
  16.2 5.6 %collective-permute-start.5 = (f32[32,1024]{1,0:T(8,128)S(1)}, f32[32,1024]{1,0:T(8,128)S(1)}, u32[]{:S(2)}, u32[]{:S(2)}) collective-permute-start(f32[32,1024]{1,0:T(8,128)S(1)} %collective-permute-done.4.refs_3_), channel_id=1, source_target_pairs={{0,2},{2,0},{4,6},{6,4},{8,10},{10,8},{12,14},{14,12},{1,3},{3,1},... | collective-permute-start | bytes 393224 | tf_op jit(solution)/shard_map/ppermute | solution.py:208
  17.2 0.9 %copy-start = (f32[32,1024]{1,0:T(8,128)S(1)}, f32[32,1024]{1,0:T(8,128)}, u32[]{:S(2)}) copy-start(f32[32,1024]{1,0:T(8,128)} %old.1) | copy-start | bytes 393220
  18.1 1.2 %copy-start.2 = (f32[128,2048]{1,0:T(8,128)S(1)}, f32[128,2048]{1,0:T(8,128)}, u32[]{:S(2)}) copy-start(f32[128,2048]{1,0:T(8,128)} %hown.1) | copy-start | bytes 3145732
  26.6 4.7 %collective-permute-start.8 = (f32[264,1024]{1,0:T(8,128)S(1)}, f32[264,1024]{1,0:T(8,128)S(1)}, u32[]{:S(2)}, u32[]{:S(2)}) collective-permute-start(f32[264,1024]{1,0:T(8,128)S(1)} %get-tuple-element.27.mine.nown), channel_id=1, source_target_pairs={{0,1},{1,0},{2,3},{3,2},{4,5},{5,4},{6,7},{7,6},{8,9},{9,8},{10,11... | collective-permute-start | bytes 3244040 | tf_op jit(solution)/shard_map/ppermute | solution.py:212
  30.7 5.0 %collective-permute-start.9 = (f32[256,1024]{1,0:T(8,128)S(1)}, f32[256,1024]{1,0:T(8,128)S(1)}, u32[]{:S(2)}, u32[]{:S(2)}) collective-permute-start(f32[256,1024]{1,0:T(8,128)S(1)} %shard_map.53.nown), channel_id=1, source_target_pairs={{0,1},{1,0},{2,3},{3,2},{4,5},{5,4},{6,7},{7,6},{8,9},{9,8},{10,11... | collective-permute-start | bytes 3145736 | tf_op jit(solution)/shard_map/ppermute | solution.py:212
  35.7 23.1 %copy-start.1 = (f32[32,1024]{1,0:T(8,128)S(1)}, f32[32,1024]{1,0:T(8,128)}, u32[]{:S(2)}) copy-start(f32[32,1024]{1,0:T(8,128)} %old.1) | copy-start | bytes 393220
  40.3 7.4 %collective-permute-start.13 = (f32[264,128]{1,0:T(8,128)S(1)}, f32[264,128]{1,0:T(8,128)S(1)}, u32[]{:S(2)}, u32[]{:S(2)}) collective-permute-start(f32[264,128]{1,0:T(8,128)S(1)} %get-tuple-element.39), channel_id=1, source_target_pairs={{0,6},{2,4},{4,2},{6,0},{8,14},{10,12},{12,10},{14,8},{1,7},{3,5},... | collective-permute-start | bytes 405512 | tf_op jit(solution)/shard_map/ppermute | solution.py:208
  42.4 7.4 %collective-permute-start.14 = (f32[264,128]{1,0:T(8,128)S(1)}, f32[264,128]{1,0:T(8,128)S(1)}, u32[]{:S(2)}, u32[]{:S(2)}) collective-permute-start(f32[264,128]{1,0:T(8,128)S(1)} %get-tuple-element.40), channel_id=1, source_target_pairs={{0,4},{2,6},{4,0},{6,2},{8,12},{10,14},{12,8},{14,10},{1,5},{3,7},... | collective-permute-start | bytes 405512 | tf_op jit(solution)/shard_map/ppermute | solution.py:208
  42.5 9.3 %collective-permute-start.15 = (f32[264,128]{1,0:T(8,128)S(1)}, f32[264,128]{1,0:T(8,128)S(1)}, u32[]{:S(2)}, u32[]{:S(2)}) collective-permute-start(f32[264,128]{1,0:T(8,128)S(1)} %get-tuple-element.41), channel_id=1, source_target_pairs={{0,2},{2,0},{4,6},{6,4},{8,10},{10,8},{12,14},{14,12},{1,3},{3,1},... | collective-permute-start | bytes 405512 | tf_op jit(solution)/shard_map/ppermute | solution.py:208
  43.8 10.4 %collective-permute-start.10 = (f32[264,128]{1,0:T(8,128)S(1)}, f32[264,128]{1,0:T(8,128)S(1)}, u32[]{:S(2)}, u32[]{:S(2)}) collective-permute-start(f32[264,128]{1,0:T(8,128)S(1)} %get-tuple-element.35), channel_id=1, source_target_pairs={{0,6},{2,4},{4,2},{6,0},{8,14},{10,12},{12,10},{14,8},{1,7},{3,5},... | collective-permute-start | bytes 405512 | tf_op jit(solution)/shard_map/ppermute | solution.py:208
  45.9 9.2 %collective-permute-start.11 = (f32[264,128]{1,0:T(8,128)S(1)}, f32[264,128]{1,0:T(8,128)S(1)}, u32[]{:S(2)}, u32[]{:S(2)}) collective-permute-start(f32[264,128]{1,0:T(8,128)S(1)} %get-tuple-element.36), channel_id=1, source_target_pairs={{0,4},{2,6},{4,0},{6,2},{8,12},{10,14},{12,8},{14,10},{1,5},{3,7},... | collective-permute-start | bytes 405512 | tf_op jit(solution)/shard_map/ppermute | solution.py:208
  47.7 7.8 %collective-permute-start.12 = (f32[264,128]{1,0:T(8,128)S(1)}, f32[264,128]{1,0:T(8,128)S(1)}, u32[]{:S(2)}, u32[]{:S(2)}) collective-permute-start(f32[264,128]{1,0:T(8,128)S(1)} %get-tuple-element.37), channel_id=1, source_target_pairs={{0,2},{2,0},{4,6},{6,4},{8,10},{10,8},{12,14},{14,12},{1,3},{3,1},... | collective-permute-start | bytes 405512 | tf_op jit(solution)/shard_map/ppermute | solution.py:208
  51.8 7.0 %collective-permute-start.16 = (f32[264,128]{1,0:T(8,128)S(1)}, f32[264,128]{1,0:T(8,128)S(1)}, u32[]{:S(2)}, u32[]{:S(2)}) collective-permute-start(f32[264,128]{1,0:T(8,128)S(1)} %add_add_fusion), channel_id=1, source_target_pairs={{0,12},{2,14},{4,8},{6,10},{8,4},{10,6},{12,0},{14,2},{1,13},{3,15... | collective-permute-start | bytes 405512 | tf_op jit(solution)/shard_map/ppermute | solution.py:208

commit v4 on v3

--- a/solution.py
+++ b/solution.py
@@ -9,9 +9,8 @@
 
 f32, bf16 = jnp.float32, jnp.bfloat16
 WHOLE = pl.BlockSpec(memory_space=pltpu.VMEM)
-SCALARS = pl.BlockSpec(memory_space=pltpu.SMEM)
 HBM = pl.BlockSpec(memory_space=pl.ANY)
-GATHER_CROSS, REDUCE_CROSS = 6, 6
+GATHER_CROSS, REDUCE_CROSS = 4, 6
 PIECES = 2
 FC, NC = 256, 512
 
@@ -46,32 +45,46 @@
     return jnp.broadcast_to(tile[:, lane : lane + 1], (8, 128))
 
 
-def prepare(idx, ws, w2, wt, mass, first):
+def whereabouts(cube):
+    place, core = lax.axis_index("frames"), lax.axis_index("bins")
+    return (place & 3, core ^ (place >> 2)) if cube else (place, core)
+
+
+def prepare(ws, w2, wt, mass, first):
     rows = ws[0].shape[0]
     half = len(ws) * rows
+    place_of_mine = whereabouts(True)[0]
     for s, w in enumerate(ws):
         x = w[...]
         hi, lo = split(x)
-        place = (idx[0] ^ (s ^ first)) if len(ws) > 1 else 0
+        place = (place_of_mine ^ (s ^ first)) if len(ws) > 1 else 0
         w2[rows_at(place, rows), :] = hi
         w2[rows_at(place + half // rows, rows), :] = lo
         mass[rows_at(place, rows), :] = jnp.broadcast_to(jnp.sum(x, axis=1, keepdims=True), (rows, 128))
     wt[...] = w2[...].T
 
 
-def prepare_kernel(idx, *refs):
+def prepare_kernel(*refs):
     *ws, w2, wt, mass = refs
-    prepare(idx, ws, w2, wt, mass, 0)
-
-
-def order_kernel(idx, hown, hoth, h, h2):
-    half = hown.shape[0]
-    for place, old in ((idx[1], hown), (1 - idx[1], hoth)):
-        x = old[...]
-        hi, lo = split(x)
-        h[rows_at(place, half), :] = x
-        h2[rows_at(place, half), :] = hi
-        h2[rows_at(place + 2, half), :] = lo
+    prepare(ws, w2, wt, mass, 0)
+
+
+def own_kernel(hown, atoms, h, h2, kept, *, cube):
+    place_rows(hown, h, h2, whereabouts(cube)[1])
+    kept[...] = atoms[...]
+
+
+def other_kernel(hoth, _h, _h2, h, h2, *, cube):
+    place_rows(hoth, h, h2, 1 - whereabouts(cube)[1])
+
+
+def place_rows(old, h, h2, place):
+    half = old.shape[0]
+    x = old[...]
+    hi, lo = split(x)
+    h[rows_at(place, half), :] = x
+    h2[rows_at(place, half), :] = hi
+    h2[rows_at(place + 2, half), :] = lo
 
 
 def by_three(parts, rows):
@@ -81,14 +94,14 @@
     return jnp.concatenate(hi + lo + hi, axis=1)
 
 
-def first_kernel(idx, v, h2, *refs, start, n_parts, masses, raw):
+def first_kernel(v, h2, *refs, start, n_parts, masses, raw):
     refs = list(refs)
     take = lambda n: [refs.pop(0) for _ in range(n)]
     w2, wt = take(n_parts), take(n_parts)
     mass, ws, (numer,) = take(masses), take(raw), take(1)
     if raw:
         made = take(3)
-        prepare(idx, ws, *made, GATHER_CROSS & 3)
+        prepare(ws, *made, GATHER_CROSS & 3)
         w2.append(made[0])
         wt.append(made[1])
         mass.append(made[2])
@@ -112,7 +125,7 @@
         numer[atoms:, :128] = pack(lambda i: mass[i // part][i % part : i % part + 8, :], atoms)
 
 
-def second_kernel(idx, v, h, mine, theirs, nown, noth, *refs, start, n_parts, before, n_out):
+def second_kernel(v, h, mine, theirs, nown, noth, *refs, start, n_parts, before, n_out):
     refs = list(refs)
     take = lambda n: [refs.pop(0) for _ in range(n)]
     wt = take(n_parts)
@@ -121,6 +134,7 @@
     (newact,) = take(1)
     outs = take(max(n_out, 2) if n_out != 1 else 1)
     fresh_own, f2, rhi, rlo, acc, scale, o_sems = refs
+    place_of_mine, half_of_mine = whereabouts(n_parts > 1)
     bins, frames = rhi.shape
     atoms = h.shape[0]
     half = atoms // 2
@@ -140,7 +154,7 @@
         sums = row if sums is None else sums + row
         written.append(
             pltpu.make_async_copy(
-                fresh_own.at[rows_at(idx[1], half), pl.ds(n, NC)],
+                fresh_own.at[rows_at(half_of_mine, half), pl.ds(n, NC)],
                 newact.at[:, pl.ds(start + n, NC)],
                 o_sems.at[n // NC],
             )
@@ -169,7 +183,7 @@
         scale[...] = row_mass
         rows = atoms // n_out
         for s, o in enumerate(outs):
-            place = (idx[0] ^ (s & 3)) + (s & 4)
+            place = (place_of_mine ^ (s & 3)) + (s & 4)
             base = pl.multiple_of(place * rows, rows)
             for i in range(rows // 8):
                 for j in range(bins // 128):
@@ -215,41 +229,45 @@
     atoms = 2 * half
     rows = atoms_by_bin.shape[0]
     cube = n_dev == 8 and rows % 16 == 0
-    place, core = lax.axis_index("frames"), lax.axis_index("bins")
-    idx = jnp.stack([place & 3, core ^ (place >> 2)] if cube else [place, core]).astype(jnp.int32)
     size = frames // PIECES
 
     def basis_outs(k):
         return [((2 * k, bins), bf16), ((bins, 2 * k), bf16), ((k, 128), f32)]
 
-    other = swap(activations)
+    ordered = [((atoms, frames), f32), ((2 * atoms, frames), bf16)]
+    h, h2, kept = call(
+        functools.partial(own_kernel, cube=cube),
+        [activations, atoms_by_bin],
+        ordered + [((rows, bins), f32)],
+        mib=16,
+        flops=10**10,
+    )
     raw = []
     if cube:
+        near = [hop(atoms_by_bin, s) for s in (1, 2, 3)]
         far = hop(atoms_by_bin, GATHER_CROSS)
-        near = [hop(atoms_by_bin, s) for s in (1, 2, 3)]
         raw = [far] + [hop(far, s) for s in (1, 2, 3)]
-        near = [atoms_by_bin, *near]
+        near = [kept, *near]
     else:
         near = [lax.all_gather(atoms_by_bin, "frames", axis=0, tiled=True)]
     h, h2 = call(
-        order_kernel,
-        [idx, activations, other],
-        [((atoms, frames), f32), ((2 * atoms, frames), bf16)],
-        in_specs=[SCALARS],
+        functools.partial(other_kernel, cube=cube),
+        [swap(activations), h, h2],
+        ordered,
+        aliases={1: 0, 2: 1},
         mib=16,
         flops=10**9,
     )
     k = sum(w.shape[0] for w in near)
-    w2, wt, mass = call(prepare_kernel, [idx, *near], basis_outs(k), in_specs=[SCALARS], mib=16, flops=10**10)
+    w2, wt, mass = call(prepare_kernel, near, basis_outs(k), mib=16, flops=10**10)
     w2, wt, mass = [w2], [wt], [mass]
     numers = []
     for p in range(PIECES):
         numer, *made = call(
             functools.partial(first_kernel, start=p * size, n_parts=len(wt), masses=len(mass), raw=len(raw)),
-            [idx, spectrum, h2, *w2, *wt, *mass, *raw],
+            [spectrum, h2, *w2, *wt, *mass, *raw],
             [((atoms + 8 * (p == 0), size), f32)] + (basis_outs(atoms - k) if raw else []),
             scratch=[((bins, size), bf16), ((bins, size), bf16)],
-            in_specs=[SCALARS],
         )
         if raw:
             w2.append(made[0])
@@ -261,7 +279,7 @@
     carried = []
     for p in range(PIECES):
         final = p == PIECES - 1
-        ins = [idx, spectrum, h, *numers[0], *numers[p], *wt]
+        ins = [spectrum, h, *numers[0], *numers[p], *wt]
         fresh, *carried = call(
             functools.partial(
                 second_kernel, start=p * size, n_parts=len(wt), before=p > 0, n_out=n_out if final else 0
@@ -278,7 +296,7 @@
                 ((atoms, 128), f32),
                 pltpu.SemaphoreType.DMA((size // NC,)),
             ],
-            in_specs=[SCALARS] + ([WHOLE] * (len(ins) + 1) + [HBM] if p else []),
+            in_specs=[WHOLE] * (len(ins) + 2) + [HBM] if p else [],
             out_specs=[HBM],
             aliases={len(ins) + 2: 0} if p else None,
         )
@@ -291,7 +309,7 @@
         total = parts[0]
         for s in (3, 2, 1):
             total = total + hop(parts[s], s)
-        (new,) = call(last_kernel, [atoms_by_bin, total, more], [((rows, bins), f32)], mib=16)
+        (new,) = call(last_kernel, [kept, total, more], [((rows, bins), f32)], mib=16)
         return fresh, new
     total = lax.psum_scatter(parts[0], "frames", scatter_dimension=0, tiled=True)
     return fresh, atoms_by_bin * total[:, :bins] / total[:, bins : bins + 1]

time: 59.7 us -> 57 us (0.955)
  Pallas kernels: 20.4 us -> 16.6 us
  waiting for transfers between devices: 13.1 us -> 15.8 us
  starting transfers between devices: 23.8 us -> 21.5 us
  local copies, waits for them, and re-layouts: 1.3 us -> 2.14 us
    pallas_call x7 -> x8, Pallas kernels: 20.4 us -> 16.6 us  [call(): pl.pallas_call(kernel, in_specs=list(in_specs) + [WHOLE] * (len(ins) - le...]
    ppermute x14, waiting for transfers between devices: 13.1 us -> 15.8 us  [hop(): return lax.ppermute(x, 'frames', [(i, i ^ step) for i in range(8)])]
    ppermute x14, starting transfers between devices: 23.2 us -> 20.9 us  [hop(): return lax.ppermute(x, 'frames', [(i, i ^ step) for i in range(8)])]
    unnamed x10 -> x8, local copies, waits for them, and re-layouts: 1.3 us -> 2.14 us
  transfers between devices with their start and end apart: 17 -> 17, of which waited for: 11 -> 9; matrix products, arithmetic and copies ran while one was open for 0% -> 0% of each run, Pallas kernels for 17% -> 14%
where the time goes in v4:
time: 57 us; the launch traced here: 56.9 us
  starting transfers between devices  21.5 us (38%)
  Pallas kernels  16.6 us (29%)
  waiting for transfers between devices  15.8 us (28%)
  local copies, waits for them, and re-layouts  2.14 us (4%)
  between operations  0.71 us (1%)
    ppermute x14, starting transfers between devices, hop(): return lax.ppermute(x, 'frames', [(i, i ^ step) for i in range(8)])  20.9 us
    pallas_call x8, Pallas kernels, call(): pl.pallas_call(kernel, in_specs=list(in_specs) + [WHOLE] * (len(ins) - le...  16.6 us
    ppermute x14, waiting for transfers between devices, hop(): return lax.ppermute(x, 'frames', [(i, i ^ step) for i in range(8)])  15.8 us
    unnamed x8, local copies, waits for them, and re-layouts  2.14 us
  transfers between devices with their start and end apart: 17, of which 9 were waited for; matrix products, arithmetic and copies ran while one was open for 0% of the time, Pallas kernels for 14%

profile of v4, /device:TPU:0, one launch (start us, length us, event | category | flops | bytes accessed | tf_op | source)
XLA Modules:
  0.0 56.9 jit_solution(11108329218376569766)
XLA Ops:
  0.6 3.1 %collective-permute-start.2 = (f32[32,1024]{1,0:T(8,128)}, f32[32,1024]{1,0:T(8,128)S(1)}, u32[]{:S(2)}, u32[]{:S(2)}) collective-permute-start(f32[32,1024]{1,0:T(8,128)} %atoms.1), channel_id=1, source_target_pairs={{0,4},{2,6},{4,0},{6,2},{8,12},{10,14},{12,8},{14,10},{1,5},{3,7},... | collective-permute-start | bytes 393224 | tf_op jit(solution)/shard_map/ppermute | solution.py:222
  3.7 1.5 %collective-permute-start.1 = (f32[32,1024]{1,0:T(8,128)}, f32[32,1024]{1,0:T(8,128)S(1)}, u32[]{:S(2)}, u32[]{:S(2)}) collective-permute-start(f32[32,1024]{1,0:T(8,128)} %atoms.1), channel_id=1, source_target_pairs={{0,2},{2,0},{4,6},{6,4},{8,10},{10,8},{12,14},{14,12},{1,3},{3,1},... | collective-permute-start | bytes 393224 | tf_op jit(solution)/shard_map/ppermute | solution.py:222
  5.2 2.6 %collective-permute-start.4 = (f32[32,1024]{1,0:T(8,128)}, f32[32,1024]{1,0:T(8,128)S(1)}, u32[]{:S(2)}, u32[]{:S(2)}) collective-permute-start(f32[32,1024]{1,0:T(8,128)} %atoms.1), channel_id=1, source_target_pairs={{0,8},{2,10},{4,12},{6,14},{8,0},{10,2},{12,4},{14,6},{1,9},{3,11}... | collective-permute-start | bytes 393224 | tf_op jit(solution)/shard_map/ppermute | solution.py:222
  7.8 0.4 collective-permute-start.3
  8.2 0.0 collective-permute-start
  8.2 0.0 copy-start
  8.2 1.2 %copy-done = f32[128,2048]{1,0:T(8,128)S(1)} copy-done((f32[128,2048]{1,0:T(8,128)S(1)}, f32[128,2048]{1,0:T(8,128)}, u32[]{:S(2)}) %copy-start) | copy-done | bytes 1048600
  9.4 0.0 copy-start.1
  9.5 0.9 %copy-done.1 = f32[32,1024]{1,0:T(8,128)S(1)} copy-done((f32[32,1024]{1,0:T(8,128)S(1)}, f32[32,1024]{1,0:T(8,128)}, u32[]{:S(2)}) %copy-start.1) | copy-done | bytes 131096
  10.4 0.2 shard_map.50
  10.6 3.3 %collective-permute-done.4.refs_3_ = f32[32,1024]{1,0:T(8,128)S(1)} collective-permute-done((f32[32,1024]{1,0:T(8,128)}, f32[32,1024]{1,0:T(8,128)S(1)}, u32[]{:S(2)}, u32[]{:S(2)}) %collective-permute-start.4) | collective-permute-done | bytes 131104 | tf_op jit(solution)/shard_map/ppermute | solution.py:222
  13.9 1.1 %collective-permute-start.7 = (f32[32,1024]{1,0:T(8,128)S(1)}, f32[32,1024]{1,0:T(8,128)S(1)}, u32[]{:S(2)}, u32[]{:S(2)}) collective-permute-start(f32[32,1024]{1,0:T(8,128)S(1)} %collective-permute-done.4.refs_3_), channel_id=1, source_target_pairs={{0,6},{2,4},{4,2},{6,0},{8,14},{10,12},{12,10},{14,8},{1,7},{3,5},... | collective-permute-start | bytes 393224 | tf_op jit(solution)/shard_map/ppermute | solution.py:222
  15.1 0.0 collective-permute-done.2.refs_2_
  15.1 0.1 collective-permute-start.6
  15.2 0.0 collective-permute-done.1.refs_1_
  15.2 2.2 %collective-permute-start.5 = (f32[32,1024]{1,0:T(8,128)S(1)}, f32[32,1024]{1,0:T(8,128)S(1)}, u32[]{:S(2)}, u32[]{:S(2)}) collective-permute-start(f32[32,1024]{1,0:T(8,128)S(1)} %collective-permute-done.4.refs_3_), channel_id=1, source_target_pairs={{0,2},{2,0},{4,6},{6,4},{8,10},{10,8},{12,14},{14,12},{1,3},{3,1},... | collective-permute-start | bytes 393224 | tf_op jit(solution)/shard_map/ppermute | solution.py:222
  17.4 0.0 collective-permute-done.3.refs_3_
  17.4 0.0 slice-start
  17.4 0.0 slice-start.1
  17.4 0.3 shard_map.52
  17.7 0.0 collective-permute-done.hoth
  17.7 0.2 shard_map.51
  18.0 1.9 %collective-permute-done.7.refs_6_ = f32[32,1024]{1,0:T(8,128)S(1)} collective-permute-done((f32[32,1024]{1,0:T(8,128)S(1)}, f32[32,1024]{1,0:T(8,128)S(1)}, u32[]{:S(2)}, u32[]{:S(2)}) %collective-permute-start.7) | collective-permute-done | bytes 131104 | tf_op jit(solution)/shard_map/ppermute | solution.py:222
  19.9 0.4 collective-permute-done.6.refs_5_
  20.3 0.9 %collective-permute-done.5.refs_4_ = f32[32,1024]{1,0:T(8,128)S(1)} collective-permute-done((f32[32,1024]{1,0:T(8,128)S(1)}, f32[32,1024]{1,0:T(8,128)S(1)}, u32[]{:S(2)}, u32[]{:S(2)}) %collective-permute-start.5) | collective-permute-done | bytes 131104 | tf_op jit(solution)/shard_map/ppermute | solution.py:222
  21.2 0.0 slice-done
  21.2 0.0 slice-done.1
  21.2 4.1 %shard_map.53 = (f32[264,1024]{1,0:T(8,128)S(1)}, bf16[256,1024]{1,0:T(8,128)(2,1)S(1)}, bf16[1024,256]{1,0:T(8,128)(2,1)S(1)}, f32[128,128]{1,0:T(8,128)}) custom-call(f32[1024,2048]{1,0:T(8,128)S(1)} %bitcast.1, bf16[512,2048]{1,0:T(8,128)(2,1)S(1)} %get-tuple-element.28.h2, bf16[256,1024]{1,0:T(8,128)(2,1)S(1)} %get-tuple-element.30.refs_0_, ...), custom_call_target="tpu_custom_call" | custom-call | tf_op jit(solution)/shard_map/pallas_call | solution.py:209
  25.4 0.0 collective-permute-start.8
  25.4 3.4 %shard_map.54.nown = f32[256,1024]{1,0:T(8,128)S(1)} custom-call(f32[1024,2048]{1,0:T(8,128)S(1)} %bitcast.1, bf16[512,2048]{1,0:T(8,128)(2,1)S(1)} %get-tuple-element.28.h2, bf16[256,1024]{1,0:T(8,128)(2,1)S(1)} %get-tuple-element.30.refs_0_, bf16[256,1024]{1,0:T(8,128)(2,1)S(1)} %get-tuple-element.34.refs_1_, ...), custom_call_target="tpu_custom_call" | custom-call | tf_op jit(solution)/shard_map/pallas_call | solution.py:209
  28.8 0.6 %collective-permute-start.9 = (f32[256,1024]{1,0:T(8,128)S(1)}, f32[256,1024]{1,0:T(8,128)S(1)}, u32[]{:S(2)}, u32[]{:S(2)}) collective-permute-start(f32[256,1024]{1,0:T(8,128)S(1)} %shard_map.54.nown), channel_id=1, source_target_pairs={{0,1},{1,0},{2,3},{3,2},{4,5},{5,4},{6,7},{7,6},{8,9},{9,8},{10,11... | collective-permute-start | bytes 3145736 | tf_op jit(solution)/shard_map/ppermute | solution.py:226
  29.4 0.0 collective-permute-done.8.theirs.noth
  29.4 3.7 %shard_map.55 = (f32[128,2048]{1,0:T(8,128)}, f32[256,1024]{1,0:T(8,128)S(1)}, f32[256,128]{1,0:T(8,128)S(1)}) custom-call(f32[1024,2048]{1,0:T(8,128)S(1)} %bitcast.1, f32[256,2048]{1,0:T(8,128)S(1)} %get-tuple-element.27.h, f32[264,1024]{1,0:T(8,128)S(1)} %get-tuple-element.33.mine.nown, f32[264,1024]{1,0:T(8,128)S(1)} %collective-permute-done.8.theirs.noth, ...), custom_call_target="tpu_custom_call" | custom-call | tf_op jit(solution)/shard_map/pallas_call | solution.py:209
  33.1 0.0 collective-permute-done.9.noth
  33.1 3.8 %shard_map.56 = (f32[128,2048]{1,0:T(8,128)}, f32[264,128]{1,0:T(8,128)S(1)}, f32[264,128]{1,0:T(8,128)S(1)}, f32[264,128]{1,0:T(8,128)S(1)}, f32[264,128]{1,0:T...) custom-call(f32[1024,2048]{1,0:T(8,128)S(1)} %bitcast.1, ...), custom_call_target="tpu_custom_call", output_to_operand_aliasing={{0}: (10, {})} | custom-call | tf_op jit(solution)/shard_map/pallas_call | solution.py:209
  37.0 1.6 %collective-permute-start.13 = (f32[264,128]{1,0:T(8,128)S(1)}, f32[264,128]{1,0:T(8,128)S(1)}, u32[]{:S(2)}, u32[]{:S(2)}) collective-permute-start(f32[264,128]{1,0:T(8,128)S(1)} %get-tuple-element.45), channel_id=1, source_target_pairs={{0,6},{2,4},{4,2},{6,0},{8,14},{10,12},{12,10},{14,8},{1,7},{3,5},... | collective-permute-start | bytes 405512 | tf_op jit(solution)/shard_map/ppermute | solution.py:222
  38.6 1.1 %collective-permute-start.14 = (f32[264,128]{1,0:T(8,128)S(1)}, f32[264,128]{1,0:T(8,128)S(1)}, u32[]{:S(2)}, u32[]{:S(2)}) collective-permute-start(f32[264,128]{1,0:T(8,128)S(1)} %get-tuple-element.46), channel_id=1, source_target_pairs={{0,4},{2,6},{4,0},{6,2},{8,12},{10,14},{12,8},{14,10},{1,5},{3,7},... | collective-permute-start | bytes 405512 | tf_op jit(solution)/shard_map/ppermute | solution.py:222
  39.7 0.9 %collective-permute-start.15 = (f32[264,128]{1,0:T(8,128)S(1)}, f32[264,128]{1,0:T(8,128)S(1)}, u32[]{:S(2)}, u32[]{:S(2)}) collective-permute-start(f32[264,128]{1,0:T(8,128)S(1)} %get-tuple-element.47), channel_id=1, source_target_pairs={{0,2},{2,0},{4,6},{6,4},{8,10},{10,8},{12,14},{14,12},{1,3},{3,1},... | collective-permute-start | bytes 405512 | tf_op jit(solution)/shard_map/ppermute | solution.py:222
  40.5 1.6 %collective-permute-start.10 = (f32[264,128]{1,0:T(8,128)S(1)}, f32[264,128]{1,0:T(8,128)S(1)}, u32[]{:S(2)}, u32[]{:S(2)}) collective-permute-start(f32[264,128]{1,0:T(8,128)S(1)} %get-tuple-element.41), channel_id=1, source_target_pairs={{0,6},{2,4},{4,2},{6,0},{8,14},{10,12},{12,10},{14,8},{1,7},{3,5},... | collective-permute-start | bytes 405512 | tf_op jit(solution)/shard_map/ppermute | solution.py:222
  42.1 1.1 %collective-permute-start.11 = (f32[264,128]{1,0:T(8,128)S(1)}, f32[264,128]{1,0:T(8,128)S(1)}, u32[]{:S(2)}, u32[]{:S(2)}) collective-permute-start(f32[264,128]{1,0:T(8,128)S(1)} %get-tuple-element.42), channel_id=1, source_target_pairs={{0,4},{2,6},{4,0},{6,2},{8,12},{10,14},{12,8},{14,10},{1,5},{3,7},... | collective-permute-start | bytes 405512 | tf_op jit(solution)/shard_map/ppermute | solution.py:222
  43.1 1.2 %collective-permute-done.13 = f32[264,128]{1,0:T(8,128)S(1)} collective-permute-done((f32[264,128]{1,0:T(8,128)S(1)}, f32[264,128]{1,0:T(8,128)S(1)}, u32[]{:S(2)}, u32[]{:S(2)}) %collective-permute-start.13) | collective-permute-done | bytes 135200 | tf_op jit(solution)/shard_map/ppermute | solution.py:222
  44.4 1.2 %collective-permute-start.12 = (f32[264,128]{1,0:T(8,128)S(1)}, f32[264,128]{1,0:T(8,128)S(1)}, u32[]{:S(2)}, u32[]{:S(2)}) collective-permute-start(f32[264,128]{1,0:T(8,128)S(1)} %get-tuple-element.43), channel_id=1, source_target_pairs={{0,2},{2,0},{4,6},{6,4},{8,10},{10,8},{12,14},{14,12},{1,3},{3,1},... | collective-permute-start | bytes 405512 | tf_op jit(solution)/shard_map/ppermute | solution.py:222
  45.5 1.4 %collective-permute-done.14 = f32[264,128]{1,0:T(8,128)S(1)} collective-permute-done((f32[264,128]{1,0:T(8,128)S(1)}, f32[264,128]{1,0:T(8,128)S(1)}, u32[]{:S(2)}, u32[]{:S(2)}) %collective-permute-start.14) | collective-permute-done | bytes 135200 | tf_op jit(solution)/shard_map/ppermute | solution.py:222
  47.0 2.1 %collective-permute-done.15 = f32[264,128]{1,0:T(8,128)S(1)} collective-permute-done((f32[264,128]{1,0:T(8,128)S(1)}, f32[264,128]{1,0:T(8,128)S(1)}, u32[]{:S(2)}, u32[]{:S(2)}) %collective-permute-start.15) | collective-permute-done | bytes 135200 | tf_op jit(solution)/shard_map/ppermute | solution.py:222
  49.1 2.5 %collective-permute-start.16 = (f32[264,128]{1,0:T(8,128)S(1)}, f32[264,128]{1,0:T(8,128)S(1)}, u32[]{:S(2)}, u32[]{:S(2)}) collective-permute-start(f32[264,128]{1,0:T(8,128)S(1)} %add_add_fusion), channel_id=1, source_target_pairs={{0,12},{2,14},{4,8},{6,10},{8,4},{10,6},{12,0},{14,2},{1,13},{3,15... | collective-permute-start | bytes 405512 | tf_op jit(solution)/shard_map/ppermute | solution.py:222
  51.6 0.0 collective-permute-done.10
  51.6 0.6 %collective-permute-done.11 = f32[264,128]{1,0:T(8,128)S(1)} collective-permute-done((f32[264,128]{1,0:T(8,128)S(1)}, f32[264,128]{1,0:T(8,128)S(1)}, u32[]{:S(2)}, u32[]{:S(2)}) %collective-permute-start.11) | collective-permute-done | bytes 135200 | tf_op jit(solution)/shard_map/ppermute | solution.py:222
  52.2 0.0 collective-permute-done.12
  52.3 3.8 %collective-permute-done.16.more = f32[264,128]{1,0:T(8,128)S(1)} collective-permute-done((f32[264,128]{1,0:T(8,128)S(1)}, f32[264,128]{1,0:T(8,128)S(1)}, u32[]{:S(2)}, u32[]{:S(2)}) %collective-permute-start.16) | collective-permute-done | bytes 135200 | tf_op jit(solution)/shard_map/ppermute | solution.py:222
  56.1 0.7 %shard_map.57 = f32[32,1024]{1,0:T(8,128)} custom-call(f32[32,1024]{1,0:T(8,128)S(1)} %get-tuple-element.29.refs_0_.old, f32[264,128]{1,0:T(8,128)S(1)} %add_add_fusion.1.total, f32[264,128]{1,0:T(8,128)S(1)} %collective-permute-done.16.more), custom_call_target="tpu_custom_call" | custom-call | tf_op jit(solution)/shard_map/pallas_call | solution.py:209
  (3 shorter events, 0.1 us)
Async XLA Ops:
  0.6 14.4 %collective-permute-start.2 = (f32[32,1024]{1,0:T(8,128)}, f32[32,1024]{1,0:T(8,128)S(1)}, u32[]{:S(2)}, u32[]{:S(2)}) collective-permute-start(f32[32,1024]{1,0:T(8,128)} %atoms.1), channel_id=1, source_target_pairs={{0,4},{2,6},{4,0},{6,2},{8,12},{10,14},{12,8},{14,10},{1,5},{3,7},... | collective-permute-start | bytes 393224 | tf_op jit(solution)/shard_map/ppermute | solution.py:222
  3.7 11.5 %collective-permute-start.1 = (f32[32,1024]{1,0:T(8,128)}, f32[32,1024]{1,0:T(8,128)S(1)}, u32[]{:S(2)}, u32[]{:S(2)}) collective-permute-start(f32[32,1024]{1,0:T(8,128)} %atoms.1), channel_id=1, source_target_pairs={{0,2},{2,0},{4,6},{6,4},{8,10},{10,8},{12,14},{14,12},{1,3},{3,1},... | collective-permute-start | bytes 393224 | tf_op jit(solution)/shard_map/ppermute | solution.py:222
  5.2 8.7 %collective-permute-start.4 = (f32[32,1024]{1,0:T(8,128)}, f32[32,1024]{1,0:T(8,128)S(1)}, u32[]{:S(2)}, u32[]{:S(2)}) collective-permute-start(f32[32,1024]{1,0:T(8,128)} %atoms.1), channel_id=1, source_target_pairs={{0,8},{2,10},{4,12},{6,14},{8,0},{10,2},{12,4},{14,6},{1,9},{3,11}... | collective-permute-start | bytes 393224 | tf_op jit(solution)/shard_map/ppermute | solution.py:222
  7.8 9.6 %collective-permute-start.3 = (f32[32,1024]{1,0:T(8,128)}, f32[32,1024]{1,0:T(8,128)S(1)}, u32[]{:S(2)}, u32[]{:S(2)}) collective-permute-start(f32[32,1024]{1,0:T(8,128)} %atoms.1), channel_id=1, source_target_pairs={{0,6},{2,4},{4,2},{6,0},{8,14},{10,12},{12,10},{14,8},{1,7},{3,5},... | collective-permute-start | bytes 393224 | tf_op jit(solution)/shard_map/ppermute | solution.py:222
  8.2 9.5 %collective-permute-start = (f32[128,2048]{1,0:T(8,128)}, f32[128,2048]{1,0:T(8,128)S(1)}, u32[]{:S(2)}, u32[]{:S(2)}) collective-permute-start(f32[128,2048]{1,0:T(8,128)} %hown.1), channel_id=1, source_target_pairs={{0,1},{1,0},{2,3},{3,2},{4,5},{5,4},{6,7},{7,6},{8,9},{9,8},{10,11... | collective-permute-start | bytes 3145736 | tf_op jit(solution)/shard_map/ppermute | solution.py:226
  8.2 1.2 %copy-start = (f32[128,2048]{1,0:T(8,128)S(1)}, f32[128,2048]{1,0:T(8,128)}, u32[]{:S(2)}) copy-start(f32[128,2048]{1,0:T(8,128)} %hown.1) | copy-start | bytes 3145732
  9.4 0.9 %copy-start.1 = (f32[32,1024]{1,0:T(8,128)S(1)}, f32[32,1024]{1,0:T(8,128)}, u32[]{:S(2)}) copy-start(f32[32,1024]{1,0:T(8,128)} %atoms.1) | copy-start | bytes 393220
  13.9 6.0 %collective-permute-start.7 = (f32[32,1024]{1,0:T(8,128)S(1)}, f32[32,1024]{1,0:T(8,128)S(1)}, u32[]{:S(2)}, u32[]{:S(2)}) collective-permute-start(f32[32,1024]{1,0:T(8,128)S(1)} %collective-permute-done.4.refs_3_), channel_id=1, source_target_pairs={{0,6},{2,4},{4,2},{6,0},{8,14},{10,12},{12,10},{14,8},{1,7},{3,5},... | collective-permute-start | bytes 393224 | tf_op jit(solution)/shard_map/ppermute | solution.py:222
  15.1 5.2 %collective-permute-start.6 = (f32[32,1024]{1,0:T(8,128)S(1)}, f32[32,1024]{1,0:T(8,128)S(1)}, u32[]{:S(2)}, u32[]{:S(2)}) collective-permute-start(f32[32,1024]{1,0:T(8,128)S(1)} %collective-permute-done.4.refs_3_), channel_id=1, source_target_pairs={{0,4},{2,6},{4,0},{6,2},{8,12},{10,14},{12,8},{14,10},{1,5},{3,7},... | collective-permute-start | bytes 393224 | tf_op jit(solution)/shard_map/ppermute | solution.py:222
  15.2 6.0 %collective-permute-start.5 = (f32[32,1024]{1,0:T(8,128)S(1)}, f32[32,1024]{1,0:T(8,128)S(1)}, u32[]{:S(2)}, u32[]{:S(2)}) collective-permute-start(f32[32,1024]{1,0:T(8,128)S(1)} %collective-permute-done.4.refs_3_), channel_id=1, source_target_pairs={{0,2},{2,0},{4,6},{6,4},{8,10},{10,8},{12,14},{14,12},{1,3},{3,1},... | collective-permute-start | bytes 393224 | tf_op jit(solution)/shard_map/ppermute | solution.py:222
  17.4 3.8 %slice-start = ((s8[8388608]{0:T(1024)(128)(4,1)}), s8[4194304]{0:T(1024)(128)(4,1)S(1)}, s32[]{:S(2)}) async-start(s8[8388608]{0:T(1024)(128)(4,1)} %bitcast), calls=%async_computation | async-start | bytes 8388608
  17.4 3.8 %slice-start.1 = ((s8[8388608]{0:T(1024)(128)(4,1)}), s8[4194304]{0:T(1024)(128)(4,1)S(1)}, s32[]{:S(2)}) async-start(s8[8388608]{0:T(1024)(128)(4,1)} %bitcast), calls=%async_computation.1 | async-start | bytes 8388608
  25.4 4.0 %collective-permute-start.8 = (f32[264,1024]{1,0:T(8,128)S(1)}, f32[264,1024]{1,0:T(8,128)S(1)}, u32[]{:S(2)}, u32[]{:S(2)}) collective-permute-start(f32[264,1024]{1,0:T(8,128)S(1)} %get-tuple-element.33.mine.nown), channel_id=1, source_target_pairs={{0,1},{1,0},{2,3},{3,2},{4,5},{5,4},{6,7},{7,6},{8,9},{9,8},{10,11... | collective-permute-start | bytes 3244040 | tf_op jit(solution)/shard_map/ppermute | solution.py:226
  28.8 4.3 %collective-permute-start.9 = (f32[256,1024]{1,0:T(8,128)S(1)}, f32[256,1024]{1,0:T(8,128)S(1)}, u32[]{:S(2)}, u32[]{:S(2)}) collective-permute-start(f32[256,1024]{1,0:T(8,128)S(1)} %shard_map.54.nown), channel_id=1, source_target_pairs={{0,1},{1,0},{2,3},{3,2},{4,5},{5,4},{6,7},{7,6},{8,9},{9,8},{10,11... | collective-permute-start | bytes 3145736 | tf_op jit(solution)/shard_map/ppermute | solution.py:226
  37.0 7.4 %collective-permute-start.13 = (f32[264,128]{1,0:T(8,128)S(1)}, f32[264,128]{1,0:T(8,128)S(1)}, u32[]{:S(2)}, u32[]{:S(2)}) collective-permute-start(f32[264,128]{1,0:T(8,128)S(1)} %get-tuple-element.45), channel_id=1, source_target_pairs={{0,6},{2,4},{4,2},{6,0},{8,14},{10,12},{12,10},{14,8},{1,7},{3,5},... | collective-permute-start | bytes 405512 | tf_op jit(solution)/shard_map/ppermute | solution.py:222
  38.6 8.4 %collective-permute-start.14 = (f32[264,128]{1,0:T(8,128)S(1)}, f32[264,128]{1,0:T(8,128)S(1)}, u32[]{:S(2)}, u32[]{:S(2)}) collective-permute-start(f32[264,128]{1,0:T(8,128)S(1)} %get-tuple-element.46), channel_id=1, source_target_pairs={{0,4},{2,6},{4,0},{6,2},{8,12},{10,14},{12,8},{14,10},{1,5},{3,7},... | collective-permute-start | bytes 405512 | tf_op jit(solution)/shard_map/ppermute | solution.py:222
  39.7 9.4 %collective-permute-start.15 = (f32[264,128]{1,0:T(8,128)S(1)}, f32[264,128]{1,0:T(8,128)S(1)}, u32[]{:S(2)}, u32[]{:S(2)}) collective-permute-start(f32[264,128]{1,0:T(8,128)S(1)} %get-tuple-element.47), channel_id=1, source_target_pairs={{0,2},{2,0},{4,6},{6,4},{8,10},{10,8},{12,14},{14,12},{1,3},{3,1},... | collective-permute-start | bytes 405512 | tf_op jit(solution)/shard_map/ppermute | solution.py:222
  40.5 11.1 %collective-permute-start.10 = (f32[264,128]{1,0:T(8,128)S(1)}, f32[264,128]{1,0:T(8,128)S(1)}, u32[]{:S(2)}, u32[]{:S(2)}) collective-permute-start(f32[264,128]{1,0:T(8,128)S(1)} %get-tuple-element.41), channel_id=1, source_target_pairs={{0,6},{2,4},{4,2},{6,0},{8,14},{10,12},{12,10},{14,8},{1,7},{3,5},... | collective-permute-start | bytes 405512 | tf_op jit(solution)/shard_map/ppermute | solution.py:222
  42.1 10.2 %collective-permute-start.11 = (f32[264,128]{1,0:T(8,128)S(1)}, f32[264,128]{1,0:T(8,128)S(1)}, u32[]{:S(2)}, u32[]{:S(2)}) collective-permute-start(f32[264,128]{1,0:T(8,128)S(1)} %get-tuple-element.42), channel_id=1, source_target_pairs={{0,4},{2,6},{4,0},{6,2},{8,12},{10,14},{12,8},{14,10},{1,5},{3,7},... | collective-permute-start | bytes 405512 | tf_op jit(solution)/shard_map/ppermute | solution.py:222
  44.4 7.9 %collective-permute-start.12 = (f32[264,128]{1,0:T(8,128)S(1)}, f32[264,128]{1,0:T(8,128)S(1)}, u32[]{:S(2)}, u32[]{:S(2)}) collective-permute-start(f32[264,128]{1,0:T(8,128)S(1)} %get-tuple-element.43), channel_id=1, source_target_pairs={{0,2},{2,0},{4,6},{6,4},{8,10},{10,8},{12,14},{14,12},{1,3},{3,1},... | collective-permute-start | bytes 405512 | tf_op jit(solution)/shard_map/ppermute | solution.py:222
  49.1 7.0 %collective-permute-start.16 = (f32[264,128]{1,0:T(8,128)S(1)}, f32[264,128]{1,0:T(8,128)S(1)}, u32[]{:S(2)}, u32[]{:S(2)}) collective-permute-start(f32[264,128]{1,0:T(8,128)S(1)} %add_add_fusion), channel_id=1, source_target_pairs={{0,12},{2,14},{4,8},{6,10},{8,4},{10,6},{12,0},{14,2},{1,13},{3,15... | collective-permute-start | bytes 405512 | tf_op jit(solution)/shard_map/ppermute | solution.py:222

commit v5 on v4

--- a/solution.py
+++ b/solution.py
@@ -50,23 +50,28 @@
     return (place & 3, core ^ (place >> 2)) if cube else (place, core)
 
 
-def prepare(ws, w2, wt, mass, first):
+def prepare(ws, w2, wt, mass, first, columns):
     rows = ws[0].shape[0]
     half = len(ws) * rows
     place_of_mine = whereabouts(True)[0]
     for s, w in enumerate(ws):
-        x = w[...]
+        x = w[:, columns]
         hi, lo = split(x)
         place = (place_of_mine ^ (s ^ first)) if len(ws) > 1 else 0
-        w2[rows_at(place, rows), :] = hi
-        w2[rows_at(place + half // rows, rows), :] = lo
-        mass[rows_at(place, rows), :] = jnp.broadcast_to(jnp.sum(x, axis=1, keepdims=True), (rows, 128))
-    wt[...] = w2[...].T
+        w2[rows_at(place, rows), columns] = hi
+        w2[rows_at(place + half // rows, rows), columns] = lo
+        total = sum(x[:, i : i + 128] for i in range(0, x.shape[1], 128))
+        if columns.start:
+            total = total + mass[rows_at(place, rows), :]
+        if columns.stop == w.shape[1]:
+            total = jnp.broadcast_to(jnp.sum(total, axis=1, keepdims=True), total.shape)
+        mass[rows_at(place, rows), :] = total
+    wt[columns, :] = w2[:, columns].T
 
 
 def prepare_kernel(*refs):
     *ws, w2, wt, mass = refs
-    prepare(ws, w2, wt, mass, 0)
+    prepare(ws, w2, wt, mass, 0, slice(0, wt.shape[0]))
 
 
 def own_kernel(hown, atoms, h, h2, kept, *, cube):
@@ -87,37 +92,55 @@
     h2[rows_at(place + 2, half), :] = lo
 
 
+def hi_lo(parts, rows):
+    half = parts[0].shape[1] // 2
+    return [w[rows, :half] for w in parts], [w[rows, half:] for w in parts]
+
+
 def by_three(parts, rows):
-    half = parts[0].shape[1] // 2
-    hi = [w[rows, :half] for w in parts]
-    lo = [w[rows, half:] for w in parts]
+    hi, lo = hi_lo(parts, rows)
     return jnp.concatenate(hi + lo + hi, axis=1)
 
 
-def first_kernel(v, h2, *refs, start, n_parts, masses, raw):
+def near_kernel(wt, h2, model):
+    half = wt.shape[1] // 2
+    h = jnp.concatenate([h2[:half, :], h2[:half, :]], axis=0)
+    for f in range(0, wt.shape[0], FC):
+        model[f : f + FC, :] = dot(wt[f : f + FC, :], h)
+
+
+def first_kernel(v, h2, *refs, start, n_parts, masses, raw, near):
     refs = list(refs)
     take = lambda n: [refs.pop(0) for _ in range(n)]
+    (model,) = take(1) if near else (None,)
     w2, wt = take(n_parts), take(n_parts)
     mass, ws, (numer,) = take(masses), take(raw), take(1)
     if raw:
         made = take(3)
-        prepare(ws, *made, GATHER_CROSS & 3)
         w2.append(made[0])
         wt.append(made[1])
         mass.append(made[2])
     rhi, rlo = refs
     bins, frames = rhi.shape
     atoms = h2.shape[0] // 2
-    whi = jnp.concatenate([w[: w.shape[0] // 2, :] for w in w2], axis=0)
-    wlo = jnp.concatenate([w[w.shape[0] // 2 :, :] for w in w2], axis=0)
     for n in range(0, frames, NC):
         at, src = slice(n, n + NC), slice(start + n, start + n + NC)
-        h3 = jnp.concatenate([h2[:atoms, src], h2[:atoms, src], h2[atoms:, src]], axis=0)
+        top = h2[atoms // 2 if near else 0 : atoms, src]
+        h3 = jnp.concatenate([top, top, h2[atoms:, src]], axis=0)
         for f in range(0, bins, FC):
-            m = dot(by_three(wt, slice(f, f + FC)), h3)
-            hi, lo = split(v[f : f + FC, src] / m)
-            rhi[f : f + FC, at] = hi
-            rlo[f : f + FC, at] = lo
+            rows = slice(f, f + FC)
+            if raw and n == 0:
+                prepare(ws, *made, GATHER_CROSS & 3, rows)
+            if near:
+                hi, lo = hi_lo(wt, rows)
+                m = model[rows, src] + dot(jnp.concatenate([hi[1], lo[1], *hi], axis=1), h3)
+            else:
+                m = dot(by_three(wt, rows), h3)
+            hi, lo = split(v[rows, src] / m)
+            rhi[rows, at] = hi
+            rlo[rows, at] = lo
+        whi = jnp.concatenate([w[: w.shape[0] // 2, :] for w in w2], axis=0)
+        wlo = jnp.concatenate([w[w.shape[0] // 2 :, :] for w in w2], axis=0)
         numer[:atoms, at] = dot(whi, rhi[:, at]) + dot(wlo, rhi[:, at]) + dot(whi, rlo[:, at])
     if mass:
         part = mass[0].shape[0]
@@ -130,14 +153,14 @@
     take = lambda n: [refs.pop(0) for _ in range(n)]
     wt = take(n_parts)
     if before:
-        acc_in, row_in, _ = take(3)
-    (newact,) = take(1)
-    outs = take(max(n_out, 2) if n_out != 1 else 1)
-    fresh_own, f2, rhi, rlo, acc, scale, o_sems = refs
-    place_of_mine, half_of_mine = whereabouts(n_parts > 1)
+        acc_in, row_in, other_rhi, other_f2, _ = take(5)
+    newact, acc, row_mass, rhi, f2 = take(5)
+    outs = take(n_out)
+    fresh, rlo, scale, cross, o_sems = refs
     bins, frames = rhi.shape
     atoms = h.shape[0]
     half = atoms // 2
+    half_of_mine = whereabouts(n_parts > 1)[1]
     tile = 1.0 / (mine[atoms:, :128] + theirs[atoms:, :128])
     for i in range(atoms // 8):
         scale[8 * i : 8 * i + 8, :] = unpack(tile, i, atoms)
@@ -145,53 +168,71 @@
     written = []
     for n in range(0, frames, NC):
         at, src = slice(n, n + NC), slice(start + n, start + n + NC)
-        fresh = h[:, src] * (nown[:atoms, at] + noth[:atoms, at]) * scale[:, :1]
-        fresh_own[:, at] = fresh
-        hhi, hlo = split(fresh)
-        f2[:atoms, at] = hhi
-        f2[atoms:, at] = hlo
-        row = jnp.sum(fresh, axis=1, keepdims=True)
+        x = h[:, src] * (nown[:atoms, at] + noth[:atoms, at]) * scale[:, :1]
+        fresh[:, at] = x
+        hi, lo = split(x)
+        f2[:atoms, at] = hi
+        f2[atoms:, at] = lo
+        row = jnp.sum(x, axis=1, keepdims=True)
         sums = row if sums is None else sums + row
         written.append(
             pltpu.make_async_copy(
-                fresh_own.at[rows_at(half_of_mine, half), pl.ds(n, NC)],
+                fresh.at[rows_at(half_of_mine, half), pl.ds(n, NC)],
                 newact.at[:, pl.ds(start + n, NC)],
                 o_sems.at[n // NC],
             )
         )
         written[-1].start()
-    for n in range(0, frames, NC):
-        at, src = slice(n, n + NC), slice(start + n, start + n + NC)
         h3 = jnp.concatenate([f2[:atoms, at], f2[:atoms, at], f2[atoms:, at]], axis=0)
         for f in range(0, bins, FC):
             m = dot(by_three(wt, slice(f, f + FC)), h3)
             hi, lo = split(v[f : f + FC, src] / m)
             rhi[f : f + FC, at] = hi
             rlo[f : f + FC, at] = lo
-    total = dot_nt(f2[:atoms, :], rhi[...]) + dot_nt(f2[atoms:, :], rhi[...]) + dot_nt(f2[:atoms, :], rlo[...])
+    row_mass[...] = jnp.broadcast_to(sums, (atoms, 128))
+    total = dot_nt(f2[:atoms, :], rlo[...])
     if before:
         total = total + acc_in[...]
-    row_mass = jnp.broadcast_to(sums, (atoms, 128))
-    if n_out == 0:
-        outs[0][...] = total
-        outs[1][...] = row_mass
-    elif n_out == 1:
-        outs[0][:, :bins] = total
-        outs[0][:, bins:] = row_mass
+        acc[...] = total[:half, :]
+        cross[...] = total[half:, :] + by_high(half, (f2, rhi), (other_f2, other_rhi))
+        write_blocks(outs, cross, row_mass, half, atoms // 8)
     else:
         acc[...] = total
-        scale[...] = row_mass
-        rows = atoms // n_out
-        for s, o in enumerate(outs):
-            place = (place_of_mine ^ (s & 3)) + (s & 4)
-            base = pl.multiple_of(place * rows, rows)
-            for i in range(rows // 8):
-                for j in range(bins // 128):
-                    k = 8 * (i * (bins // 128) + j)
-                    o[k : k + 8, :] = acc[pl.ds(base + 8 * i, 8), 128 * j : 128 * (j + 1)]
-            o[rows * bins // 128 :, :] = pack(lambda i: scale[pl.ds(base + i, 8), :], rows)
     for copy in written:
         copy.wait()
+
+
+def by_high(start, *pairs):
+    total = None
+    for f2, rhi in pairs:
+        atoms = f2.shape[0] // 2
+        half = atoms // 2
+        rows = [f2[start : start + half, :], f2[atoms + start : atoms + start + half, :]]
+        x = dot_nt(jnp.concatenate(rows, axis=0), rhi[...])
+        total = x if total is None else total + x
+    return total[: total.shape[0] // 2, :] + total[total.shape[0] // 2 :, :]
+
+
+def write_blocks(outs, acc, row_mass, start, rows):
+    bins = acc.shape[1]
+    if len(outs) == 1:
+        outs[0][:, :bins] = acc[...]
+        outs[0][:, bins:] = row_mass[start : start + acc.shape[0], :]
+        return
+    place_of_mine = whereabouts(True)[0]
+    for s, o in enumerate(outs):
+        base = pl.multiple_of((place_of_mine ^ s) * rows, rows)
+        for i in range(rows // 8):
+            for j in range(bins // 128):
+                k = 8 * (i * (bins // 128) + j)
+                o[k : k + 8, :] = acc[pl.ds(base + 8 * i, 8), 128 * j : 128 * (j + 1)]
+        o[rows * bins // 128 :, :] = pack(lambda i: row_mass[pl.ds(start + base + i, 8), :], rows)
+
+
+def third_kernel(acc, row_mass, rhi_a, f2_a, rhi_b, f2_b, *refs):
+    *outs, own = refs
+    own[...] = acc[...] + by_high(0, (f2_b, rhi_b), (f2_a, rhi_a))
+    write_blocks(outs, own, row_mass, 0, f2_a.shape[0] // 16)
 
 
 def last_kernel(old, total, more, new):
@@ -260,12 +301,13 @@
     )
     k = sum(w.shape[0] for w in near)
     w2, wt, mass = call(prepare_kernel, near, basis_outs(k), mib=16, flops=10**10)
+    model = call(near_kernel, [wt, h2], [((bins, frames), f32)], mib=16, flops=10**10) if cube else []
     w2, wt, mass = [w2], [wt], [mass]
     numers = []
     for p in range(PIECES):
         numer, *made = call(
-            functools.partial(first_kernel, start=p * size, n_parts=len(wt), masses=len(mass), raw=len(raw)),
-            [spectrum, h2, *w2, *wt, *mass, *raw],
+            functools.partial(first_kernel, start=p * size, n_parts=len(wt), masses=len(mass), raw=len(raw), near=cube),
+            [spectrum, h2, *model, *w2, *wt, *mass, *raw],
             [((atoms + 8 * (p == 0), size), f32)] + (basis_outs(atoms - k) if raw else []),
             scratch=[((bins, size), bf16), ((bins, size), bf16)],
         )
@@ -274,44 +316,48 @@
             wt.append(made[1])
         raw, mass = [], []
         numers.append((numer, swap(numer)))
-    n_out = n_dev if cube else 1
-    block = (rows * bins // 128 + 8, 128) if cube else (atoms, bins + 128)
+    n_out = 4 if cube else 1
+    block = ((rows * bins // 128 + 8, 128) if cube else (half, bins + 128), f32)
     carried = []
     for p in range(PIECES):
         final = p == PIECES - 1
-        ins = [spectrum, h, *numers[0], *numers[p], *wt]
-        fresh, *carried = call(
-            functools.partial(
-                second_kernel, start=p * size, n_parts=len(wt), before=p > 0, n_out=n_out if final else 0
-            ),
-            ins + carried + ([fresh] if p else []),
-            [((half, frames), f32)]
-            + ([(block, f32)] * n_out if final else [((atoms, bins), f32), ((atoms, 128), f32)]),
+        ins = [spectrum, h, *numers[0], *numers[p], *wt, *carried]
+        outs = [
+            ((half, frames), f32),
+            ((half if final else atoms, bins), f32),
+            ((atoms, 128), f32),
+            ((bins, size), bf16),
+            ((2 * atoms, size), bf16),
+        ]
+        fresh, *made = call(
+            functools.partial(second_kernel, start=p * size, n_parts=len(wt), before=p > 0, n_out=n_out * final),
+            ins + ([fresh] if p else []),
+            outs + [block] * n_out * final,
             scratch=[
                 ((atoms, size), f32),
-                ((2 * atoms, size), bf16),
                 ((bins, size), bf16),
-                ((bins, size), bf16),
-                ((atoms, bins), f32),
                 ((atoms, 128), f32),
+                ((half, bins), f32),
                 pltpu.SemaphoreType.DMA((size // NC,)),
             ],
-            in_specs=[WHOLE] * (len(ins) + 2) + [HBM] if p else [],
+            in_specs=[WHOLE] * len(ins) + [HBM] if p else [],
             out_specs=[HBM],
-            aliases={len(ins) + 2: 0} if p else None,
+            aliases={len(ins): 0} if p else None,
         )
-    parts = carried
+        before, carried = carried[2:], made[:4]
+    away = made[4:]
+    home = call(third_kernel, carried + before, [block] * n_out, scratch=[((half, bins), f32)], flops=10**9)
     if cube:
-        total = parts[REDUCE_CROSS]
+        total = away[REDUCE_CROSS & 3]
         for s in (3, 2, 1):
-            total = total + hop(parts[s ^ REDUCE_CROSS], s)
+            total = total + hop(away[s ^ (REDUCE_CROSS & 3)], s)
         more = hop(total, REDUCE_CROSS)
-        total = parts[0]
+        total = home[0]
         for s in (3, 2, 1):
-            total = total + hop(parts[s], s)
+            total = total + hop(home[s], s)
         (new,) = call(last_kernel, [kept, total, more], [((rows, bins), f32)], mib=16)
         return fresh, new
-    total = lax.psum_scatter(parts[0], "frames", scatter_dimension=0, tiled=True)
+    total = lax.psum_scatter(jnp.concatenate([*home, *away]), "frames", scatter_dimension=0, tiled=True)
     return fresh, atoms_by_bin * total[:, :bins] / total[:, bins : bins + 1]
 
 

time: 57 us -> 55.2 us (0.968)
  waiting for transfers between devices: 15.8 us -> 13.2 us
  Pallas kernels: 16.6 us -> 17.5 us
    ppermute x14, waiting for transfers between devices: 15.8 us -> 13.2 us  [hop(): return lax.ppermute(x, 'frames', [(i, i ^ step) for i in range(8)])]
    pallas_call x8 -> x10, Pallas kernels: 16.6 us -> 17.5 us  [call(): pl.pallas_call(kernel, in_specs=list(in_specs) + [WHOLE] * (len(ins) - le...]
  transfers between devices with their start and end apart: 17 -> 17, of which waited for: 9 -> 10; matrix products, arithmetic and copies ran while one was open for 0% -> 0% of each run, Pallas kernels for 14% -> 17%
where the time goes in v5:
time: 55.2 us; the launch traced here: 55 us
  starting transfers between devices  21.2 us (38%)
  Pallas kernels  17.5 us (32%)
  waiting for transfers between devices  13.2 us (24%)
  local copies, waits for them, and re-layouts  2.36 us (4%)
  between operations  0.73 us (1%)
    ppermute x14, starting transfers between devices, hop(): return lax.ppermute(x, 'frames', [(i, i ^ step) for i in range(8)])  20.6 us
    pallas_call x10, Pallas kernels, call(): pl.pallas_call(kernel, in_specs=list(in_specs) + [WHOLE] * (len(ins) - le...  17.5 us
    ppermute x14, waiting for transfers between devices, hop(): return lax.ppermute(x, 'frames', [(i, i ^ step) for i in range(8)])  13.2 us
    unnamed x8, local copies, waits for them, and re-layouts  2.36 us
  transfers between devices with their start and end apart: 17, of which 10 were waited for; matrix products, arithmetic and copies ran while one was open for 0% of the time, Pallas kernels for 17%

profile of v5, /device:TPU:0, one launch (start us, length us, event | category | flops | bytes accessed | tf_op | source)
XLA Modules:
  0.0 55.0 jit_solution(14249531176916350702)
XLA Ops:
  0.6 3.1 %collective-permute-start.2 = (f32[32,1024]{1,0:T(8,128)}, f32[32,1024]{1,0:T(8,128)S(1)}, u32[]{:S(2)}, u32[]{:S(2)}) collective-permute-start(f32[32,1024]{1,0:T(8,128)} %atoms.1), channel_id=1, source_target_pairs={{0,4},{2,6},{4,0},{6,2},{8,12},{10,14},{12,8},{14,10},{1,5},{3,7},... | collective-permute-start | bytes 393224 | tf_op jit(solution)/shard_map/ppermute | solution.py:263
  3.7 1.5 %collective-permute-start.1 = (f32[32,1024]{1,0:T(8,128)}, f32[32,1024]{1,0:T(8,128)S(1)}, u32[]{:S(2)}, u32[]{:S(2)}) collective-permute-start(f32[32,1024]{1,0:T(8,128)} %atoms.1), channel_id=1, source_target_pairs={{0,2},{2,0},{4,6},{6,4},{8,10},{10,8},{12,14},{14,12},{1,3},{3,1},... | collective-permute-start | bytes 393224 | tf_op jit(solution)/shard_map/ppermute | solution.py:263
  5.2 2.6 %collective-permute-start.4 = (f32[32,1024]{1,0:T(8,128)}, f32[32,1024]{1,0:T(8,128)S(1)}, u32[]{:S(2)}, u32[]{:S(2)}) collective-permute-start(f32[32,1024]{1,0:T(8,128)} %atoms.1), channel_id=1, source_target_pairs={{0,8},{2,10},{4,12},{6,14},{8,0},{10,2},{12,4},{14,6},{1,9},{3,11}... | collective-permute-start | bytes 393224 | tf_op jit(solution)/shard_map/ppermute | solution.py:263
  7.8 0.4 collective-permute-start.3
  8.2 0.0 collective-permute-start
  8.2 0.0 copy-start
  8.2 1.2 %copy-done = f32[128,2048]{1,0:T(8,128)S(1)} copy-done((f32[128,2048]{1,0:T(8,128)S(1)}, f32[128,2048]{1,0:T(8,128)}, u32[]{:S(2)}) %copy-start) | copy-done | bytes 1048600
  9.4 0.0 copy-start.1
  9.5 0.9 %copy-done.1 = f32[32,1024]{1,0:T(8,128)S(1)} copy-done((f32[32,1024]{1,0:T(8,128)S(1)}, f32[32,1024]{1,0:T(8,128)}, u32[]{:S(2)}) %copy-start.1) | copy-done | bytes 131096
  10.4 0.2 shard_map.50
  10.6 3.3 %collective-permute-done.4.refs_4_ = f32[32,1024]{1,0:T(8,128)S(1)} collective-permute-done((f32[32,1024]{1,0:T(8,128)}, f32[32,1024]{1,0:T(8,128)S(1)}, u32[]{:S(2)}, u32[]{:S(2)}) %collective-permute-start.4) | collective-permute-done | bytes 131104 | tf_op jit(solution)/shard_map/ppermute | solution.py:263
  13.9 1.1 %collective-permute-start.7 = (f32[32,1024]{1,0:T(8,128)S(1)}, f32[32,1024]{1,0:T(8,128)S(1)}, u32[]{:S(2)}, u32[]{:S(2)}) collective-permute-start(f32[32,1024]{1,0:T(8,128)S(1)} %collective-permute-done.4.refs_4_), channel_id=1, source_target_pairs={{0,6},{2,4},{4,2},{6,0},{8,14},{10,12},{12,10},{14,8},{1,7},{3,5},... | collective-permute-start | bytes 393224 | tf_op jit(solution)/shard_map/ppermute | solution.py:263
  15.1 0.0 collective-permute-done.2.refs_2_
  15.1 0.1 collective-permute-start.6
  15.2 0.0 collective-permute-done.1.refs_1_
  15.2 2.2 %collective-permute-start.5 = (f32[32,1024]{1,0:T(8,128)S(1)}, f32[32,1024]{1,0:T(8,128)S(1)}, u32[]{:S(2)}, u32[]{:S(2)}) collective-permute-start(f32[32,1024]{1,0:T(8,128)S(1)} %collective-permute-done.4.refs_4_), channel_id=1, source_target_pairs={{0,2},{2,0},{4,6},{6,4},{8,10},{10,8},{12,14},{14,12},{1,3},{3,1},... | collective-permute-start | bytes 393224 | tf_op jit(solution)/shard_map/ppermute | solution.py:263
  17.4 0.0 collective-permute-done.3.refs_3_
  17.4 0.3 shard_map.52
  17.7 0.0 collective-permute-done.hoth
  17.7 0.2 shard_map.51
  18.0 0.0 slice-start
  18.0 0.0 slice-start.1
  18.0 1.3 %shard_map.53.refs_0_ = f32[1024,2048]{1,0:T(8,128)S(1)} custom-call(bf16[1024,256]{1,0:T(8,128)(2,1)S(1)} %get-tuple-element.36.wt.refs_2_.refs_3_.refs_0_, bf16[512,2048]{1,0:T(8,128)(2,1)S(1)} %get-tuple-element.34.h2), custom_call_target="tpu_custom_call" | custom-call | flops 10000000000 | tf_op jit(solution)/shard_map/pallas_call | solution.py:250
  19.3 0.7 %collective-permute-done.7.refs_7_ = f32[32,1024]{1,0:T(8,128)S(1)} collective-permute-done((f32[32,1024]{1,0:T(8,128)S(1)}, f32[32,1024]{1,0:T(8,128)S(1)}, u32[]{:S(2)}, u32[]{:S(2)}) %collective-permute-start.7) | collective-permute-done | bytes 131104 | tf_op jit(solution)/shard_map/ppermute | solution.py:263
  19.9 0.4 collective-permute-done.6.refs_6_
  20.3 0.9 %collective-permute-done.5.refs_5_ = f32[32,1024]{1,0:T(8,128)S(1)} collective-permute-done((f32[32,1024]{1,0:T(8,128)S(1)}, f32[32,1024]{1,0:T(8,128)S(1)}, u32[]{:S(2)}, u32[]{:S(2)}) %collective-permute-start.5) | collective-permute-done | bytes 131104 | tf_op jit(solution)/shard_map/ppermute | solution.py:263
  21.2 0.0 slice-done
  21.2 0.2 slice-done.1
  21.5 3.5 %shard_map.54 = (f32[264,1024]{1,0:T(8,128)S(1)}, bf16[256,1024]{1,0:T(8,128)(2,1)S(1)}, bf16[1024,256]{1,0:T(8,128)(2,1)S(1)}, f32[128,128]{1,0:T(8,128)}) custom-call(f32[1024,2048]{1,0:T(8,128)S(1)} %bitcast.1, bf16[512,2048]{1,0:T(8,128)(2,1)S(1)} %get-tuple-element.34.h2, f32[1024,2048]{1,0:T(8,128)S(1)} %shard_map.53.refs_0_, ...), custom_call_target="tpu_custom_call" | custom-call | tf_op jit(solution)/shard_map/pallas_call | solution.py:250
  25.0 0.0 collective-permute-start.8
  25.0 3.0 %shard_map.55.nown = f32[256,1024]{1,0:T(8,128)S(1)} custom-call(f32[1024,2048]{1,0:T(8,128)S(1)} %bitcast.1, bf16[512,2048]{1,0:T(8,128)(2,1)S(1)} %get-tuple-element.34.h2, f32[1024,2048]{1,0:T(8,128)S(1)} %shard_map.53.refs_0_, bf16[256,1024]{1,0:T(8,128)(2,1)S(1)} %get-tuple-element.37.refs_1_, bf16[256,1024]{1,0:T(8,128)(2,1)S(1)} %get-tuple-element.40.refs_2_, ...), custom_call_target="tpu_custom_call" | custom-call | tf_op jit(solution)/shard_map/pallas_call | solution.py:250
  28.0 0.6 %collective-permute-start.9 = (f32[256,1024]{1,0:T(8,128)S(1)}, f32[256,1024]{1,0:T(8,128)S(1)}, u32[]{:S(2)}, u32[]{:S(2)}) collective-permute-start(f32[256,1024]{1,0:T(8,128)S(1)} %shard_map.55.nown), channel_id=1, source_target_pairs={{0,1},{1,0},{2,3},{3,2},{4,5},{5,4},{6,7},{7,6},{8,9},{9,8},{10,11... | collective-permute-start | bytes 3145736 | tf_op jit(solution)/shard_map/ppermute | solution.py:267
  28.6 0.0 collective-permute-done.8.theirs.noth
  28.6 2.8 %shard_map.56 = (f32[128,2048]{1,0:T(8,128)}, f32[256,1024]{1,0:T(8,128)S(1)}, f32[256,128]{1,0:T(8,128)S(1)}, bf16[1024,1024]{1,0:T(8,128)(2,1)S(1)}, bf16[512,1024]{1,0:T(8,128)(2,1)S(1)}) custom-call(f32[1024,2048]{1,0:T(8,128)S(1)} %bitcast.1, f32[256,2048]{1,0:T(8,128)S(1)} %get-tuple-element.33.h, f32[264,1024]{1,0:T(8,128)S(1)} %get-tuple-element.39.mine.nown, ...), custom_call_target="tpu_custom_call" | custom-call | tf_op jit(solution)/shard_map/pallas_call | solution.py:250
  31.4 0.0 collective-permute-done.9.noth
  31.4 4.1 %shard_map.57 = (f32[128,2048]{1,0:T(8,128)}, f32[128,1024]{1,0:T(8,128)S(1)}, f32[256,128]{1,0:T(8,128)S(1)}, bf16[1024,1024]{1,0:T(8,128)(2,1)S(1)}, bf16[512,...) custom-call(f32[1024,2048]{1,0:T(8,128)S(1)} %bitcast.1, ...), custom_call_target="tpu_custom_call", output_to_operand_aliasing={{0}: (12, {})} | custom-call | tf_op jit(solution)/shard_map/pallas_call | solution.py:250
  35.4 1.4 %collective-permute-start.13 = (f32[264,128]{1,0:T(8,128)S(1)}, f32[264,128]{1,0:T(8,128)S(1)}, u32[]{:S(2)}, u32[]{:S(2)}) collective-permute-start(f32[264,128]{1,0:T(8,128)S(1)} %get-tuple-element.57), channel_id=1, source_target_pairs={{0,6},{2,4},{4,2},{6,0},{8,14},{10,12},{12,10},{14,8},{1,7},{3,5},... | collective-permute-start | bytes 405512 | tf_op jit(solution)/shard_map/ppermute | solution.py:263
  36.9 1.0 %collective-permute-start.14 = (f32[264,128]{1,0:T(8,128)S(1)}, f32[264,128]{1,0:T(8,128)S(1)}, u32[]{:S(2)}, u32[]{:S(2)}) collective-permute-start(f32[264,128]{1,0:T(8,128)S(1)} %get-tuple-element.58), channel_id=1, source_target_pairs={{0,4},{2,6},{4,0},{6,2},{8,12},{10,14},{12,8},{14,10},{1,5},{3,7},... | collective-permute-start | bytes 405512 | tf_op jit(solution)/shard_map/ppermute | solution.py:263
  37.9 1.1 %collective-permute-start.15 = (f32[264,128]{1,0:T(8,128)S(1)}, f32[264,128]{1,0:T(8,128)S(1)}, u32[]{:S(2)}, u32[]{:S(2)}) collective-permute-start(f32[264,128]{1,0:T(8,128)S(1)} %get-tuple-element.59), channel_id=1, source_target_pairs={{0,2},{2,0},{4,6},{6,4},{8,10},{10,8},{12,14},{14,12},{1,3},{3,1},... | collective-permute-start | bytes 405512 | tf_op jit(solution)/shard_map/ppermute | solution.py:263
  39.0 1.3 %shard_map.58 = (f32[264,128]{1,0:T(8,128)S(1)}, f32[264,128]{1,0:T(8,128)S(1)}, f32[264,128]{1,0:T(8,128)S(1)}, f32[264,128]{1,0:T(8,128)S(1)}) custom-call(f32[128,1024]{1,0:T(8,128)S(1)} %get-tuple-element.48.acc, f32[256,128]{1,0:T(8,128)S(1)} %get-tuple-element.49.row_mass, bf16[1024,1024]{1,0:T(8,128)(2,1)S(1)} %get-tuple-element.50.rhi_a, ...), custom_call_target="tpu_custom_call" | custom-call | flops 1000000000 | tf_op jit(solution)/shard_map/pallas_call | solution.py:250
  40.3 1.4 %collective-permute-start.10 = (f32[264,128]{1,0:T(8,128)S(1)}, f32[264,128]{1,0:T(8,128)S(1)}, u32[]{:S(2)}, u32[]{:S(2)}) collective-permute-start(f32[264,128]{1,0:T(8,128)S(1)} %get-tuple-element.53), channel_id=1, source_target_pairs={{0,6},{2,4},{4,2},{6,0},{8,14},{10,12},{12,10},{14,8},{1,7},{3,5},... | collective-permute-start | bytes 405512 | tf_op jit(solution)/shard_map/ppermute | solution.py:263
  41.7 1.0 %collective-permute-start.11 = (f32[264,128]{1,0:T(8,128)S(1)}, f32[264,128]{1,0:T(8,128)S(1)}, u32[]{:S(2)}, u32[]{:S(2)}) collective-permute-start(f32[264,128]{1,0:T(8,128)S(1)} %get-tuple-element.54), channel_id=1, source_target_pairs={{0,4},{2,6},{4,0},{6,2},{8,12},{10,14},{12,8},{14,10},{1,5},{3,7},... | collective-permute-start | bytes 405512 | tf_op jit(solution)/shard_map/ppermute | solution.py:263
  42.8 0.1 collective-permute-done.13
  42.9 1.0 %collective-permute-start.12 = (f32[264,128]{1,0:T(8,128)S(1)}, f32[264,128]{1,0:T(8,128)S(1)}, u32[]{:S(2)}, u32[]{:S(2)}) collective-permute-start(f32[264,128]{1,0:T(8,128)S(1)} %get-tuple-element.55), channel_id=1, source_target_pairs={{0,2},{2,0},{4,6},{6,4},{8,10},{10,8},{12,14},{14,12},{1,3},{3,1},... | collective-permute-start | bytes 405512 | tf_op jit(solution)/shard_map/ppermute | solution.py:263
  43.9 1.4 %collective-permute-done.14 = f32[264,128]{1,0:T(8,128)S(1)} collective-permute-done((f32[264,128]{1,0:T(8,128)S(1)}, f32[264,128]{1,0:T(8,128)S(1)}, u32[]{:S(2)}, u32[]{:S(2)}) %collective-permute-start.14) | collective-permute-done | bytes 135200 | tf_op jit(solution)/shard_map/ppermute | solution.py:263
  45.2 2.0 %collective-permute-done.15 = f32[264,128]{1,0:T(8,128)S(1)} collective-permute-done((f32[264,128]{1,0:T(8,128)S(1)}, f32[264,128]{1,0:T(8,128)S(1)}, u32[]{:S(2)}, u32[]{:S(2)}) %collective-permute-start.15) | collective-permute-done | bytes 135200 | tf_op jit(solution)/shard_map/ppermute | solution.py:263
  47.2 0.1 add_add_fusion
  47.3 2.5 %collective-permute-start.16 = (f32[264,128]{1,0:T(8,128)S(1)}, f32[264,128]{1,0:T(8,128)S(1)}, u32[]{:S(2)}, u32[]{:S(2)}) collective-permute-start(f32[264,128]{1,0:T(8,128)S(1)} %add_add_fusion), channel_id=1, source_target_pairs={{0,12},{2,14},{4,8},{6,10},{8,4},{10,6},{12,0},{14,2},{1,13},{3,15... | collective-permute-start | bytes 405512 | tf_op jit(solution)/shard_map/ppermute | solution.py:263
  49.8 0.0 collective-permute-done.10
  49.8 0.6 %collective-permute-done.11 = f32[264,128]{1,0:T(8,128)S(1)} collective-permute-done((f32[264,128]{1,0:T(8,128)S(1)}, f32[264,128]{1,0:T(8,128)S(1)}, u32[]{:S(2)}, u32[]{:S(2)}) %collective-permute-start.11) | collective-permute-done | bytes 135200 | tf_op jit(solution)/shard_map/ppermute | solution.py:263
  50.3 0.3 collective-permute-done.12
  50.6 0.1 add_add_fusion.1.total
  50.7 3.6 %collective-permute-done.16.more = f32[264,128]{1,0:T(8,128)S(1)} collective-permute-done((f32[264,128]{1,0:T(8,128)S(1)}, f32[264,128]{1,0:T(8,128)S(1)}, u32[]{:S(2)}, u32[]{:S(2)}) %collective-permute-start.16) | collective-permute-done | bytes 135200 | tf_op jit(solution)/shard_map/ppermute | solution.py:263
  54.3 0.7 %shard_map.59 = f32[32,1024]{1,0:T(8,128)} custom-call(f32[32,1024]{1,0:T(8,128)S(1)} %get-tuple-element.35.refs_0_.old, f32[264,128]{1,0:T(8,128)S(1)} %add_add_fusion.1.total, f32[264,128]{1,0:T(8,128)S(1)} %collective-permute-done.16.more), custom_call_target="tpu_custom_call" | custom-call | tf_op jit(solution)/shard_map/pallas_call | solution.py:250
  (1 shorter events, 0.0 us)
Async XLA Ops:
  0.6 14.4 %collective-permute-start.2 = (f32[32,1024]{1,0:T(8,128)}, f32[32,1024]{1,0:T(8,128)S(1)}, u32[]{:S(2)}, u32[]{:S(2)}) collective-permute-start(f32[32,1024]{1,0:T(8,128)} %atoms.1), channel_id=1, source_target_pairs={{0,4},{2,6},{4,0},{6,2},{8,12},{10,14},{12,8},{14,10},{1,5},{3,7},... | collective-permute-start | bytes 393224 | tf_op jit(solution)/shard_map/ppermute | solution.py:263
  3.7 11.5 %collective-permute-start.1 = (f32[32,1024]{1,0:T(8,128)}, f32[32,1024]{1,0:T(8,128)S(1)}, u32[]{:S(2)}, u32[]{:S(2)}) collective-permute-start(f32[32,1024]{1,0:T(8,128)} %atoms.1), channel_id=1, source_target_pairs={{0,2},{2,0},{4,6},{6,4},{8,10},{10,8},{12,14},{14,12},{1,3},{3,1},... | collective-permute-start | bytes 393224 | tf_op jit(solution)/shard_map/ppermute | solution.py:263
  5.2 8.7 %collective-permute-start.4 = (f32[32,1024]{1,0:T(8,128)}, f32[32,1024]{1,0:T(8,128)S(1)}, u32[]{:S(2)}, u32[]{:S(2)}) collective-permute-start(f32[32,1024]{1,0:T(8,128)} %atoms.1), channel_id=1, source_target_pairs={{0,8},{2,10},{4,12},{6,14},{8,0},{10,2},{12,4},{14,6},{1,9},{3,11}... | collective-permute-start | bytes 393224 | tf_op jit(solution)/shard_map/ppermute | solution.py:263
  7.8 9.6 %collective-permute-start.3 = (f32[32,1024]{1,0:T(8,128)}, f32[32,1024]{1,0:T(8,128)S(1)}, u32[]{:S(2)}, u32[]{:S(2)}) collective-permute-start(f32[32,1024]{1,0:T(8,128)} %atoms.1), channel_id=1, source_target_pairs={{0,6},{2,4},{4,2},{6,0},{8,14},{10,12},{12,10},{14,8},{1,7},{3,5},... | collective-permute-start | bytes 393224 | tf_op jit(solution)/shard_map/ppermute | solution.py:263
  8.2 9.5 %collective-permute-start = (f32[128,2048]{1,0:T(8,128)}, f32[128,2048]{1,0:T(8,128)S(1)}, u32[]{:S(2)}, u32[]{:S(2)}) collective-permute-start(f32[128,2048]{1,0:T(8,128)} %hown.1), channel_id=1, source_target_pairs={{0,1},{1,0},{2,3},{3,2},{4,5},{5,4},{6,7},{7,6},{8,9},{9,8},{10,11... | collective-permute-start | bytes 3145736 | tf_op jit(solution)/shard_map/ppermute | solution.py:267
  8.2 1.2 %copy-start = (f32[128,2048]{1,0:T(8,128)S(1)}, f32[128,2048]{1,0:T(8,128)}, u32[]{:S(2)}) copy-start(f32[128,2048]{1,0:T(8,128)} %hown.1) | copy-start | bytes 3145732
  9.4 0.9 %copy-start.1 = (f32[32,1024]{1,0:T(8,128)S(1)}, f32[32,1024]{1,0:T(8,128)}, u32[]{:S(2)}) copy-start(f32[32,1024]{1,0:T(8,128)} %atoms.1) | copy-start | bytes 393220
  13.9 6.0 %collective-permute-start.7 = (f32[32,1024]{1,0:T(8,128)S(1)}, f32[32,1024]{1,0:T(8,128)S(1)}, u32[]{:S(2)}, u32[]{:S(2)}) collective-permute-start(f32[32,1024]{1,0:T(8,128)S(1)} %collective-permute-done.4.refs_4_), channel_id=1, source_target_pairs={{0,6},{2,4},{4,2},{6,0},{8,14},{10,12},{12,10},{14,8},{1,7},{3,5},... | collective-permute-start | bytes 393224 | tf_op jit(solution)/shard_map/ppermute | solution.py:263
  15.1 5.2 %collective-permute-start.6 = (f32[32,1024]{1,0:T(8,128)S(1)}, f32[32,1024]{1,0:T(8,128)S(1)}, u32[]{:S(2)}, u32[]{:S(2)}) collective-permute-start(f32[32,1024]{1,0:T(8,128)S(1)} %collective-permute-done.4.refs_4_), channel_id=1, source_target_pairs={{0,4},{2,6},{4,0},{6,2},{8,12},{10,14},{12,8},{14,10},{1,5},{3,7},... | collective-permute-start | bytes 393224 | tf_op jit(solution)/shard_map/ppermute | solution.py:263
  15.2 6.0 %collective-permute-start.5 = (f32[32,1024]{1,0:T(8,128)S(1)}, f32[32,1024]{1,0:T(8,128)S(1)}, u32[]{:S(2)}, u32[]{:S(2)}) collective-permute-start(f32[32,1024]{1,0:T(8,128)S(1)} %collective-permute-done.4.refs_4_), channel_id=1, source_target_pairs={{0,2},{2,0},{4,6},{6,4},{8,10},{10,8},{12,14},{14,12},{1,3},{3,1},... | collective-permute-start | bytes 393224 | tf_op jit(solution)/shard_map/ppermute | solution.py:263
  18.0 3.2 %slice-start = ((s8[8388608]{0:T(1024)(128)(4,1)}), s8[4194304]{0:T(1024)(128)(4,1)S(1)}, s32[]{:S(2)}) async-start(s8[8388608]{0:T(1024)(128)(4,1)} %bitcast), calls=%async_computation | async-start | bytes 8388608
  18.0 3.5 %slice-start.1 = ((s8[8388608]{0:T(1024)(128)(4,1)}), s8[4194304]{0:T(1024)(128)(4,1)S(1)}, s32[]{:S(2)}) async-start(s8[8388608]{0:T(1024)(128)(4,1)} %bitcast), calls=%async_computation.1 | async-start | bytes 8388608
  25.0 3.6 %collective-permute-start.8 = (f32[264,1024]{1,0:T(8,128)S(1)}, f32[264,1024]{1,0:T(8,128)S(1)}, u32[]{:S(2)}, u32[]{:S(2)}) collective-permute-start(f32[264,1024]{1,0:T(8,128)S(1)} %get-tuple-element.39.mine.nown), channel_id=1, source_target_pairs={{0,1},{1,0},{2,3},{3,2},{4,5},{5,4},{6,7},{7,6},{8,9},{9,8},{10,11... | collective-permute-start | bytes 3244040 | tf_op jit(solution)/shard_map/ppermute | solution.py:267
  28.0 3.3 %collective-permute-start.9 = (f32[256,1024]{1,0:T(8,128)S(1)}, f32[256,1024]{1,0:T(8,128)S(1)}, u32[]{:S(2)}, u32[]{:S(2)}) collective-permute-start(f32[256,1024]{1,0:T(8,128)S(1)} %shard_map.55.nown), channel_id=1, source_target_pairs={{0,1},{1,0},{2,3},{3,2},{4,5},{5,4},{6,7},{7,6},{8,9},{9,8},{10,11... | collective-permute-start | bytes 3145736 | tf_op jit(solution)/shard_map/ppermute | solution.py:267
  35.4 7.4 %collective-permute-start.13 = (f32[264,128]{1,0:T(8,128)S(1)}, f32[264,128]{1,0:T(8,128)S(1)}, u32[]{:S(2)}, u32[]{:S(2)}) collective-permute-start(f32[264,128]{1,0:T(8,128)S(1)} %get-tuple-element.57), channel_id=1, source_target_pairs={{0,6},{2,4},{4,2},{6,0},{8,14},{10,12},{12,10},{14,8},{1,7},{3,5},... | collective-permute-start | bytes 405512 | tf_op jit(solution)/shard_map/ppermute | solution.py:263
  36.9 8.4 %collective-permute-start.14 = (f32[264,128]{1,0:T(8,128)S(1)}, f32[264,128]{1,0:T(8,128)S(1)}, u32[]{:S(2)}, u32[]{:S(2)}) collective-permute-start(f32[264,128]{1,0:T(8,128)S(1)} %get-tuple-element.58), channel_id=1, source_target_pairs={{0,4},{2,6},{4,0},{6,2},{8,12},{10,14},{12,8},{14,10},{1,5},{3,7},... | collective-permute-start | bytes 405512 | tf_op jit(solution)/shard_map/ppermute | solution.py:263
  37.9 9.3 %collective-permute-start.15 = (f32[264,128]{1,0:T(8,128)S(1)}, f32[264,128]{1,0:T(8,128)S(1)}, u32[]{:S(2)}, u32[]{:S(2)}) collective-permute-start(f32[264,128]{1,0:T(8,128)S(1)} %get-tuple-element.59), channel_id=1, source_target_pairs={{0,2},{2,0},{4,6},{6,4},{8,10},{10,8},{12,14},{14,12},{1,3},{3,1},... | collective-permute-start | bytes 405512 | tf_op jit(solution)/shard_map/ppermute | solution.py:263
  40.3 9.4 %collective-permute-start.10 = (f32[264,128]{1,0:T(8,128)S(1)}, f32[264,128]{1,0:T(8,128)S(1)}, u32[]{:S(2)}, u32[]{:S(2)}) collective-permute-start(f32[264,128]{1,0:T(8,128)S(1)} %get-tuple-element.53), channel_id=1, source_target_pairs={{0,6},{2,4},{4,2},{6,0},{8,14},{10,12},{12,10},{14,8},{1,7},{3,5},... | collective-permute-start | bytes 405512 | tf_op jit(solution)/shard_map/ppermute | solution.py:263
  41.7 8.6 %collective-permute-start.11 = (f32[264,128]{1,0:T(8,128)S(1)}, f32[264,128]{1,0:T(8,128)S(1)}, u32[]{:S(2)}, u32[]{:S(2)}) collective-permute-start(f32[264,128]{1,0:T(8,128)S(1)} %get-tuple-element.54), channel_id=1, source_target_pairs={{0,4},{2,6},{4,0},{6,2},{8,12},{10,14},{12,8},{14,10},{1,5},{3,7},... | collective-permute-start | bytes 405512 | tf_op jit(solution)/shard_map/ppermute | solution.py:263
  42.9 7.8 %collective-permute-start.12 = (f32[264,128]{1,0:T(8,128)S(1)}, f32[264,128]{1,0:T(8,128)S(1)}, u32[]{:S(2)}, u32[]{:S(2)}) collective-permute-start(f32[264,128]{1,0:T(8,128)S(1)} %get-tuple-element.55), channel_id=1, source_target_pairs={{0,2},{2,0},{4,6},{6,4},{8,10},{10,8},{12,14},{14,12},{1,3},{3,1},... | collective-permute-start | bytes 405512 | tf_op jit(solution)/shard_map/ppermute | solution.py:263
  47.3 7.0 %collective-permute-start.16 = (f32[264,128]{1,0:T(8,128)S(1)}, f32[264,128]{1,0:T(8,128)S(1)}, u32[]{:S(2)}, u32[]{:S(2)}) collective-permute-start(f32[264,128]{1,0:T(8,128)S(1)} %add_add_fusion), channel_id=1, source_target_pairs={{0,12},{2,14},{4,8},{6,10},{8,4},{10,6},{12,0},{14,2},{1,13},{3,15... | collective-permute-start | bytes 405512 | tf_op jit(solution)/shard_map/ppermute | solution.py:263

commit v6 on v5

--- a/solution.py
+++ b/solution.py
@@ -349,11 +349,11 @@
     home = call(third_kernel, carried + before, [block] * n_out, scratch=[((half, bins), f32)], flops=10**9)
     if cube:
         total = away[REDUCE_CROSS & 3]
-        for s in (3, 2, 1):
+        for s in (2, 1, 3):
             total = total + hop(away[s ^ (REDUCE_CROSS & 3)], s)
         more = hop(total, REDUCE_CROSS)
         total = home[0]
-        for s in (3, 2, 1):
+        for s in (1, 3, 2):
             total = total + hop(home[s], s)
         (new,) = call(last_kernel, [kept, total, more], [((rows, bins), f32)], mib=16)
         return fresh, new

time: 55.2 us -> 54.3 us (0.984)
  waiting for transfers between devices: 13.2 us -> 12.3 us
    ppermute x14, waiting for transfers between devices: 13.2 us -> 12.3 us  [hop(): return lax.ppermute(x, 'frames', [(i, i ^ step) for i in range(8)])]
  transfers between devices with their start and end apart: 17 -> 17, of which waited for: 10 -> 8; matrix products, arithmetic and copies ran while one was open for 0% -> 0% of each run, Pallas kernels for 17% -> 17%
where the time goes in v6:
time: 54.3 us; the launch traced here: 54.2 us
  starting transfers between devices  21.2 us (39%)
  Pallas kernels  17.5 us (32%)
  waiting for transfers between devices  12.3 us (23%)
  local copies, waits for them, and re-layouts  2.36 us (4%)
  between operations  0.73 us (1%)
    ppermute x14, starting transfers between devices, hop(): return lax.ppermute(x, 'frames', [(i, i ^ step) for i in range(8)])  20.7 us
    pallas_call x10, Pallas kernels, call(): pl.pallas_call(kernel, in_specs=list(in_specs) + [WHOLE] * (len(ins) - le...  17.5 us
    ppermute x14, waiting for transfers between devices, hop(): return lax.ppermute(x, 'frames', [(i, i ^ step) for i in range(8)])  12.3 us
    unnamed x8, local copies, waits for them, and re-layouts  2.36 us
  transfers between devices with their start and end apart: 17, of which 8 were waited for; matrix products, arithmetic and copies ran while one was open for 0% of the time, Pallas kernels for 17%

profile of v6, /device:TPU:0, one launch (start us, length us, event | category | flops | bytes accessed | tf_op | source)
XLA Modules:
  0.0 54.2 jit_solution(7824053121132648459)
XLA Ops:
  0.6 3.1 %collective-permute-start.2 = (f32[32,1024]{1,0:T(8,128)}, f32[32,1024]{1,0:T(8,128)S(1)}, u32[]{:S(2)}, u32[]{:S(2)}) collective-permute-start(f32[32,1024]{1,0:T(8,128)} %atoms.1), channel_id=1, source_target_pairs={{0,4},{2,6},{4,0},{6,2},{8,12},{10,14},{12,8},{14,10},{1,5},{3,7},... | collective-permute-start | bytes 393224 | tf_op jit(solution)/shard_map/ppermute | solution.py:263
  3.7 1.5 %collective-permute-start.1 = (f32[32,1024]{1,0:T(8,128)}, f32[32,1024]{1,0:T(8,128)S(1)}, u32[]{:S(2)}, u32[]{:S(2)}) collective-permute-start(f32[32,1024]{1,0:T(8,128)} %atoms.1), channel_id=1, source_target_pairs={{0,2},{2,0},{4,6},{6,4},{8,10},{10,8},{12,14},{14,12},{1,3},{3,1},... | collective-permute-start | bytes 393224 | tf_op jit(solution)/shard_map/ppermute | solution.py:263
  5.2 2.6 %collective-permute-start.4 = (f32[32,1024]{1,0:T(8,128)}, f32[32,1024]{1,0:T(8,128)S(1)}, u32[]{:S(2)}, u32[]{:S(2)}) collective-permute-start(f32[32,1024]{1,0:T(8,128)} %atoms.1), channel_id=1, source_target_pairs={{0,8},{2,10},{4,12},{6,14},{8,0},{10,2},{12,4},{14,6},{1,9},{3,11}... | collective-permute-start | bytes 393224 | tf_op jit(solution)/shard_map/ppermute | solution.py:263
  7.8 0.4 collective-permute-start.3
  8.2 0.0 collective-permute-start
  8.2 0.0 copy-start
  8.2 1.2 %copy-done = f32[128,2048]{1,0:T(8,128)S(1)} copy-done((f32[128,2048]{1,0:T(8,128)S(1)}, f32[128,2048]{1,0:T(8,128)}, u32[]{:S(2)}) %copy-start) | copy-done | bytes 1048600
  9.4 0.0 copy-start.1
  9.5 0.9 %copy-done.1 = f32[32,1024]{1,0:T(8,128)S(1)} copy-done((f32[32,1024]{1,0:T(8,128)S(1)}, f32[32,1024]{1,0:T(8,128)}, u32[]{:S(2)}) %copy-start.1) | copy-done | bytes 131096
  10.4 0.2 shard_map.50
  10.6 3.3 %collective-permute-done.4.refs_4_ = f32[32,1024]{1,0:T(8,128)S(1)} collective-permute-done((f32[32,1024]{1,0:T(8,128)}, f32[32,1024]{1,0:T(8,128)S(1)}, u32[]{:S(2)}, u32[]{:S(2)}) %collective-permute-start.4) | collective-permute-done | bytes 131104 | tf_op jit(solution)/shard_map/ppermute | solution.py:263
  13.9 1.1 %collective-permute-start.7 = (f32[32,1024]{1,0:T(8,128)S(1)}, f32[32,1024]{1,0:T(8,128)S(1)}, u32[]{:S(2)}, u32[]{:S(2)}) collective-permute-start(f32[32,1024]{1,0:T(8,128)S(1)} %collective-permute-done.4.refs_4_), channel_id=1, source_target_pairs={{0,6},{2,4},{4,2},{6,0},{8,14},{10,12},{12,10},{14,8},{1,7},{3,5},... | collective-permute-start | bytes 393224 | tf_op jit(solution)/shard_map/ppermute | solution.py:263
  15.1 0.0 collective-permute-done.2.refs_2_
  15.1 0.1 collective-permute-start.6
  15.2 0.0 collective-permute-done.1.refs_1_
  15.2 2.2 %collective-permute-start.5 = (f32[32,1024]{1,0:T(8,128)S(1)}, f32[32,1024]{1,0:T(8,128)S(1)}, u32[]{:S(2)}, u32[]{:S(2)}) collective-permute-start(f32[32,1024]{1,0:T(8,128)S(1)} %collective-permute-done.4.refs_4_), channel_id=1, source_target_pairs={{0,2},{2,0},{4,6},{6,4},{8,10},{10,8},{12,14},{14,12},{1,3},{3,1},... | collective-permute-start | bytes 393224 | tf_op jit(solution)/shard_map/ppermute | solution.py:263
  17.4 0.0 collective-permute-done.3.refs_3_
  17.4 0.3 shard_map.52
  17.7 0.0 collective-permute-done.hoth
  17.7 0.2 shard_map.51
  18.0 0.0 slice-start
  18.0 0.0 slice-start.1
  18.0 1.3 %shard_map.53.refs_0_ = f32[1024,2048]{1,0:T(8,128)S(1)} custom-call(bf16[1024,256]{1,0:T(8,128)(2,1)S(1)} %get-tuple-element.36.wt.refs_2_.refs_3_.refs_0_, bf16[512,2048]{1,0:T(8,128)(2,1)S(1)} %get-tuple-element.34.h2), custom_call_target="tpu_custom_call" | custom-call | flops 10000000000 | tf_op jit(solution)/shard_map/pallas_call | solution.py:250
  19.3 0.7 %collective-permute-done.7.refs_7_ = f32[32,1024]{1,0:T(8,128)S(1)} collective-permute-done((f32[32,1024]{1,0:T(8,128)S(1)}, f32[32,1024]{1,0:T(8,128)S(1)}, u32[]{:S(2)}, u32[]{:S(2)}) %collective-permute-start.7) | collective-permute-done | bytes 131104 | tf_op jit(solution)/shard_map/ppermute | solution.py:263
  19.9 0.4 collective-permute-done.6.refs_6_
  20.3 0.9 %collective-permute-done.5.refs_5_ = f32[32,1024]{1,0:T(8,128)S(1)} collective-permute-done((f32[32,1024]{1,0:T(8,128)S(1)}, f32[32,1024]{1,0:T(8,128)S(1)}, u32[]{:S(2)}, u32[]{:S(2)}) %collective-permute-start.5) | collective-permute-done | bytes 131104 | tf_op jit(solution)/shard_map/ppermute | solution.py:263
  21.2 0.0 slice-done
  21.2 0.2 slice-done.1
  21.5 3.5 %shard_map.54 = (f32[264,1024]{1,0:T(8,128)S(1)}, bf16[256,1024]{1,0:T(8,128)(2,1)S(1)}, bf16[1024,256]{1,0:T(8,128)(2,1)S(1)}, f32[128,128]{1,0:T(8,128)}) custom-call(f32[1024,2048]{1,0:T(8,128)S(1)} %bitcast.1, bf16[512,2048]{1,0:T(8,128)(2,1)S(1)} %get-tuple-element.34.h2, f32[1024,2048]{1,0:T(8,128)S(1)} %shard_map.53.refs_0_, ...), custom_call_target="tpu_custom_call" | custom-call | tf_op jit(solution)/shard_map/pallas_call | solution.py:250
  25.0 0.0 collective-permute-start.8
  25.0 3.0 %shard_map.55.nown = f32[256,1024]{1,0:T(8,128)S(1)} custom-call(f32[1024,2048]{1,0:T(8,128)S(1)} %bitcast.1, bf16[512,2048]{1,0:T(8,128)(2,1)S(1)} %get-tuple-element.34.h2, f32[1024,2048]{1,0:T(8,128)S(1)} %shard_map.53.refs_0_, bf16[256,1024]{1,0:T(8,128)(2,1)S(1)} %get-tuple-element.37.refs_1_, bf16[256,1024]{1,0:T(8,128)(2,1)S(1)} %get-tuple-element.40.refs_2_, ...), custom_call_target="tpu_custom_call" | custom-call | tf_op jit(solution)/shard_map/pallas_call | solution.py:250
  28.0 0.6 %collective-permute-start.9 = (f32[256,1024]{1,0:T(8,128)S(1)}, f32[256,1024]{1,0:T(8,128)S(1)}, u32[]{:S(2)}, u32[]{:S(2)}) collective-permute-start(f32[256,1024]{1,0:T(8,128)S(1)} %shard_map.55.nown), channel_id=1, source_target_pairs={{0,1},{1,0},{2,3},{3,2},{4,5},{5,4},{6,7},{7,6},{8,9},{9,8},{10,11... | collective-permute-start | bytes 3145736 | tf_op jit(solution)/shard_map/ppermute | solution.py:267
  28.6 0.0 collective-permute-done.8.theirs.noth
  28.6 2.8 %shard_map.56 = (f32[128,2048]{1,0:T(8,128)}, f32[256,1024]{1,0:T(8,128)S(1)}, f32[256,128]{1,0:T(8,128)S(1)}, bf16[1024,1024]{1,0:T(8,128)(2,1)S(1)}, bf16[512,1024]{1,0:T(8,128)(2,1)S(1)}) custom-call(f32[1024,2048]{1,0:T(8,128)S(1)} %bitcast.1, f32[256,2048]{1,0:T(8,128)S(1)} %get-tuple-element.33.h, f32[264,1024]{1,0:T(8,128)S(1)} %get-tuple-element.39.mine.nown, ...), custom_call_target="tpu_custom_call" | custom-call | tf_op jit(solution)/shard_map/pallas_call | solution.py:250
  31.4 0.0 collective-permute-done.9.noth
  31.4 4.1 %shard_map.57 = (f32[128,2048]{1,0:T(8,128)}, f32[128,1024]{1,0:T(8,128)S(1)}, f32[256,128]{1,0:T(8,128)S(1)}, bf16[1024,1024]{1,0:T(8,128)(2,1)S(1)}, bf16[512,...) custom-call(f32[1024,2048]{1,0:T(8,128)S(1)} %bitcast.1, ...), custom_call_target="tpu_custom_call", output_to_operand_aliasing={{0}: (12, {})} | custom-call | tf_op jit(solution)/shard_map/pallas_call | solution.py:250
  35.4 0.7 %collective-permute-start.13 = (f32[264,128]{1,0:T(8,128)S(1)}, f32[264,128]{1,0:T(8,128)S(1)}, u32[]{:S(2)}, u32[]{:S(2)}) collective-permute-start(f32[264,128]{1,0:T(8,128)S(1)} %get-tuple-element.57), channel_id=1, source_target_pairs={{0,4},{2,6},{4,0},{6,2},{8,12},{10,14},{12,8},{14,10},{1,5},{3,7},... | collective-permute-start | bytes 405512 | tf_op jit(solution)/shard_map/ppermute | solution.py:263
  36.1 1.3 %collective-permute-start.14 = (f32[264,128]{1,0:T(8,128)S(1)}, f32[264,128]{1,0:T(8,128)S(1)}, u32[]{:S(2)}, u32[]{:S(2)}) collective-permute-start(f32[264,128]{1,0:T(8,128)S(1)} %get-tuple-element.58), channel_id=1, source_target_pairs={{0,2},{2,0},{4,6},{6,4},{8,10},{10,8},{12,14},{14,12},{1,3},{3,1},... | collective-permute-start | bytes 405512 | tf_op jit(solution)/shard_map/ppermute | solution.py:263
  37.4 1.6 %collective-permute-start.15 = (f32[264,128]{1,0:T(8,128)S(1)}, f32[264,128]{1,0:T(8,128)S(1)}, u32[]{:S(2)}, u32[]{:S(2)}) collective-permute-start(f32[264,128]{1,0:T(8,128)S(1)} %get-tuple-element.59), channel_id=1, source_target_pairs={{0,6},{2,4},{4,2},{6,0},{8,14},{10,12},{12,10},{14,8},{1,7},{3,5},... | collective-permute-start | bytes 405512 | tf_op jit(solution)/shard_map/ppermute | solution.py:263
  39.0 1.3 %shard_map.58 = (f32[264,128]{1,0:T(8,128)S(1)}, f32[264,128]{1,0:T(8,128)S(1)}, f32[264,128]{1,0:T(8,128)S(1)}, f32[264,128]{1,0:T(8,128)S(1)}) custom-call(f32[128,1024]{1,0:T(8,128)S(1)} %get-tuple-element.48.acc, f32[256,128]{1,0:T(8,128)S(1)} %get-tuple-element.49.row_mass, bf16[1024,1024]{1,0:T(8,128)(2,1)S(1)} %get-tuple-element.50.rhi_a, ...), custom_call_target="tpu_custom_call" | custom-call | flops 1000000000 | tf_op jit(solution)/shard_map/pallas_call | solution.py:250
  40.3 1.0 %collective-permute-start.10 = (f32[264,128]{1,0:T(8,128)S(1)}, f32[264,128]{1,0:T(8,128)S(1)}, u32[]{:S(2)}, u32[]{:S(2)}) collective-permute-start(f32[264,128]{1,0:T(8,128)S(1)} %get-tuple-element.53), channel_id=1, source_target_pairs={{0,2},{2,0},{4,6},{6,4},{8,10},{10,8},{12,14},{14,12},{1,3},{3,1},... | collective-permute-start | bytes 405512 | tf_op jit(solution)/shard_map/ppermute | solution.py:263
  41.3 1.1 %collective-permute-start.11 = (f32[264,128]{1,0:T(8,128)S(1)}, f32[264,128]{1,0:T(8,128)S(1)}, u32[]{:S(2)}, u32[]{:S(2)}) collective-permute-start(f32[264,128]{1,0:T(8,128)S(1)} %get-tuple-element.54), channel_id=1, source_target_pairs={{0,6},{2,4},{4,2},{6,0},{8,14},{10,12},{12,10},{14,8},{1,7},{3,5},... | collective-permute-start | bytes 405512 | tf_op jit(solution)/shard_map/ppermute | solution.py:263
  42.5 0.0 collective-permute-done.13
  42.5 1.4 %collective-permute-start.12 = (f32[264,128]{1,0:T(8,128)S(1)}, f32[264,128]{1,0:T(8,128)S(1)}, u32[]{:S(2)}, u32[]{:S(2)}) collective-permute-start(f32[264,128]{1,0:T(8,128)S(1)} %get-tuple-element.55), channel_id=1, source_target_pairs={{0,4},{2,6},{4,0},{6,2},{8,12},{10,14},{12,8},{14,10},{1,5},{3,7},... | collective-permute-start | bytes 405512 | tf_op jit(solution)/shard_map/ppermute | solution.py:263
  43.9 0.0 collective-permute-done.14
  43.9 1.1 %collective-permute-done.15 = f32[264,128]{1,0:T(8,128)S(1)} collective-permute-done((f32[264,128]{1,0:T(8,128)S(1)}, f32[264,128]{1,0:T(8,128)S(1)}, u32[]{:S(2)}, u32[]{:S(2)}) %collective-permute-start.15) | collective-permute-done | bytes 135200 | tf_op jit(solution)/shard_map/ppermute | solution.py:263
  45.0 2.5 %collective-permute-start.16 = (f32[264,128]{1,0:T(8,128)S(1)}, f32[264,128]{1,0:T(8,128)S(1)}, u32[]{:S(2)}, u32[]{:S(2)}) collective-permute-start(f32[264,128]{1,0:T(8,128)S(1)} %add_add_fusion), channel_id=1, source_target_pairs={{0,12},{2,14},{4,8},{6,10},{8,4},{10,6},{12,0},{14,2},{1,13},{3,15... | collective-permute-start | bytes 405512 | tf_op jit(solution)/shard_map/ppermute | solution.py:263
  47.5 2.6 %collective-permute-done.10 = f32[264,128]{1,0:T(8,128)S(1)} collective-permute-done((f32[264,128]{1,0:T(8,128)S(1)}, f32[264,128]{1,0:T(8,128)S(1)}, u32[]{:S(2)}, u32[]{:S(2)}) %collective-permute-start.10) | collective-permute-done | bytes 135200 | tf_op jit(solution)/shard_map/ppermute | solution.py:263
  50.1 0.0 collective-permute-done.11
  50.1 0.4 collective-permute-done.12
  50.5 2.9 %collective-permute-done.16.more = f32[264,128]{1,0:T(8,128)S(1)} collective-permute-done((f32[264,128]{1,0:T(8,128)S(1)}, f32[264,128]{1,0:T(8,128)S(1)}, u32[]{:S(2)}, u32[]{:S(2)}) %collective-permute-start.16) | collective-permute-done | bytes 135200 | tf_op jit(solution)/shard_map/ppermute | solution.py:263
  53.4 0.7 %shard_map.59 = f32[32,1024]{1,0:T(8,128)} custom-call(f32[32,1024]{1,0:T(8,128)S(1)} %get-tuple-element.35.refs_0_.old, f32[264,128]{1,0:T(8,128)S(1)} %add_add_fusion.1.total, f32[264,128]{1,0:T(8,128)S(1)} %collective-permute-done.16.more), custom_call_target="tpu_custom_call" | custom-call | tf_op jit(solution)/shard_map/pallas_call | solution.py:250
  (3 shorter events, 0.1 us)
Async XLA Ops:
  0.6 14.4 %collective-permute-start.2 = (f32[32,1024]{1,0:T(8,128)}, f32[32,1024]{1,0:T(8,128)S(1)}, u32[]{:S(2)}, u32[]{:S(2)}) collective-permute-start(f32[32,1024]{1,0:T(8,128)} %atoms.1), channel_id=1, source_target_pairs={{0,4},{2,6},{4,0},{6,2},{8,12},{10,14},{12,8},{14,10},{1,5},{3,7},... | collective-permute-start | bytes 393224 | tf_op jit(solution)/shard_map/ppermute | solution.py:263
  3.7 11.5 %collective-permute-start.1 = (f32[32,1024]{1,0:T(8,128)}, f32[32,1024]{1,0:T(8,128)S(1)}, u32[]{:S(2)}, u32[]{:S(2)}) collective-permute-start(f32[32,1024]{1,0:T(8,128)} %atoms.1), channel_id=1, source_target_pairs={{0,2},{2,0},{4,6},{6,4},{8,10},{10,8},{12,14},{14,12},{1,3},{3,1},... | collective-permute-start | bytes 393224 | tf_op jit(solution)/shard_map/ppermute | solution.py:263
  5.2 8.7 %collective-permute-start.4 = (f32[32,1024]{1,0:T(8,128)}, f32[32,1024]{1,0:T(8,128)S(1)}, u32[]{:S(2)}, u32[]{:S(2)}) collective-permute-start(f32[32,1024]{1,0:T(8,128)} %atoms.1), channel_id=1, source_target_pairs={{0,8},{2,10},{4,12},{6,14},{8,0},{10,2},{12,4},{14,6},{1,9},{3,11}... | collective-permute-start | bytes 393224 | tf_op jit(solution)/shard_map/ppermute | solution.py:263
  7.8 9.6 %collective-permute-start.3 = (f32[32,1024]{1,0:T(8,128)}, f32[32,1024]{1,0:T(8,128)S(1)}, u32[]{:S(2)}, u32[]{:S(2)}) collective-permute-start(f32[32,1024]{1,0:T(8,128)} %atoms.1), channel_id=1, source_target_pairs={{0,6},{2,4},{4,2},{6,0},{8,14},{10,12},{12,10},{14,8},{1,7},{3,5},... | collective-permute-start | bytes 393224 | tf_op jit(solution)/shard_map/ppermute | solution.py:263
  8.2 9.5 %collective-permute-start = (f32[128,2048]{1,0:T(8,128)}, f32[128,2048]{1,0:T(8,128)S(1)}, u32[]{:S(2)}, u32[]{:S(2)}) collective-permute-start(f32[128,2048]{1,0:T(8,128)} %hown.1), channel_id=1, source_target_pairs={{0,1},{1,0},{2,3},{3,2},{4,5},{5,4},{6,7},{7,6},{8,9},{9,8},{10,11... | collective-permute-start | bytes 3145736 | tf_op jit(solution)/shard_map/ppermute | solution.py:267
  8.2 1.2 %copy-start = (f32[128,2048]{1,0:T(8,128)S(1)}, f32[128,2048]{1,0:T(8,128)}, u32[]{:S(2)}) copy-start(f32[128,2048]{1,0:T(8,128)} %hown.1) | copy-start | bytes 3145732
  9.4 0.9 %copy-start.1 = (f32[32,1024]{1,0:T(8,128)S(1)}, f32[32,1024]{1,0:T(8,128)}, u32[]{:S(2)}) copy-start(f32[32,1024]{1,0:T(8,128)} %atoms.1) | copy-start | bytes 393220
  13.9 6.0 %collective-permute-start.7 = (f32[32,1024]{1,0:T(8,128)S(1)}, f32[32,1024]{1,0:T(8,128)S(1)}, u32[]{:S(2)}, u32[]{:S(2)}) collective-permute-start(f32[32,1024]{1,0:T(8,128)S(1)} %collective-permute-done.4.refs_4_), channel_id=1, source_target_pairs={{0,6},{2,4},{4,2},{6,0},{8,14},{10,12},{12,10},{14,8},{1,7},{3,5},... | collective-permute-start | bytes 393224 | tf_op jit(solution)/shard_map/ppermute | solution.py:263
  15.1 5.2 %collective-permute-start.6 = (f32[32,1024]{1,0:T(8,128)S(1)}, f32[32,1024]{1,0:T(8,128)S(1)}, u32[]{:S(2)}, u32[]{:S(2)}) collective-permute-start(f32[32,1024]{1,0:T(8,128)S(1)} %collective-permute-done.4.refs_4_), channel_id=1, source_target_pairs={{0,4},{2,6},{4,0},{6,2},{8,12},{10,14},{12,8},{14,10},{1,5},{3,7},... | collective-permute-start | bytes 393224 | tf_op jit(solution)/shard_map/ppermute | solution.py:263
  15.2 6.0 %collective-permute-start.5 = (f32[32,1024]{1,0:T(8,128)S(1)}, f32[32,1024]{1,0:T(8,128)S(1)}, u32[]{:S(2)}, u32[]{:S(2)}) collective-permute-start(f32[32,1024]{1,0:T(8,128)S(1)} %collective-permute-done.4.refs_4_), channel_id=1, source_target_pairs={{0,2},{2,0},{4,6},{6,4},{8,10},{10,8},{12,14},{14,12},{1,3},{3,1},... | collective-permute-start | bytes 393224 | tf_op jit(solution)/shard_map/ppermute | solution.py:263
  18.0 3.2 %slice-start = ((s8[8388608]{0:T(1024)(128)(4,1)}), s8[4194304]{0:T(1024)(128)(4,1)S(1)}, s32[]{:S(2)}) async-start(s8[8388608]{0:T(1024)(128)(4,1)} %bitcast), calls=%async_computation | async-start | bytes 8388608
  18.0 3.5 %slice-start.1 = ((s8[8388608]{0:T(1024)(128)(4,1)}), s8[4194304]{0:T(1024)(128)(4,1)S(1)}, s32[]{:S(2)}) async-start(s8[8388608]{0:T(1024)(128)(4,1)} %bitcast), calls=%async_computation.1 | async-start | bytes 8388608
  25.0 3.6 %collective-permute-start.8 = (f32[264,1024]{1,0:T(8,128)S(1)}, f32[264,1024]{1,0:T(8,128)S(1)}, u32[]{:S(2)}, u32[]{:S(2)}) collective-permute-start(f32[264,1024]{1,0:T(8,128)S(1)} %get-tuple-element.39.mine.nown), channel_id=1, source_target_pairs={{0,1},{1,0},{2,3},{3,2},{4,5},{5,4},{6,7},{7,6},{8,9},{9,8},{10,11... | collective-permute-start | bytes 3244040 | tf_op jit(solution)/shard_map/ppermute | solution.py:267
  28.0 3.3 %collective-permute-start.9 = (f32[256,1024]{1,0:T(8,128)S(1)}, f32[256,1024]{1,0:T(8,128)S(1)}, u32[]{:S(2)}, u32[]{:S(2)}) collective-permute-start(f32[256,1024]{1,0:T(8,128)S(1)} %shard_map.55.nown), channel_id=1, source_target_pairs={{0,1},{1,0},{2,3},{3,2},{4,5},{5,4},{6,7},{7,6},{8,9},{9,8},{10,11... | collective-permute-start | bytes 3145736 | tf_op jit(solution)/shard_map/ppermute | solution.py:267
  35.4 7.0 %collective-permute-start.13 = (f32[264,128]{1,0:T(8,128)S(1)}, f32[264,128]{1,0:T(8,128)S(1)}, u32[]{:S(2)}, u32[]{:S(2)}) collective-permute-start(f32[264,128]{1,0:T(8,128)S(1)} %get-tuple-element.57), channel_id=1, source_target_pairs={{0,4},{2,6},{4,0},{6,2},{8,12},{10,14},{12,8},{14,10},{1,5},{3,7},... | collective-permute-start | bytes 405512 | tf_op jit(solution)/shard_map/ppermute | solution.py:263
  36.1 7.7 %collective-permute-start.14 = (f32[264,128]{1,0:T(8,128)S(1)}, f32[264,128]{1,0:T(8,128)S(1)}, u32[]{:S(2)}, u32[]{:S(2)}) collective-permute-start(f32[264,128]{1,0:T(8,128)S(1)} %get-tuple-element.58), channel_id=1, source_target_pairs={{0,2},{2,0},{4,6},{6,4},{8,10},{10,8},{12,14},{14,12},{1,3},{3,1},... | collective-permute-start | bytes 405512 | tf_op jit(solution)/shard_map/ppermute | solution.py:263
  37.4 7.5 %collective-permute-start.15 = (f32[264,128]{1,0:T(8,128)S(1)}, f32[264,128]{1,0:T(8,128)S(1)}, u32[]{:S(2)}, u32[]{:S(2)}) collective-permute-start(f32[264,128]{1,0:T(8,128)S(1)} %get-tuple-element.59), channel_id=1, source_target_pairs={{0,6},{2,4},{4,2},{6,0},{8,14},{10,12},{12,10},{14,8},{1,7},{3,5},... | collective-permute-start | bytes 405512 | tf_op jit(solution)/shard_map/ppermute | solution.py:263
  40.3 9.7 %collective-permute-start.10 = (f32[264,128]{1,0:T(8,128)S(1)}, f32[264,128]{1,0:T(8,128)S(1)}, u32[]{:S(2)}, u32[]{:S(2)}) collective-permute-start(f32[264,128]{1,0:T(8,128)S(1)} %get-tuple-element.53), channel_id=1, source_target_pairs={{0,2},{2,0},{4,6},{6,4},{8,10},{10,8},{12,14},{14,12},{1,3},{3,1},... | collective-permute-start | bytes 405512 | tf_op jit(solution)/shard_map/ppermute | solution.py:263
  41.3 8.7 %collective-permute-start.11 = (f32[264,128]{1,0:T(8,128)S(1)}, f32[264,128]{1,0:T(8,128)S(1)}, u32[]{:S(2)}, u32[]{:S(2)}) collective-permute-start(f32[264,128]{1,0:T(8,128)S(1)} %get-tuple-element.54), channel_id=1, source_target_pairs={{0,6},{2,4},{4,2},{6,0},{8,14},{10,12},{12,10},{14,8},{1,7},{3,5},... | collective-permute-start | bytes 405512 | tf_op jit(solution)/shard_map/ppermute | solution.py:263
  42.5 8.0 %collective-permute-start.12 = (f32[264,128]{1,0:T(8,128)S(1)}, f32[264,128]{1,0:T(8,128)S(1)}, u32[]{:S(2)}, u32[]{:S(2)}) collective-permute-start(f32[264,128]{1,0:T(8,128)S(1)} %get-tuple-element.55), channel_id=1, source_target_pairs={{0,4},{2,6},{4,0},{6,2},{8,12},{10,14},{12,8},{14,10},{1,5},{3,7},... | collective-permute-start | bytes 405512 | tf_op jit(solution)/shard_map/ppermute | solution.py:263
  45.0 8.4 %collective-permute-start.16 = (f32[264,128]{1,0:T(8,128)S(1)}, f32[264,128]{1,0:T(8,128)S(1)}, u32[]{:S(2)}, u32[]{:S(2)}) collective-permute-start(f32[264,128]{1,0:T(8,128)S(1)} %add_add_fusion), channel_id=1, source_target_pairs={{0,12},{2,14},{4,8},{6,10},{8,4},{10,6},{12,0},{14,2},{1,13},{3,15... | collective-permute-start | bytes 405512 | tf_op jit(solution)/shard_map/ppermute | solution.py:263

commit v7 on v6

--- a/solution.py
+++ b/solution.py
@@ -12,7 +12,7 @@
 HBM = pl.BlockSpec(memory_space=pl.ANY)
 GATHER_CROSS, REDUCE_CROSS = 4, 6
 PIECES = 2
-FC, NC = 256, 512
+FC, FIRST_FC, NC = 256, 128, 512
 
 
 def split(x):
@@ -127,8 +127,8 @@
         at, src = slice(n, n + NC), slice(start + n, start + n + NC)
         top = h2[atoms // 2 if near else 0 : atoms, src]
         h3 = jnp.concatenate([top, top, h2[atoms:, src]], axis=0)
-        for f in range(0, bins, FC):
-            rows = slice(f, f + FC)
+        for f in range(0, bins, FIRST_FC):
+            rows = slice(f, f + FIRST_FC)
             if raw and n == 0:
                 prepare(ws, *made, GATHER_CROSS & 3, rows)
             if near:
@@ -301,7 +301,7 @@
     )
     k = sum(w.shape[0] for w in near)
     w2, wt, mass = call(prepare_kernel, near, basis_outs(k), mib=16, flops=10**10)
-    model = call(near_kernel, [wt, h2], [((bins, frames), f32)], mib=16, flops=10**10) if cube else []
+    model = call(near_kernel, [wt, h2], [((bins, frames), f32)], mib=16, flops=10**9) if cube else []
     w2, wt, mass = [w2], [wt], [mass]
     numers = []
     for p in range(PIECES):

time: 54.3 us -> 54 us (level)
  no operation moved by 1% of the time
where the time goes in v7:
time: 54 us; the launch traced here: 53.8 us
  starting transfers between devices  21.2 us (39%)
  Pallas kernels  17.3 us (32%)
  waiting for transfers between devices  12.4 us (23%)
  local copies, waits for them, and re-layouts  2.19 us (4%)
  between operations  0.73 us (1%)
    ppermute x14, starting transfers between devices, hop(): return lax.ppermute(x, 'frames', [(i, i ^ step) for i in range(8)])  20.6 us
    pallas_call x10, Pallas kernels, call(): pl.pallas_call(kernel, in_specs=list(in_specs) + [WHOLE] * (len(ins) - le...  17.3 us
    ppermute x14, waiting for transfers between devices, hop(): return lax.ppermute(x, 'frames', [(i, i ^ step) for i in range(8)])  12.4 us
    unnamed x8, local copies, waits for them, and re-layouts  2.19 us
  transfers between devices with their start and end apart: 17, of which 8 were waited for; matrix products, arithmetic and copies ran while one was open for 0% of the time, Pallas kernels for 17%

profile of v7, /device:TPU:0, one launch (start us, length us, event | category | flops | bytes accessed | tf_op | source)
XLA Modules:
  0.0 53.8 jit_solution(17100294022130737760)
XLA Ops:
  0.6 3.1 %collective-permute-start.2 = (f32[32,1024]{1,0:T(8,128)}, f32[32,1024]{1,0:T(8,128)S(1)}, u32[]{:S(2)}, u32[]{:S(2)}) collective-permute-start(f32[32,1024]{1,0:T(8,128)} %atoms.1), channel_id=1, source_target_pairs={{0,4},{2,6},{4,0},{6,2},{8,12},{10,14},{12,8},{14,10},{1,5},{3,7},... | collective-permute-start | bytes 393224 | tf_op jit(solution)/shard_map/ppermute | solution.py:263
  3.7 1.5 %collective-permute-start.1 = (f32[32,1024]{1,0:T(8,128)}, f32[32,1024]{1,0:T(8,128)S(1)}, u32[]{:S(2)}, u32[]{:S(2)}) collective-permute-start(f32[32,1024]{1,0:T(8,128)} %atoms.1), channel_id=1, source_target_pairs={{0,2},{2,0},{4,6},{6,4},{8,10},{10,8},{12,14},{14,12},{1,3},{3,1},... | collective-permute-start | bytes 393224 | tf_op jit(solution)/shard_map/ppermute | solution.py:263
  5.2 2.6 %collective-permute-start.4 = (f32[32,1024]{1,0:T(8,128)}, f32[32,1024]{1,0:T(8,128)S(1)}, u32[]{:S(2)}, u32[]{:S(2)}) collective-permute-start(f32[32,1024]{1,0:T(8,128)} %atoms.1), channel_id=1, source_target_pairs={{0,8},{2,10},{4,12},{6,14},{8,0},{10,2},{12,4},{14,6},{1,9},{3,11}... | collective-permute-start | bytes 393224 | tf_op jit(solution)/shard_map/ppermute | solution.py:263
  7.8 0.4 collective-permute-start.3
  8.2 0.0 collective-permute-start
  8.2 0.0 copy-start
  8.2 1.2 %copy-done = f32[128,2048]{1,0:T(8,128)S(1)} copy-done((f32[128,2048]{1,0:T(8,128)S(1)}, f32[128,2048]{1,0:T(8,128)}, u32[]{:S(2)}) %copy-start) | copy-done | bytes 1048600
  9.4 0.0 copy-start.1
  9.5 0.9 %copy-done.1 = f32[32,1024]{1,0:T(8,128)S(1)} copy-done((f32[32,1024]{1,0:T(8,128)S(1)}, f32[32,1024]{1,0:T(8,128)}, u32[]{:S(2)}) %copy-start.1) | copy-done | bytes 131096
  10.4 0.2 shard_map.50
  10.6 3.3 %collective-permute-done.4.refs_4_ = f32[32,1024]{1,0:T(8,128)S(1)} collective-permute-done((f32[32,1024]{1,0:T(8,128)}, f32[32,1024]{1,0:T(8,128)S(1)}, u32[]{:S(2)}, u32[]{:S(2)}) %collective-permute-start.4) | collective-permute-done | bytes 131104 | tf_op jit(solution)/shard_map/ppermute | solution.py:263
  13.9 1.1 %collective-permute-start.7 = (f32[32,1024]{1,0:T(8,128)S(1)}, f32[32,1024]{1,0:T(8,128)S(1)}, u32[]{:S(2)}, u32[]{:S(2)}) collective-permute-start(f32[32,1024]{1,0:T(8,128)S(1)} %collective-permute-done.4.refs_4_), channel_id=1, source_target_pairs={{0,6},{2,4},{4,2},{6,0},{8,14},{10,12},{12,10},{14,8},{1,7},{3,5},... | collective-permute-start | bytes 393224 | tf_op jit(solution)/shard_map/ppermute | solution.py:263
  15.1 0.0 collective-permute-done.2.refs_2_
  15.1 0.1 collective-permute-start.6
  15.2 0.0 collective-permute-done.1.refs_1_
  15.2 2.2 %collective-permute-start.5 = (f32[32,1024]{1,0:T(8,128)S(1)}, f32[32,1024]{1,0:T(8,128)S(1)}, u32[]{:S(2)}, u32[]{:S(2)}) collective-permute-start(f32[32,1024]{1,0:T(8,128)S(1)} %collective-permute-done.4.refs_4_), channel_id=1, source_target_pairs={{0,2},{2,0},{4,6},{6,4},{8,10},{10,8},{12,14},{14,12},{1,3},{3,1},... | collective-permute-start | bytes 393224 | tf_op jit(solution)/shard_map/ppermute | solution.py:263
  17.4 0.0 collective-permute-done.3.refs_3_
  17.4 0.3 shard_map.52
  17.7 0.0 collective-permute-done.hoth
  17.7 0.0 slice-start
  17.7 0.2 shard_map.51
  18.0 0.0 slice-start.1
  18.0 1.3 %shard_map.53.refs_0_ = f32[1024,2048]{1,0:T(8,128)S(1)} custom-call(bf16[1024,256]{1,0:T(8,128)(2,1)S(1)} %get-tuple-element.36.wt.refs_2_.refs_3_.refs_0_, bf16[512,2048]{1,0:T(8,128)(2,1)S(1)} %get-tuple-element.34.h2), custom_call_target="tpu_custom_call" | custom-call | flops 1000000000 | tf_op jit(solution)/shard_map/pallas_call | solution.py:250
  19.3 0.7 %collective-permute-done.7.refs_7_ = f32[32,1024]{1,0:T(8,128)S(1)} collective-permute-done((f32[32,1024]{1,0:T(8,128)S(1)}, f32[32,1024]{1,0:T(8,128)S(1)}, u32[]{:S(2)}, u32[]{:S(2)}) %collective-permute-start.7) | collective-permute-done | bytes 131104 | tf_op jit(solution)/shard_map/ppermute | solution.py:263
  19.9 0.4 collective-permute-done.6.refs_6_
  20.3 0.9 %collective-permute-done.5.refs_5_ = f32[32,1024]{1,0:T(8,128)S(1)} collective-permute-done((f32[32,1024]{1,0:T(8,128)S(1)}, f32[32,1024]{1,0:T(8,128)S(1)}, u32[]{:S(2)}, u32[]{:S(2)}) %collective-permute-start.5) | collective-permute-done | bytes 131104 | tf_op jit(solution)/shard_map/ppermute | solution.py:263
  21.2 0.0 slice-done
  21.2 0.0 slice-done.1
  21.3 3.5 %shard_map.54 = (f32[264,1024]{1,0:T(8,128)S(1)}, bf16[256,1024]{1,0:T(8,128)(2,1)S(1)}, bf16[1024,256]{1,0:T(8,128)(2,1)S(1)}, f32[128,128]{1,0:T(8,128)}) custom-call(f32[1024,2048]{1,0:T(8,128)S(1)} %bitcast.1, bf16[512,2048]{1,0:T(8,128)(2,1)S(1)} %get-tuple-element.34.h2, f32[1024,2048]{1,0:T(8,128)S(1)} %shard_map.53.refs_0_, ...), custom_call_target="tpu_custom_call" | custom-call | tf_op jit(solution)/shard_map/pallas_call | solution.py:250
  24.7 0.0 collective-permute-start.8
  24.7 2.9 %shard_map.55.nown = f32[256,1024]{1,0:T(8,128)S(1)} custom-call(f32[1024,2048]{1,0:T(8,128)S(1)} %bitcast.1, bf16[512,2048]{1,0:T(8,128)(2,1)S(1)} %get-tuple-element.34.h2, f32[1024,2048]{1,0:T(8,128)S(1)} %shard_map.53.refs_0_, bf16[256,1024]{1,0:T(8,128)(2,1)S(1)} %get-tuple-element.37.refs_1_, bf16[256,1024]{1,0:T(8,128)(2,1)S(1)} %get-tuple-element.40.refs_2_, ...), custom_call_target="tpu_custom_call" | custom-call | tf_op jit(solution)/shard_map/pallas_call | solution.py:250
  27.7 0.6 %collective-permute-start.9 = (f32[256,1024]{1,0:T(8,128)S(1)}, f32[256,1024]{1,0:T(8,128)S(1)}, u32[]{:S(2)}, u32[]{:S(2)}) collective-permute-start(f32[256,1024]{1,0:T(8,128)S(1)} %shard_map.55.nown), channel_id=1, source_target_pairs={{0,1},{1,0},{2,3},{3,2},{4,5},{5,4},{6,7},{7,6},{8,9},{9,8},{10,11... | collective-permute-start | bytes 3145736 | tf_op jit(solution)/shard_map/ppermute | solution.py:267
  28.3 0.0 collective-permute-done.8.theirs.noth
  28.3 2.8 %shard_map.56 = (f32[128,2048]{1,0:T(8,128)}, f32[256,1024]{1,0:T(8,128)S(1)}, f32[256,128]{1,0:T(8,128)S(1)}, bf16[1024,1024]{1,0:T(8,128)(2,1)S(1)}, bf16[512,1024]{1,0:T(8,128)(2,1)S(1)}) custom-call(f32[1024,2048]{1,0:T(8,128)S(1)} %bitcast.1, f32[256,2048]{1,0:T(8,128)S(1)} %get-tuple-element.33.h, f32[264,1024]{1,0:T(8,128)S(1)} %get-tuple-element.39.mine.nown, ...), custom_call_target="tpu_custom_call" | custom-call | tf_op jit(solution)/shard_map/pallas_call | solution.py:250
  31.0 0.0 collective-permute-done.9.noth
  31.0 4.1 %shard_map.57 = (f32[128,2048]{1,0:T(8,128)}, f32[128,1024]{1,0:T(8,128)S(1)}, f32[256,128]{1,0:T(8,128)S(1)}, bf16[1024,1024]{1,0:T(8,128)(2,1)S(1)}, bf16[512,...) custom-call(f32[1024,2048]{1,0:T(8,128)S(1)} %bitcast.1, ...), custom_call_target="tpu_custom_call", output_to_operand_aliasing={{0}: (12, {})} | custom-call | tf_op jit(solution)/shard_map/pallas_call | solution.py:250
  35.1 0.9 %collective-permute-start.13 = (f32[264,128]{1,0:T(8,128)S(1)}, f32[264,128]{1,0:T(8,128)S(1)}, u32[]{:S(2)}, u32[]{:S(2)}) collective-permute-start(f32[264,128]{1,0:T(8,128)S(1)} %get-tuple-element.57), channel_id=1, source_target_pairs={{0,4},{2,6},{4,0},{6,2},{8,12},{10,14},{12,8},{14,10},{1,5},{3,7},... | collective-permute-start | bytes 405512 | tf_op jit(solution)/shard_map/ppermute | solution.py:263
  36.0 1.3 %collective-permute-start.14 = (f32[264,128]{1,0:T(8,128)S(1)}, f32[264,128]{1,0:T(8,128)S(1)}, u32[]{:S(2)}, u32[]{:S(2)}) collective-permute-start(f32[264,128]{1,0:T(8,128)S(1)} %get-tuple-element.58), channel_id=1, source_target_pairs={{0,2},{2,0},{4,6},{6,4},{8,10},{10,8},{12,14},{14,12},{1,3},{3,1},... | collective-permute-start | bytes 405512 | tf_op jit(solution)/shard_map/ppermute | solution.py:263
  37.3 1.4 %collective-permute-start.15 = (f32[264,128]{1,0:T(8,128)S(1)}, f32[264,128]{1,0:T(8,128)S(1)}, u32[]{:S(2)}, u32[]{:S(2)}) collective-permute-start(f32[264,128]{1,0:T(8,128)S(1)} %get-tuple-element.59), channel_id=1, source_target_pairs={{0,6},{2,4},{4,2},{6,0},{8,14},{10,12},{12,10},{14,8},{1,7},{3,5},... | collective-permute-start | bytes 405512 | tf_op jit(solution)/shard_map/ppermute | solution.py:263
  38.7 1.3 %shard_map.58 = (f32[264,128]{1,0:T(8,128)S(1)}, f32[264,128]{1,0:T(8,128)S(1)}, f32[264,128]{1,0:T(8,128)S(1)}, f32[264,128]{1,0:T(8,128)S(1)}) custom-call(f32[128,1024]{1,0:T(8,128)S(1)} %get-tuple-element.48.acc, f32[256,128]{1,0:T(8,128)S(1)} %get-tuple-element.49.row_mass, bf16[1024,1024]{1,0:T(8,128)(2,1)S(1)} %get-tuple-element.50.rhi_a, ...), custom_call_target="tpu_custom_call" | custom-call | flops 1000000000 | tf_op jit(solution)/shard_map/pallas_call | solution.py:250
  40.0 1.2 %collective-permute-start.10 = (f32[264,128]{1,0:T(8,128)S(1)}, f32[264,128]{1,0:T(8,128)S(1)}, u32[]{:S(2)}, u32[]{:S(2)}) collective-permute-start(f32[264,128]{1,0:T(8,128)S(1)} %get-tuple-element.53), channel_id=1, source_target_pairs={{0,2},{2,0},{4,6},{6,4},{8,10},{10,8},{12,14},{14,12},{1,3},{3,1},... | collective-permute-start | bytes 405512 | tf_op jit(solution)/shard_map/ppermute | solution.py:263
  41.2 1.1 %collective-permute-start.11 = (f32[264,128]{1,0:T(8,128)S(1)}, f32[264,128]{1,0:T(8,128)S(1)}, u32[]{:S(2)}, u32[]{:S(2)}) collective-permute-start(f32[264,128]{1,0:T(8,128)S(1)} %get-tuple-element.54), channel_id=1, source_target_pairs={{0,6},{2,4},{4,2},{6,0},{8,14},{10,12},{12,10},{14,8},{1,7},{3,5},... | collective-permute-start | bytes 405512 | tf_op jit(solution)/shard_map/ppermute | solution.py:263
  42.3 0.0 collective-permute-done.13
  42.3 1.2 %collective-permute-start.12 = (f32[264,128]{1,0:T(8,128)S(1)}, f32[264,128]{1,0:T(8,128)S(1)}, u32[]{:S(2)}, u32[]{:S(2)}) collective-permute-start(f32[264,128]{1,0:T(8,128)S(1)} %get-tuple-element.55), channel_id=1, source_target_pairs={{0,4},{2,6},{4,0},{6,2},{8,12},{10,14},{12,8},{14,10},{1,5},{3,7},... | collective-permute-start | bytes 405512 | tf_op jit(solution)/shard_map/ppermute | solution.py:263
  43.5 1.3 %collective-permute-done.14 = f32[264,128]{1,0:T(8,128)S(1)} collective-permute-done((f32[264,128]{1,0:T(8,128)S(1)}, f32[264,128]{1,0:T(8,128)S(1)}, u32[]{:S(2)}, u32[]{:S(2)}) %collective-permute-start.14) | collective-permute-done | bytes 135200 | tf_op jit(solution)/shard_map/ppermute | solution.py:263
  44.9 0.0 collective-permute-done.15
  44.9 0.1 add_add_fusion
  44.9 2.4 %collective-permute-start.16 = (f32[264,128]{1,0:T(8,128)S(1)}, f32[264,128]{1,0:T(8,128)S(1)}, u32[]{:S(2)}, u32[]{:S(2)}) collective-permute-start(f32[264,128]{1,0:T(8,128)S(1)} %add_add_fusion), channel_id=1, source_target_pairs={{0,12},{2,14},{4,8},{6,10},{8,4},{10,6},{12,0},{14,2},{1,13},{3,15... | collective-permute-start | bytes 405512 | tf_op jit(solution)/shard_map/ppermute | solution.py:263
  47.3 2.6 %collective-permute-done.10 = f32[264,128]{1,0:T(8,128)S(1)} collective-permute-done((f32[264,128]{1,0:T(8,128)S(1)}, f32[264,128]{1,0:T(8,128)S(1)}, u32[]{:S(2)}, u32[]{:S(2)}) %collective-permute-start.10) | collective-permute-done | bytes 135200 | tf_op jit(solution)/shard_map/ppermute | solution.py:263
  49.9 0.0 collective-permute-done.11
  49.9 0.2 collective-permute-done.12
  50.2 2.9 %collective-permute-done.16.more = f32[264,128]{1,0:T(8,128)S(1)} collective-permute-done((f32[264,128]{1,0:T(8,128)S(1)}, f32[264,128]{1,0:T(8,128)S(1)}, u32[]{:S(2)}, u32[]{:S(2)}) %collective-permute-start.16) | collective-permute-done | bytes 135200 | tf_op jit(solution)/shard_map/ppermute | solution.py:263
  53.1 0.7 %shard_map.59 = f32[32,1024]{1,0:T(8,128)} custom-call(f32[32,1024]{1,0:T(8,128)S(1)} %get-tuple-element.35.refs_0_.old, f32[264,128]{1,0:T(8,128)S(1)} %add_add_fusion.1.total, f32[264,128]{1,0:T(8,128)S(1)} %collective-permute-done.16.more), custom_call_target="tpu_custom_call" | custom-call | tf_op jit(solution)/shard_map/pallas_call | solution.py:250
  (2 shorter events, 0.0 us)
Async XLA Ops:
  0.6 14.4 %collective-permute-start.2 = (f32[32,1024]{1,0:T(8,128)}, f32[32,1024]{1,0:T(8,128)S(1)}, u32[]{:S(2)}, u32[]{:S(2)}) collective-permute-start(f32[32,1024]{1,0:T(8,128)} %atoms.1), channel_id=1, source_target_pairs={{0,4},{2,6},{4,0},{6,2},{8,12},{10,14},{12,8},{14,10},{1,5},{3,7},... | collective-permute-start | bytes 393224 | tf_op jit(solution)/shard_map/ppermute | solution.py:263
  3.7 11.5 %collective-permute-start.1 = (f32[32,1024]{1,0:T(8,128)}, f32[32,1024]{1,0:T(8,128)S(1)}, u32[]{:S(2)}, u32[]{:S(2)}) collective-permute-start(f32[32,1024]{1,0:T(8,128)} %atoms.1), channel_id=1, source_target_pairs={{0,2},{2,0},{4,6},{6,4},{8,10},{10,8},{12,14},{14,12},{1,3},{3,1},... | collective-permute-start | bytes 393224 | tf_op jit(solution)/shard_map/ppermute | solution.py:263
  5.2 8.7 %collective-permute-start.4 = (f32[32,1024]{1,0:T(8,128)}, f32[32,1024]{1,0:T(8,128)S(1)}, u32[]{:S(2)}, u32[]{:S(2)}) collective-permute-start(f32[32,1024]{1,0:T(8,128)} %atoms.1), channel_id=1, source_target_pairs={{0,8},{2,10},{4,12},{6,14},{8,0},{10,2},{12,4},{14,6},{1,9},{3,11}... | collective-permute-start | bytes 393224 | tf_op jit(solution)/shard_map/ppermute | solution.py:263
  7.8 9.6 %collective-permute-start.3 = (f32[32,1024]{1,0:T(8,128)}, f32[32,1024]{1,0:T(8,128)S(1)}, u32[]{:S(2)}, u32[]{:S(2)}) collective-permute-start(f32[32,1024]{1,0:T(8,128)} %atoms.1), channel_id=1, source_target_pairs={{0,6},{2,4},{4,2},{6,0},{8,14},{10,12},{12,10},{14,8},{1,7},{3,5},... | collective-permute-start | bytes 393224 | tf_op jit(solution)/shard_map/ppermute | solution.py:263
  8.2 9.5 %collective-permute-start = (f32[128,2048]{1,0:T(8,128)}, f32[128,2048]{1,0:T(8,128)S(1)}, u32[]{:S(2)}, u32[]{:S(2)}) collective-permute-start(f32[128,2048]{1,0:T(8,128)} %hown.1), channel_id=1, source_target_pairs={{0,1},{1,0},{2,3},{3,2},{4,5},{5,4},{6,7},{7,6},{8,9},{9,8},{10,11... | collective-permute-start | bytes 3145736 | tf_op jit(solution)/shard_map/ppermute | solution.py:267
  8.2 1.2 %copy-start = (f32[128,2048]{1,0:T(8,128)S(1)}, f32[128,2048]{1,0:T(8,128)}, u32[]{:S(2)}) copy-start(f32[128,2048]{1,0:T(8,128)} %hown.1) | copy-start | bytes 3145732
  9.4 0.9 %copy-start.1 = (f32[32,1024]{1,0:T(8,128)S(1)}, f32[32,1024]{1,0:T(8,128)}, u32[]{:S(2)}) copy-start(f32[32,1024]{1,0:T(8,128)} %atoms.1) | copy-start | bytes 393220
  13.9 6.0 %collective-permute-start.7 = (f32[32,1024]{1,0:T(8,128)S(1)}, f32[32,1024]{1,0:T(8,128)S(1)}, u32[]{:S(2)}, u32[]{:S(2)}) collective-permute-start(f32[32,1024]{1,0:T(8,128)S(1)} %collective-permute-done.4.refs_4_), channel_id=1, source_target_pairs={{0,6},{2,4},{4,2},{6,0},{8,14},{10,12},{12,10},{14,8},{1,7},{3,5},... | collective-permute-start | bytes 393224 | tf_op jit(solution)/shard_map/ppermute | solution.py:263
  15.1 5.2 %collective-permute-start.6 = (f32[32,1024]{1,0:T(8,128)S(1)}, f32[32,1024]{1,0:T(8,128)S(1)}, u32[]{:S(2)}, u32[]{:S(2)}) collective-permute-start(f32[32,1024]{1,0:T(8,128)S(1)} %collective-permute-done.4.refs_4_), channel_id=1, source_target_pairs={{0,4},{2,6},{4,0},{6,2},{8,12},{10,14},{12,8},{14,10},{1,5},{3,7},... | collective-permute-start | bytes 393224 | tf_op jit(solution)/shard_map/ppermute | solution.py:263
  15.2 6.0 %collective-permute-start.5 = (f32[32,1024]{1,0:T(8,128)S(1)}, f32[32,1024]{1,0:T(8,128)S(1)}, u32[]{:S(2)}, u32[]{:S(2)}) collective-permute-start(f32[32,1024]{1,0:T(8,128)S(1)} %collective-permute-done.4.refs_4_), channel_id=1, source_target_pairs={{0,2},{2,0},{4,6},{6,4},{8,10},{10,8},{12,14},{14,12},{1,3},{3,1},... | collective-permute-start | bytes 393224 | tf_op jit(solution)/shard_map/ppermute | solution.py:263
  17.7 3.5 %slice-start = ((s8[8388608]{0:T(1024)(128)(4,1)}), s8[4194304]{0:T(1024)(128)(4,1)S(1)}, s32[]{:S(2)}) async-start(s8[8388608]{0:T(1024)(128)(4,1)} %bitcast), calls=%async_computation | async-start | bytes 8388608
  18.0 3.3 %slice-start.1 = ((s8[8388608]{0:T(1024)(128)(4,1)}), s8[4194304]{0:T(1024)(128)(4,1)S(1)}, s32[]{:S(2)}) async-start(s8[8388608]{0:T(1024)(128)(4,1)} %bitcast), calls=%async_computation.1 | async-start | bytes 8388608
  24.7 3.5 %collective-permute-start.8 = (f32[264,1024]{1,0:T(8,128)S(1)}, f32[264,1024]{1,0:T(8,128)S(1)}, u32[]{:S(2)}, u32[]{:S(2)}) collective-permute-start(f32[264,1024]{1,0:T(8,128)S(1)} %get-tuple-element.39.mine.nown), channel_id=1, source_target_pairs={{0,1},{1,0},{2,3},{3,2},{4,5},{5,4},{6,7},{7,6},{8,9},{9,8},{10,11... | collective-permute-start | bytes 3244040 | tf_op jit(solution)/shard_map/ppermute | solution.py:267
  27.7 3.3 %collective-permute-start.9 = (f32[256,1024]{1,0:T(8,128)S(1)}, f32[256,1024]{1,0:T(8,128)S(1)}, u32[]{:S(2)}, u32[]{:S(2)}) collective-permute-start(f32[256,1024]{1,0:T(8,128)S(1)} %shard_map.55.nown), channel_id=1, source_target_pairs={{0,1},{1,0},{2,3},{3,2},{4,5},{5,4},{6,7},{7,6},{8,9},{9,8},{10,11... | collective-permute-start | bytes 3145736 | tf_op jit(solution)/shard_map/ppermute | solution.py:267
  35.1 7.2 %collective-permute-start.13 = (f32[264,128]{1,0:T(8,128)S(1)}, f32[264,128]{1,0:T(8,128)S(1)}, u32[]{:S(2)}, u32[]{:S(2)}) collective-permute-start(f32[264,128]{1,0:T(8,128)S(1)} %get-tuple-element.57), channel_id=1, source_target_pairs={{0,4},{2,6},{4,0},{6,2},{8,12},{10,14},{12,8},{14,10},{1,5},{3,7},... | collective-permute-start | bytes 405512 | tf_op jit(solution)/shard_map/ppermute | solution.py:263
  36.0 8.9 %collective-permute-start.14 = (f32[264,128]{1,0:T(8,128)S(1)}, f32[264,128]{1,0:T(8,128)S(1)}, u32[]{:S(2)}, u32[]{:S(2)}) collective-permute-start(f32[264,128]{1,0:T(8,128)S(1)} %get-tuple-element.58), channel_id=1, source_target_pairs={{0,2},{2,0},{4,6},{6,4},{8,10},{10,8},{12,14},{14,12},{1,3},{3,1},... | collective-permute-start | bytes 405512 | tf_op jit(solution)/shard_map/ppermute | solution.py:263
  37.3 7.6 %collective-permute-start.15 = (f32[264,128]{1,0:T(8,128)S(1)}, f32[264,128]{1,0:T(8,128)S(1)}, u32[]{:S(2)}, u32[]{:S(2)}) collective-permute-start(f32[264,128]{1,0:T(8,128)S(1)} %get-tuple-element.59), channel_id=1, source_target_pairs={{0,6},{2,4},{4,2},{6,0},{8,14},{10,12},{12,10},{14,8},{1,7},{3,5},... | collective-permute-start | bytes 405512 | tf_op jit(solution)/shard_map/ppermute | solution.py:263
  40.0 9.9 %collective-permute-start.10 = (f32[264,128]{1,0:T(8,128)S(1)}, f32[264,128]{1,0:T(8,128)S(1)}, u32[]{:S(2)}, u32[]{:S(2)}) collective-permute-start(f32[264,128]{1,0:T(8,128)S(1)} %get-tuple-element.53), channel_id=1, source_target_pairs={{0,2},{2,0},{4,6},{6,4},{8,10},{10,8},{12,14},{14,12},{1,3},{3,1},... | collective-permute-start | bytes 405512 | tf_op jit(solution)/shard_map/ppermute | solution.py:263
  41.2 8.7 %collective-permute-start.11 = (f32[264,128]{1,0:T(8,128)S(1)}, f32[264,128]{1,0:T(8,128)S(1)}, u32[]{:S(2)}, u32[]{:S(2)}) collective-permute-start(f32[264,128]{1,0:T(8,128)S(1)} %get-tuple-element.54), channel_id=1, source_target_pairs={{0,6},{2,4},{4,2},{6,0},{8,14},{10,12},{12,10},{14,8},{1,7},{3,5},... | collective-permute-start | bytes 405512 | tf_op jit(solution)/shard_map/ppermute | solution.py:263
  42.3 7.8 %collective-permute-start.12 = (f32[264,128]{1,0:T(8,128)S(1)}, f32[264,128]{1,0:T(8,128)S(1)}, u32[]{:S(2)}, u32[]{:S(2)}) collective-permute-start(f32[264,128]{1,0:T(8,128)S(1)} %get-tuple-element.55), channel_id=1, source_target_pairs={{0,4},{2,6},{4,0},{6,2},{8,12},{10,14},{12,8},{14,10},{1,5},{3,7},... | collective-permute-start | bytes 405512 | tf_op jit(solution)/shard_map/ppermute | solution.py:263
  44.9 8.2 %collective-permute-start.16 = (f32[264,128]{1,0:T(8,128)S(1)}, f32[264,128]{1,0:T(8,128)S(1)}, u32[]{:S(2)}, u32[]{:S(2)}) collective-permute-start(f32[264,128]{1,0:T(8,128)S(1)} %add_add_fusion), channel_id=1, source_target_pairs={{0,12},{2,14},{4,8},{6,10},{8,4},{10,6},{12,0},{14,2},{1,13},{3,15... | collective-permute-start | bytes 405512 | tf_op jit(solution)/shard_map/ppermute | solution.py:263

commit v8 on v7

--- a/solution.py
+++ b/solution.py
@@ -140,8 +140,14 @@
             rhi[rows, at] = hi
             rlo[rows, at] = lo
         whi = jnp.concatenate([w[: w.shape[0] // 2, :] for w in w2], axis=0)
-        wlo = jnp.concatenate([w[w.shape[0] // 2 :, :] for w in w2], axis=0)
-        numer[:atoms, at] = dot(whi, rhi[:, at]) + dot(wlo, rhi[:, at]) + dot(whi, rlo[:, at])
+        both = dot(jnp.concatenate([w[...] for w in w2], axis=0), rhi[:, at])
+        low = dot(whi, rlo[:, at])
+        part = atoms // len(w2)
+        for p in range(len(w2)):
+            hi_rows = slice(2 * p * part, (2 * p + 1) * part)
+            lo_rows = slice((2 * p + 1) * part, (2 * p + 2) * part)
+            rows = slice(p * part, (p + 1) * part)
+            numer[rows, at] = both[hi_rows, :] + both[lo_rows, :] + low[rows, :]
     if mass:
         part = mass[0].shape[0]
         numer[atoms:, :] = jnp.zeros((8, frames), f32)

time: 54 us -> 54.1 us (level)
  no operation moved by 1% of the time
where the time goes in v8:
time: 54.1 us; the launch traced here: 53.9 us
  starting transfers between devices  21.2 us (39%)
  Pallas kernels  17.4 us (32%)
  waiting for transfers between devices  12.3 us (23%)
  local copies, waits for them, and re-layouts  2.19 us (4%)
  between operations  0.73 us (1%)
    ppermute x14, starting transfers between devices, hop(): return lax.ppermute(x, 'frames', [(i, i ^ step) for i in range(8)])  20.6 us
    pallas_call x10, Pallas kernels, call(): pl.pallas_call(kernel, in_specs=list(in_specs) + [WHOLE] * (len(ins) - le...  17.4 us
    ppermute x14, waiting for transfers between devices, hop(): return lax.ppermute(x, 'frames', [(i, i ^ step) for i in range(8)])  12.3 us
    unnamed x8, local copies, waits for them, and re-layouts  2.19 us
  transfers between devices with their start and end apart: 17, of which 8 were waited for; matrix products, arithmetic and copies ran while one was open for 0% of the time, Pallas kernels for 17%

profile of v8, /device:TPU:0, one launch (start us, length us, event | category | flops | bytes accessed | tf_op | source)
XLA Modules:
  0.0 53.9 jit_solution(9395688770410291557)
XLA Ops:
  0.6 3.1 %collective-permute-start.2 = (f32[32,1024]{1,0:T(8,128)}, f32[32,1024]{1,0:T(8,128)S(1)}, u32[]{:S(2)}, u32[]{:S(2)}) collective-permute-start(f32[32,1024]{1,0:T(8,128)} %atoms.1), channel_id=1, source_target_pairs={{0,4},{2,6},{4,0},{6,2},{8,12},{10,14},{12,8},{14,10},{1,5},{3,7},... | collective-permute-start | bytes 393224 | tf_op jit(solution)/shard_map/ppermute | solution.py:269
  3.7 1.5 %collective-permute-start.1 = (f32[32,1024]{1,0:T(8,128)}, f32[32,1024]{1,0:T(8,128)S(1)}, u32[]{:S(2)}, u32[]{:S(2)}) collective-permute-start(f32[32,1024]{1,0:T(8,128)} %atoms.1), channel_id=1, source_target_pairs={{0,2},{2,0},{4,6},{6,4},{8,10},{10,8},{12,14},{14,12},{1,3},{3,1},... | collective-permute-start | bytes 393224 | tf_op jit(solution)/shard_map/ppermute | solution.py:269
  5.2 2.6 %collective-permute-start.4 = (f32[32,1024]{1,0:T(8,128)}, f32[32,1024]{1,0:T(8,128)S(1)}, u32[]{:S(2)}, u32[]{:S(2)}) collective-permute-start(f32[32,1024]{1,0:T(8,128)} %atoms.1), channel_id=1, source_target_pairs={{0,8},{2,10},{4,12},{6,14},{8,0},{10,2},{12,4},{14,6},{1,9},{3,11}... | collective-permute-start | bytes 393224 | tf_op jit(solution)/shard_map/ppermute | solution.py:269
  7.8 0.4 collective-permute-start.3
  8.2 0.0 collective-permute-start
  8.2 0.0 copy-start
  8.2 1.2 %copy-done = f32[128,2048]{1,0:T(8,128)S(1)} copy-done((f32[128,2048]{1,0:T(8,128)S(1)}, f32[128,2048]{1,0:T(8,128)}, u32[]{:S(2)}) %copy-start) | copy-done | bytes 1048600
  9.4 0.0 copy-start.1
  9.5 0.9 %copy-done.1 = f32[32,1024]{1,0:T(8,128)S(1)} copy-done((f32[32,1024]{1,0:T(8,128)S(1)}, f32[32,1024]{1,0:T(8,128)}, u32[]{:S(2)}) %copy-start.1) | copy-done | bytes 131096
  10.4 0.2 shard_map.50
  10.6 3.3 %collective-permute-done.4.refs_4_ = f32[32,1024]{1,0:T(8,128)S(1)} collective-permute-done((f32[32,1024]{1,0:T(8,128)}, f32[32,1024]{1,0:T(8,128)S(1)}, u32[]{:S(2)}, u32[]{:S(2)}) %collective-permute-start.4) | collective-permute-done | bytes 131104 | tf_op jit(solution)/shard_map/ppermute | solution.py:269
  13.9 1.1 %collective-permute-start.7 = (f32[32,1024]{1,0:T(8,128)S(1)}, f32[32,1024]{1,0:T(8,128)S(1)}, u32[]{:S(2)}, u32[]{:S(2)}) collective-permute-start(f32[32,1024]{1,0:T(8,128)S(1)} %collective-permute-done.4.refs_4_), channel_id=1, source_target_pairs={{0,6},{2,4},{4,2},{6,0},{8,14},{10,12},{12,10},{14,8},{1,7},{3,5},... | collective-permute-start | bytes 393224 | tf_op jit(solution)/shard_map/ppermute | solution.py:269
  15.1 0.0 collective-permute-done.2.refs_2_
  15.1 0.1 collective-permute-start.6
  15.2 0.0 collective-permute-done.1.refs_1_
  15.2 2.2 %collective-permute-start.5 = (f32[32,1024]{1,0:T(8,128)S(1)}, f32[32,1024]{1,0:T(8,128)S(1)}, u32[]{:S(2)}, u32[]{:S(2)}) collective-permute-start(f32[32,1024]{1,0:T(8,128)S(1)} %collective-permute-done.4.refs_4_), channel_id=1, source_target_pairs={{0,2},{2,0},{4,6},{6,4},{8,10},{10,8},{12,14},{14,12},{1,3},{3,1},... | collective-permute-start | bytes 393224 | tf_op jit(solution)/shard_map/ppermute | solution.py:269
  17.4 0.0 collective-permute-done.3.refs_3_
  17.4 0.3 shard_map.52
  17.7 0.0 collective-permute-done.hoth
  17.7 0.0 slice-start
  17.7 0.2 shard_map.51
  18.0 0.0 slice-start.1
  18.0 1.3 %shard_map.53.refs_0_ = f32[1024,2048]{1,0:T(8,128)S(1)} custom-call(bf16[1024,256]{1,0:T(8,128)(2,1)S(1)} %get-tuple-element.36.wt.refs_2_.refs_3_.refs_0_, bf16[512,2048]{1,0:T(8,128)(2,1)S(1)} %get-tuple-element.34.h2), custom_call_target="tpu_custom_call" | custom-call | flops 1000000000 | tf_op jit(solution)/shard_map/pallas_call | solution.py:256
  19.3 0.7 %collective-permute-done.7.refs_7_ = f32[32,1024]{1,0:T(8,128)S(1)} collective-permute-done((f32[32,1024]{1,0:T(8,128)S(1)}, f32[32,1024]{1,0:T(8,128)S(1)}, u32[]{:S(2)}, u32[]{:S(2)}) %collective-permute-start.7) | collective-permute-done | bytes 131104 | tf_op jit(solution)/shard_map/ppermute | solution.py:269
  19.9 0.4 collective-permute-done.6.refs_6_
  20.3 0.9 %collective-permute-done.5.refs_5_ = f32[32,1024]{1,0:T(8,128)S(1)} collective-permute-done((f32[32,1024]{1,0:T(8,128)S(1)}, f32[32,1024]{1,0:T(8,128)S(1)}, u32[]{:S(2)}, u32[]{:S(2)}) %collective-permute-start.5) | collective-permute-done | bytes 131104 | tf_op jit(solution)/shard_map/ppermute | solution.py:269
  21.2 0.0 slice-done
  21.2 0.0 slice-done.1
  21.3 3.5 %shard_map.54 = (f32[264,1024]{1,0:T(8,128)S(1)}, bf16[256,1024]{1,0:T(8,128)(2,1)S(1)}, bf16[1024,256]{1,0:T(8,128)(2,1)S(1)}, f32[128,128]{1,0:T(8,128)}) custom-call(f32[1024,2048]{1,0:T(8,128)S(1)} %bitcast.1, bf16[512,2048]{1,0:T(8,128)(2,1)S(1)} %get-tuple-element.34.h2, f32[1024,2048]{1,0:T(8,128)S(1)} %shard_map.53.refs_0_, ...), custom_call_target="tpu_custom_call" | custom-call | tf_op jit(solution)/shard_map/pallas_call | solution.py:256
  24.8 0.0 collective-permute-start.8
  24.8 2.9 %shard_map.55.nown = f32[256,1024]{1,0:T(8,128)S(1)} custom-call(f32[1024,2048]{1,0:T(8,128)S(1)} %bitcast.1, bf16[512,2048]{1,0:T(8,128)(2,1)S(1)} %get-tuple-element.34.h2, f32[1024,2048]{1,0:T(8,128)S(1)} %shard_map.53.refs_0_, bf16[256,1024]{1,0:T(8,128)(2,1)S(1)} %get-tuple-element.37.refs_1_, bf16[256,1024]{1,0:T(8,128)(2,1)S(1)} %get-tuple-element.40.refs_2_, ...), custom_call_target="tpu_custom_call" | custom-call | tf_op jit(solution)/shard_map/pallas_call | solution.py:256
  27.8 0.6 %collective-permute-start.9 = (f32[256,1024]{1,0:T(8,128)S(1)}, f32[256,1024]{1,0:T(8,128)S(1)}, u32[]{:S(2)}, u32[]{:S(2)}) collective-permute-start(f32[256,1024]{1,0:T(8,128)S(1)} %shard_map.55.nown), channel_id=1, source_target_pairs={{0,1},{1,0},{2,3},{3,2},{4,5},{5,4},{6,7},{7,6},{8,9},{9,8},{10,11... | collective-permute-start | bytes 3145736 | tf_op jit(solution)/shard_map/ppermute | solution.py:273
  28.3 0.0 collective-permute-done.8.theirs.noth
  28.3 2.8 %shard_map.56 = (f32[128,2048]{1,0:T(8,128)}, f32[256,1024]{1,0:T(8,128)S(1)}, f32[256,128]{1,0:T(8,128)S(1)}, bf16[1024,1024]{1,0:T(8,128)(2,1)S(1)}, bf16[512,1024]{1,0:T(8,128)(2,1)S(1)}) custom-call(f32[1024,2048]{1,0:T(8,128)S(1)} %bitcast.1, f32[256,2048]{1,0:T(8,128)S(1)} %get-tuple-element.33.h, f32[264,1024]{1,0:T(8,128)S(1)} %get-tuple-element.39.mine.nown, ...), custom_call_target="tpu_custom_call" | custom-call | tf_op jit(solution)/shard_map/pallas_call | solution.py:256
  31.1 0.0 collective-permute-done.9.noth
  31.1 4.1 %shard_map.57 = (f32[128,2048]{1,0:T(8,128)}, f32[128,1024]{1,0:T(8,128)S(1)}, f32[256,128]{1,0:T(8,128)S(1)}, bf16[1024,1024]{1,0:T(8,128)(2,1)S(1)}, bf16[512,...) custom-call(f32[1024,2048]{1,0:T(8,128)S(1)} %bitcast.1, ...), custom_call_target="tpu_custom_call", output_to_operand_aliasing={{0}: (12, {})} | custom-call | tf_op jit(solution)/shard_map/pallas_call | solution.py:256
  35.2 0.9 %collective-permute-start.13 = (f32[264,128]{1,0:T(8,128)S(1)}, f32[264,128]{1,0:T(8,128)S(1)}, u32[]{:S(2)}, u32[]{:S(2)}) collective-permute-start(f32[264,128]{1,0:T(8,128)S(1)} %get-tuple-element.57), channel_id=1, source_target_pairs={{0,4},{2,6},{4,0},{6,2},{8,12},{10,14},{12,8},{14,10},{1,5},{3,7},... | collective-permute-start | bytes 405512 | tf_op jit(solution)/shard_map/ppermute | solution.py:269
  36.1 1.3 %collective-permute-start.14 = (f32[264,128]{1,0:T(8,128)S(1)}, f32[264,128]{1,0:T(8,128)S(1)}, u32[]{:S(2)}, u32[]{:S(2)}) collective-permute-start(f32[264,128]{1,0:T(8,128)S(1)} %get-tuple-element.58), channel_id=1, source_target_pairs={{0,2},{2,0},{4,6},{6,4},{8,10},{10,8},{12,14},{14,12},{1,3},{3,1},... | collective-permute-start | bytes 405512 | tf_op jit(solution)/shard_map/ppermute | solution.py:269
  37.4 1.4 %collective-permute-start.15 = (f32[264,128]{1,0:T(8,128)S(1)}, f32[264,128]{1,0:T(8,128)S(1)}, u32[]{:S(2)}, u32[]{:S(2)}) collective-permute-start(f32[264,128]{1,0:T(8,128)S(1)} %get-tuple-element.59), channel_id=1, source_target_pairs={{0,6},{2,4},{4,2},{6,0},{8,14},{10,12},{12,10},{14,8},{1,7},{3,5},... | collective-permute-start | bytes 405512 | tf_op jit(solution)/shard_map/ppermute | solution.py:269
  38.7 1.3 %shard_map.58 = (f32[264,128]{1,0:T(8,128)S(1)}, f32[264,128]{1,0:T(8,128)S(1)}, f32[264,128]{1,0:T(8,128)S(1)}, f32[264,128]{1,0:T(8,128)S(1)}) custom-call(f32[128,1024]{1,0:T(8,128)S(1)} %get-tuple-element.48.acc, f32[256,128]{1,0:T(8,128)S(1)} %get-tuple-element.49.row_mass, bf16[1024,1024]{1,0:T(8,128)(2,1)S(1)} %get-tuple-element.50.rhi_a, ...), custom_call_target="tpu_custom_call" | custom-call | flops 1000000000 | tf_op jit(solution)/shard_map/pallas_call | solution.py:256
  40.1 1.2 %collective-permute-start.10 = (f32[264,128]{1,0:T(8,128)S(1)}, f32[264,128]{1,0:T(8,128)S(1)}, u32[]{:S(2)}, u32[]{:S(2)}) collective-permute-start(f32[264,128]{1,0:T(8,128)S(1)} %get-tuple-element.53), channel_id=1, source_target_pairs={{0,2},{2,0},{4,6},{6,4},{8,10},{10,8},{12,14},{14,12},{1,3},{3,1},... | collective-permute-start | bytes 405512 | tf_op jit(solution)/shard_map/ppermute | solution.py:269
  41.3 1.1 %collective-permute-start.11 = (f32[264,128]{1,0:T(8,128)S(1)}, f32[264,128]{1,0:T(8,128)S(1)}, u32[]{:S(2)}, u32[]{:S(2)}) collective-permute-start(f32[264,128]{1,0:T(8,128)S(1)} %get-tuple-element.54), channel_id=1, source_target_pairs={{0,6},{2,4},{4,2},{6,0},{8,14},{10,12},{12,10},{14,8},{1,7},{3,5},... | collective-permute-start | bytes 405512 | tf_op jit(solution)/shard_map/ppermute | solution.py:269
  42.4 0.0 collective-permute-done.13
  42.4 1.2 %collective-permute-start.12 = (f32[264,128]{1,0:T(8,128)S(1)}, f32[264,128]{1,0:T(8,128)S(1)}, u32[]{:S(2)}, u32[]{:S(2)}) collective-permute-start(f32[264,128]{1,0:T(8,128)S(1)} %get-tuple-element.55), channel_id=1, source_target_pairs={{0,4},{2,6},{4,0},{6,2},{8,12},{10,14},{12,8},{14,10},{1,5},{3,7},... | collective-permute-start | bytes 405512 | tf_op jit(solution)/shard_map/ppermute | solution.py:269
  43.6 1.3 %collective-permute-done.14 = f32[264,128]{1,0:T(8,128)S(1)} collective-permute-done((f32[264,128]{1,0:T(8,128)S(1)}, f32[264,128]{1,0:T(8,128)S(1)}, u32[]{:S(2)}, u32[]{:S(2)}) %collective-permute-start.14) | collective-permute-done | bytes 135200 | tf_op jit(solution)/shard_map/ppermute | solution.py:269
  44.9 0.0 collective-permute-done.15
  44.9 0.1 add_add_fusion
  45.0 2.4 %collective-permute-start.16 = (f32[264,128]{1,0:T(8,128)S(1)}, f32[264,128]{1,0:T(8,128)S(1)}, u32[]{:S(2)}, u32[]{:S(2)}) collective-permute-start(f32[264,128]{1,0:T(8,128)S(1)} %add_add_fusion), channel_id=1, source_target_pairs={{0,12},{2,14},{4,8},{6,10},{8,4},{10,6},{12,0},{14,2},{1,13},{3,15... | collective-permute-start | bytes 405512 | tf_op jit(solution)/shard_map/ppermute | solution.py:269
  47.4 2.6 %collective-permute-done.10 = f32[264,128]{1,0:T(8,128)S(1)} collective-permute-done((f32[264,128]{1,0:T(8,128)S(1)}, f32[264,128]{1,0:T(8,128)S(1)}, u32[]{:S(2)}, u32[]{:S(2)}) %collective-permute-start.10) | collective-permute-done | bytes 135200 | tf_op jit(solution)/shard_map/ppermute | solution.py:269
  50.0 0.0 collective-permute-done.11
  50.0 0.2 collective-permute-done.12
  50.2 2.9 %collective-permute-done.16.more = f32[264,128]{1,0:T(8,128)S(1)} collective-permute-done((f32[264,128]{1,0:T(8,128)S(1)}, f32[264,128]{1,0:T(8,128)S(1)}, u32[]{:S(2)}, u32[]{:S(2)}) %collective-permute-start.16) | collective-permute-done | bytes 135200 | tf_op jit(solution)/shard_map/ppermute | solution.py:269
  53.2 0.7 %shard_map.59 = f32[32,1024]{1,0:T(8,128)} custom-call(f32[32,1024]{1,0:T(8,128)S(1)} %get-tuple-element.35.refs_0_.old, f32[264,128]{1,0:T(8,128)S(1)} %add_add_fusion.1.total, f32[264,128]{1,0:T(8,128)S(1)} %collective-permute-done.16.more), custom_call_target="tpu_custom_call" | custom-call | tf_op jit(solution)/shard_map/pallas_call | solution.py:256
  (2 shorter events, 0.0 us)
Async XLA Ops:
  0.6 14.4 %collective-permute-start.2 = (f32[32,1024]{1,0:T(8,128)}, f32[32,1024]{1,0:T(8,128)S(1)}, u32[]{:S(2)}, u32[]{:S(2)}) collective-permute-start(f32[32,1024]{1,0:T(8,128)} %atoms.1), channel_id=1, source_target_pairs={{0,4},{2,6},{4,0},{6,2},{8,12},{10,14},{12,8},{14,10},{1,5},{3,7},... | collective-permute-start | bytes 393224 | tf_op jit(solution)/shard_map/ppermute | solution.py:269
  3.7 11.5 %collective-permute-start.1 = (f32[32,1024]{1,0:T(8,128)}, f32[32,1024]{1,0:T(8,128)S(1)}, u32[]{:S(2)}, u32[]{:S(2)}) collective-permute-start(f32[32,1024]{1,0:T(8,128)} %atoms.1), channel_id=1, source_target_pairs={{0,2},{2,0},{4,6},{6,4},{8,10},{10,8},{12,14},{14,12},{1,3},{3,1},... | collective-permute-start | bytes 393224 | tf_op jit(solution)/shard_map/ppermute | solution.py:269
  5.2 8.7 %collective-permute-start.4 = (f32[32,1024]{1,0:T(8,128)}, f32[32,1024]{1,0:T(8,128)S(1)}, u32[]{:S(2)}, u32[]{:S(2)}) collective-permute-start(f32[32,1024]{1,0:T(8,128)} %atoms.1), channel_id=1, source_target_pairs={{0,8},{2,10},{4,12},{6,14},{8,0},{10,2},{12,4},{14,6},{1,9},{3,11}... | collective-permute-start | bytes 393224 | tf_op jit(solution)/shard_map/ppermute | solution.py:269
  7.8 9.6 %collective-permute-start.3 = (f32[32,1024]{1,0:T(8,128)}, f32[32,1024]{1,0:T(8,128)S(1)}, u32[]{:S(2)}, u32[]{:S(2)}) collective-permute-start(f32[32,1024]{1,0:T(8,128)} %atoms.1), channel_id=1, source_target_pairs={{0,6},{2,4},{4,2},{6,0},{8,14},{10,12},{12,10},{14,8},{1,7},{3,5},... | collective-permute-start | bytes 393224 | tf_op jit(solution)/shard_map/ppermute | solution.py:269
  8.2 9.5 %collective-permute-start = (f32[128,2048]{1,0:T(8,128)}, f32[128,2048]{1,0:T(8,128)S(1)}, u32[]{:S(2)}, u32[]{:S(2)}) collective-permute-start(f32[128,2048]{1,0:T(8,128)} %hown.1), channel_id=1, source_target_pairs={{0,1},{1,0},{2,3},{3,2},{4,5},{5,4},{6,7},{7,6},{8,9},{9,8},{10,11... | collective-permute-start | bytes 3145736 | tf_op jit(solution)/shard_map/ppermute | solution.py:273
  8.2 1.2 %copy-start = (f32[128,2048]{1,0:T(8,128)S(1)}, f32[128,2048]{1,0:T(8,128)}, u32[]{:S(2)}) copy-start(f32[128,2048]{1,0:T(8,128)} %hown.1) | copy-start | bytes 3145732
  9.4 0.9 %copy-start.1 = (f32[32,1024]{1,0:T(8,128)S(1)}, f32[32,1024]{1,0:T(8,128)}, u32[]{:S(2)}) copy-start(f32[32,1024]{1,0:T(8,128)} %atoms.1) | copy-start | bytes 393220
  13.9 6.0 %collective-permute-start.7 = (f32[32,1024]{1,0:T(8,128)S(1)}, f32[32,1024]{1,0:T(8,128)S(1)}, u32[]{:S(2)}, u32[]{:S(2)}) collective-permute-start(f32[32,1024]{1,0:T(8,128)S(1)} %collective-permute-done.4.refs_4_), channel_id=1, source_target_pairs={{0,6},{2,4},{4,2},{6,0},{8,14},{10,12},{12,10},{14,8},{1,7},{3,5},... | collective-permute-start | bytes 393224 | tf_op jit(solution)/shard_map/ppermute | solution.py:269
  15.1 5.2 %collective-permute-start.6 = (f32[32,1024]{1,0:T(8,128)S(1)}, f32[32,1024]{1,0:T(8,128)S(1)}, u32[]{:S(2)}, u32[]{:S(2)}) collective-permute-start(f32[32,1024]{1,0:T(8,128)S(1)} %collective-permute-done.4.refs_4_), channel_id=1, source_target_pairs={{0,4},{2,6},{4,0},{6,2},{8,12},{10,14},{12,8},{14,10},{1,5},{3,7},... | collective-permute-start | bytes 393224 | tf_op jit(solution)/shard_map/ppermute | solution.py:269
  15.2 6.0 %collective-permute-start.5 = (f32[32,1024]{1,0:T(8,128)S(1)}, f32[32,1024]{1,0:T(8,128)S(1)}, u32[]{:S(2)}, u32[]{:S(2)}) collective-permute-start(f32[32,1024]{1,0:T(8,128)S(1)} %collective-permute-done.4.refs_4_), channel_id=1, source_target_pairs={{0,2},{2,0},{4,6},{6,4},{8,10},{10,8},{12,14},{14,12},{1,3},{3,1},... | collective-permute-start | bytes 393224 | tf_op jit(solution)/shard_map/ppermute | solution.py:269
  17.7 3.5 %slice-start = ((s8[8388608]{0:T(1024)(128)(4,1)}), s8[4194304]{0:T(1024)(128)(4,1)S(1)}, s32[]{:S(2)}) async-start(s8[8388608]{0:T(1024)(128)(4,1)} %bitcast), calls=%async_computation | async-start | bytes 8388608
  18.0 3.3 %slice-start.1 = ((s8[8388608]{0:T(1024)(128)(4,1)}), s8[4194304]{0:T(1024)(128)(4,1)S(1)}, s32[]{:S(2)}) async-start(s8[8388608]{0:T(1024)(128)(4,1)} %bitcast), calls=%async_computation.1 | async-start | bytes 8388608
  24.8 3.5 %collective-permute-start.8 = (f32[264,1024]{1,0:T(8,128)S(1)}, f32[264,1024]{1,0:T(8,128)S(1)}, u32[]{:S(2)}, u32[]{:S(2)}) collective-permute-start(f32[264,1024]{1,0:T(8,128)S(1)} %get-tuple-element.39.mine.nown), channel_id=1, source_target_pairs={{0,1},{1,0},{2,3},{3,2},{4,5},{5,4},{6,7},{7,6},{8,9},{9,8},{10,11... | collective-permute-start | bytes 3244040 | tf_op jit(solution)/shard_map/ppermute | solution.py:273
  27.8 3.3 %collective-permute-start.9 = (f32[256,1024]{1,0:T(8,128)S(1)}, f32[256,1024]{1,0:T(8,128)S(1)}, u32[]{:S(2)}, u32[]{:S(2)}) collective-permute-start(f32[256,1024]{1,0:T(8,128)S(1)} %shard_map.55.nown), channel_id=1, source_target_pairs={{0,1},{1,0},{2,3},{3,2},{4,5},{5,4},{6,7},{7,6},{8,9},{9,8},{10,11... | collective-permute-start | bytes 3145736 | tf_op jit(solution)/shard_map/ppermute | solution.py:273
  35.2 7.2 %collective-permute-start.13 = (f32[264,128]{1,0:T(8,128)S(1)}, f32[264,128]{1,0:T(8,128)S(1)}, u32[]{:S(2)}, u32[]{:S(2)}) collective-permute-start(f32[264,128]{1,0:T(8,128)S(1)} %get-tuple-element.57), channel_id=1, source_target_pairs={{0,4},{2,6},{4,0},{6,2},{8,12},{10,14},{12,8},{14,10},{1,5},{3,7},... | collective-permute-start | bytes 405512 | tf_op jit(solution)/shard_map/ppermute | solution.py:269
  36.1 8.9 %collective-permute-start.14 = (f32[264,128]{1,0:T(8,128)S(1)}, f32[264,128]{1,0:T(8,128)S(1)}, u32[]{:S(2)}, u32[]{:S(2)}) collective-permute-start(f32[264,128]{1,0:T(8,128)S(1)} %get-tuple-element.58), channel_id=1, source_target_pairs={{0,2},{2,0},{4,6},{6,4},{8,10},{10,8},{12,14},{14,12},{1,3},{3,1},... | collective-permute-start | bytes 405512 | tf_op jit(solution)/shard_map/ppermute | solution.py:269
  37.4 7.6 %collective-permute-start.15 = (f32[264,128]{1,0:T(8,128)S(1)}, f32[264,128]{1,0:T(8,128)S(1)}, u32[]{:S(2)}, u32[]{:S(2)}) collective-permute-start(f32[264,128]{1,0:T(8,128)S(1)} %get-tuple-element.59), channel_id=1, source_target_pairs={{0,6},{2,4},{4,2},{6,0},{8,14},{10,12},{12,10},{14,8},{1,7},{3,5},... | collective-permute-start | bytes 405512 | tf_op jit(solution)/shard_map/ppermute | solution.py:269
  40.1 9.9 %collective-permute-start.10 = (f32[264,128]{1,0:T(8,128)S(1)}, f32[264,128]{1,0:T(8,128)S(1)}, u32[]{:S(2)}, u32[]{:S(2)}) collective-permute-start(f32[264,128]{1,0:T(8,128)S(1)} %get-tuple-element.53), channel_id=1, source_target_pairs={{0,2},{2,0},{4,6},{6,4},{8,10},{10,8},{12,14},{14,12},{1,3},{3,1},... | collective-permute-start | bytes 405512 | tf_op jit(solution)/shard_map/ppermute | solution.py:269
  41.3 8.7 %collective-permute-start.11 = (f32[264,128]{1,0:T(8,128)S(1)}, f32[264,128]{1,0:T(8,128)S(1)}, u32[]{:S(2)}, u32[]{:S(2)}) collective-permute-start(f32[264,128]{1,0:T(8,128)S(1)} %get-tuple-element.54), channel_id=1, source_target_pairs={{0,6},{2,4},{4,2},{6,0},{8,14},{10,12},{12,10},{14,8},{1,7},{3,5},... | collective-permute-start | bytes 405512 | tf_op jit(solution)/shard_map/ppermute | solution.py:269
  42.4 7.8 %collective-permute-start.12 = (f32[264,128]{1,0:T(8,128)S(1)}, f32[264,128]{1,0:T(8,128)S(1)}, u32[]{:S(2)}, u32[]{:S(2)}) collective-permute-start(f32[264,128]{1,0:T(8,128)S(1)} %get-tuple-element.55), channel_id=1, source_target_pairs={{0,4},{2,6},{4,0},{6,2},{8,12},{10,14},{12,8},{14,10},{1,5},{3,7},... | collective-permute-start | bytes 405512 | tf_op jit(solution)/shard_map/ppermute | solution.py:269
  45.0 8.2 %collective-permute-start.16 = (f32[264,128]{1,0:T(8,128)S(1)}, f32[264,128]{1,0:T(8,128)S(1)}, u32[]{:S(2)}, u32[]{:S(2)}) collective-permute-start(f32[264,128]{1,0:T(8,128)S(1)} %add_add_fusion), channel_id=1, source_target_pairs={{0,12},{2,14},{4,8},{6,10},{8,4},{10,6},{12,0},{14,2},{1,13},{3,15... | collective-permute-start | bytes 405512 | tf_op jit(solution)/shard_map/ppermute | solution.py:269
